TPU v7x, 32 devices: a whole 2x2x4 slice. The times are simulated.
32 devices in a mesh: user: 4 (over y, x), item: 8 (over z, core).
Axes of the slice: x: 2, y: 2, z: 4, core: 2. Of those that a mesh axis runs over, the one named last changes fastest.
Arguments:
- item_features: bfloat16 [1024, 256], P('item'), may hold values from -6 to 6
- level_weights: bfloat16 [3, 256, 512], replicated, may hold values from -0.21875 to 0.21875
- tile_values: bfloat16 [4, 8, 24, 128, 128], P('user', 'item'), may hold values from -0.1875 to 0.1875
- tile_order: int32 [4, 96], P('user'), may hold values from 0 to 95, each once within a row
- tile_counts: int32 [4, 8], P('user'), may hold values from 1 to 24, 96 in all within a row
- cotangent: bfloat16 [2048, 512], P(('user', 'item')), may hold values from -6 to 6
Outputs:
- hidden: bfloat16 [2048, 512], P(('user', 'item'))
- item_grad: float32 [1024, 256], P('item')
- weight_grad: float32 [3, 256, 512], replicated
Inputs may be any that keep to these rules, and one draw needn't show every extreme that they name: `tile_order`: each row is a permutation of all 96 slots of the group. `tile_counts`: each row sums to 96; in every row some cell holds exactly 24 tiles.
All inputs are finite; a program needn't handle non-finite values.
Results may differ from a plain program's by a relative error of at most 0.009.
Values may be sent and summed in bfloat16 or wider, within the bound.
No kernel may reach another device: no remote copies, remote signals or barrier semaphores. Data moves between devices by JAX's collectives and lax.ppermute only.
A program may use at most 64 MiB of HBM per device.

v0:
```python
import jax
import jax.numpy as jnp
from jax import lax
from jax.sharding import PartitionSpec as P


def silu_slope(values):
    sigmoid_v = jax.nn.sigmoid(values)
    return sigmoid_v * (1.0 + values * (1.0 - sigmoid_v))


def per_device(item_features, level_weights, tile_values, tile_order, tile_counts, cotangent):
    item_groups = lax.axis_size("item")
    item_index = lax.axis_index("item")
    levels_count = level_weights.shape[0]
    feature_width = level_weights.shape[1]
    tile_size = tile_values.shape[-1]
    capacity = tile_values.shape[2]
    local_items = item_features.shape[0]
    block_count = local_items * item_groups // tile_size
    user_blocks = tile_order.shape[1] // (levels_count * block_count)
    group_rows = user_blocks * tile_size
    target_count = levels_count * user_blocks
    tiles_local = tile_values[0, 0]
    counts_row = tile_counts[0]
    columns = jnp.arange(item_groups, dtype=jnp.int32)
    before = jnp.sum(jnp.where(columns < item_index, counts_row, 0))
    holding = jnp.sum(jnp.where(columns == item_index, counts_row, 0))
    padded = jnp.concatenate([tile_order[0], jnp.zeros((capacity,), jnp.int32)])
    cell_slots = lax.dynamic_slice_in_dim(padded, before, capacity)
    positions = jnp.arange(capacity, dtype=jnp.int32)
    live_slots = positions < holding
    slot_blocks = cell_slots % block_count
    slot_targets = cell_slots // block_count
    whole_rows = lax.all_gather(item_features, "item", axis=0, tiled=True)
    row_blocks = whole_rows.reshape(block_count, tile_size, feature_width)
    picked = jnp.take(row_blocks, slot_blocks, axis=0)
    products = jnp.einsum("tub,tbd->tud", tiles_local, picked, preferred_element_type=jnp.float32)
    target_ids = jnp.arange(target_count, dtype=jnp.int32)
    target_hot = ((target_ids[:, None] == slot_targets[None, :]) & live_slots[None, :]).astype(
        jnp.float32
    )
    aggregate = jnp.dot(
        target_hot,
        products.reshape(capacity, tile_size * feature_width),
        precision=lax.Precision.HIGHEST,
    )
    aggregate = aggregate.reshape(levels_count * group_rows, feature_width)
    stacked = aggregate.astype(jnp.bfloat16).reshape(levels_count, group_rows, feature_width)
    partial_pre = jnp.einsum(
        "rud,rdh->uh", stacked, level_weights, preferred_element_type=jnp.float32
    )
    pre_share = lax.psum_scatter(partial_pre, "item", scatter_dimension=0, tiled=True)
    hidden = jax.nn.silu(pre_share).astype(jnp.bfloat16)
    slope_share = (cotangent.astype(jnp.float32) * silu_slope(pre_share)).astype(jnp.bfloat16)
    slopes = lax.all_gather(slope_share, "item", axis=0, tiled=True)
    grad_terms = jnp.einsum("rud,uh->rdh", stacked, slopes, preferred_element_type=jnp.float32)
    users_total = group_rows * lax.axis_size("user")
    weight_grad = lax.psum(grad_terms, ("user", "item")) / jnp.sqrt(jnp.float32(users_total))
    back_rows = jnp.einsum(
        "uh,rdh->rud", slopes, level_weights, preferred_element_type=jnp.float32
    ).astype(jnp.bfloat16)
    back_flat = back_rows.reshape(levels_count * group_rows, feature_width)
    back_blocks = back_flat.reshape(target_count, tile_size, feature_width)
    taken_back = jnp.take(back_blocks, slot_targets, axis=0)
    back_products = jnp.einsum(
        "tub,tud->tbd", tiles_local, taken_back, preferred_element_type=jnp.float32
    )
    back_products = back_products.reshape(capacity, tile_size * feature_width)
    block_span = lax.axis_size("item") * local_items // tile_size
    wanted = jnp.arange(block_span, dtype=jnp.int32)
    block_hot = ((wanted[:, None] == slot_blocks[None, :]) & live_slots[None, :]).astype(
        jnp.float32
    )
    summed_rows = jnp.dot(block_hot, back_products, precision=lax.Precision.HIGHEST)
    item_part = lax.psum_scatter(
        summed_rows.reshape(lax.axis_size("item") * local_items, feature_width),
        "item",
        scatter_dimension=0,
        tiled=True,
    )
    item_grad = lax.psum(item_part, "user")
    return (hidden, item_grad, weight_grad)


def solution(mesh):
    in_specs = (
        P("item", None),
        P(),
        P("user", "item", None, None, None),
        P("user", None),
        P("user", None),
        P(("user", "item"), None),
    )
    out_specs = (P(("user", "item"), None), P("item", None), P())
    return jax.shard_map(
        per_device, mesh=mesh, in_specs=in_specs, out_specs=out_specs, check_vma=False
    )
```

profile of v0, /device:TPU:0, one launch (start us, length us, event | category | flops | bytes accessed | tf_op | source)
XLA Modules:
  0.0 323.4 jit_solution(17720200380496915662)
XLA Ops:
  7.2 16.9 %all_gather.6 = bf16[1024,256]{1,0:T(8,128)(2,1)S(1)} all-gather(bf16[128,256]{1,0:T(8,128)(2,1)} %param.6), channel_id=1, replica_groups=mesh['user'=4,'item'=8] {'item'}, dimensions={0}, use_global_device_ids=true | all-gather | bytes 589824 | tf_op jit(solution)/shard_map/all_gather | solution.py:35
  24.2 1.3 fusion.21
  27.4 1.5 compare_and_fusion
  28.9 0.6 gather_fusion
  29.6 2.3 convolution_bitcast_fusion.1
  31.9 3.6 %copy.18 = f32[3,8,128,256]{3,1,2,0:T(8,128)} copy(f32[3,8,128,256]{2,3,1,0:T(8,128)} %bitcast.38) | data formatting | bytes 6291456
  35.5 3.2 convolution_convert_fusion
  38.7 0.7 convert_element_type.25
  39.8 1.5 convolution_bitcast_fusion.2
  41.5 33.5 %reduce-scatter.3.cloned.1.call-done = f32[64,512]{1,0:T(8,128)} async-done(((f32[512,512]{1,0:T(8,128)}), f32[64,512]{1,0:T(8,128)}) %reduce-scatter.3.cloned.1.call-update) | async-done | bytes 131088 | tf_op jit(solution)/shard_map/reduce_scatter | solution.py:53
  75.0 1.6 multiply_convert_fusion
  76.5 15.0 %all_gather.7 = bf16[512,512]{1,0:T(8,128)(2,1)S(1)} all-gather(bf16[64,512]{1,0:T(8,128)(2,1)S(1)} %get-tuple-element.10), channel_id=1, replica_groups=mesh['user'=4,'item'=8] {'item'}, dimensions={0}, use_global_device_ids=true | all-gather | bytes 589824 | tf_op jit(solution)/shard_map/all_gather | solution.py:56
  91.6 1.5 convolution_convert_fusion.1
  93.1 1.8 gather_fusion.1
  94.8 2.3 convolution_bitcast_fusion
  97.2 3.6 %copy.19 = f32[3,8,128,256]{3,1,2,0:T(8,128)} copy(f32[3,8,128,256]{2,3,1,0:T(8,128)} %bitcast.39) | data formatting | bytes 6291456
  100.8 3.0 fusion.15
  103.8 1.1 reshape.41
  105.0 1.7 fusion.8
  106.8 28.6 %reduce-scatter.5.cloned.1.call-done = f32[128,256]{1,0:T(8,128)} async-done(((f32[1024,256]{1,0:T(8,128)}), f32[128,256]{1,0:T(8,128)}) %reduce-scatter.5.cloned.1.call-update) | async-done | bytes 131088 | tf_op jit(solution)/shard_map/reduce_scatter | solution.py:76
  135.5 136.2 %all-reduce.6.cloned.1.call-done = f32[3,256,512]{2,1,0:T(8,128)} async-done(((f32[3,256,512]{2,1,0:T(8,128)}), f32[3,256,512]{2,1,0:T(8,128)}) %all-reduce.6.cloned.1.call-update) | async-done | bytes 1572880 | tf_op jit(solution)/shard_map/psum | solution.py:59
  271.6 2.8 broadcast_multiply_fusion
  274.4 40.9 %all-reduce.4.cloned.1.call-done = f32[128,256]{1,0:T(8,128)} async-done(((f32[128,256]{1,0:T(8,128)}), f32[128,256]{1,0:T(8,128)}) %all-reduce.4.cloned.1.call-update) | async-done | bytes 131088 | tf_op jit(solution)/shard_map/psum | solution.py:82
  315.3 1.6 copy.24
  (23 shorter events, 0.7 us)
Async XLA Ops:
  7.2 22.4 %copy-start = (bf16[1,1,24,128,128]{4,3,2,1,0:T(8,128)(2,1)S(1)}, bf16[1,1,24,128,128]{4,3,2,1,0:T(8,128)(2,1)}, u32[]{:S(2)}) copy-start(bf16[1,1,24,128,128]{4,3,2,1,0:T(8,128)(2,1)} %param.8) | copy-start | bytes 2359300
  7.2 67.8 %reduce-scatter.3.cloned.1.call-start = ((), (), s32[]{:S(2)}) async-start(), calls=%async_computation.2 | async-start | bytes 1179648 | tf_op jit(solution)/shard_map/reduce_scatter | solution.py:53
  38.7 1.1 copy-start.3
  39.8 35.1 %copy-start.4 = (bf16[64,512]{1,0:T(8,128)(2,1)S(1)}, bf16[64,512]{1,0:T(8,128)(2,1)}, u32[]{:S(2)}) copy-start(bf16[64,512]{1,0:T(8,128)(2,1)} %param.11) | copy-start | bytes 196612
  41.4 94.1 %reduce-scatter.5.cloned.1.call-start = ((), (), s32[]{:S(2)}) async-start(), calls=%async_computation.3 | async-start | bytes 1179648 | tf_op jit(solution)/shard_map/reduce_scatter | solution.py:76
  91.6 1.5 copy-start.1
  103.8 1.2 copy-start.2
  105.0 166.7 %all-reduce.6.cloned.1.call-start = ((), (), s32[]{:S(2)}) async-start(), calls=%async_computation.5 | async-start | bytes 3145728 | tf_op jit(solution)/shard_map/psum | solution.py:59
  106.8 208.5 %all-reduce.4.cloned.1.call-start = ((), (), s32[]{:S(2)}) async-start(), calls=%async_computation.4 | async-start | bytes 262144 | tf_op jit(solution)/shard_map/psum | solution.py:82
Sparse Core Ops, SparseCore 0:
  41.5 33.3 reduce-scatter.2
  105.1 30.3 reduce-scatter.4
  141.3 130.2 all-reduce.5
  274.4 40.8 all-reduce.3
where the time goes:
time: 324 us; the launch traced here: 323 us
  waiting for transfers between devices  239 us (74%)
  blocking collectives  31.9 us (10%)
  between operations  15.8 us (5%)
  matrix products  15.7 us (5%)
  local copies, waits for them, and re-layouts  13.4 us (4%)
  other arithmetic  7.17 us (2%)
    psum x1, waiting for transfers between devices, per_device(): lax.psum(grad_terms, ('user', 'item')) / jnp.sqrt(jnp.float32(users_total))  136 us
    psum x1, waiting for transfers between devices, per_device(): item_grad = lax.psum(item_part, 'user')  40.9 us
    reduce_scatter x1, waiting for transfers between devices, per_device(): lax.psum_scatter(partial_pre, 'item', scatter_dimension=0, tiled=True)  33.5 us
    reduce_scatter x1, waiting for transfers between devices, per_device(): lax.psum_scatter(summed_rows.reshape(lax.axis_size('item') * local_items,...  28.6 us
    all_gather x1, blocking collectives, per_device(): whole_rows = lax.all_gather(item_features, 'item', axis=0, tiled=True)  16.9 us
    all_gather x1, blocking collectives, per_device(): slopes = lax.all_gather(slope_share, 'item', axis=0, tiled=True)  15 us
    unnamed x13, local copies, waits for them, and re-layouts  9.16 us
  transfers between devices with their start and end apart: 4, of which 4 were waited for; matrix products, arithmetic and copies ran while one was open for 1% of the time, Pallas kernels for 0%

commit v1 on v0

v1 whole, which is shorter than its diff:
```python
import functools
import jax
import jax.numpy as jnp
from jax import lax
from jax.experimental import pallas as pl
from jax.experimental.pallas import tpu as pltpu
from jax.sharding import PartitionSpec as P

BF16 = jnp.bfloat16
F32 = jnp.float32
VMEM_LIMIT = 24 * 1024 * 1024


def partners(axis, step):
    return [(i, i ^ step) for i in range(lax.axis_size(axis))]


def swap(array, axis, step):
    return lax.ppermute(array, axis, partners(axis, step))


def tree_sum(parts):
    while len(parts) > 1:
        parts = [parts[i] + parts[i + 1] for i in range(0, len(parts), 2)]
    return parts[0]


def call(body, out_shapes, args, scratch=(), specs=None, cost=None):
    vmem = pl.BlockSpec(memory_space=pltpu.VMEM)
    return pl.pallas_call(
        body,
        out_shape=out_shapes,
        in_specs=specs if specs is not None else [vmem] * len(args),
        out_specs=jax.tree.map(lambda _: vmem, out_shapes),
        scratch_shapes=list(scratch),
        compiler_params=pltpu.CompilerParams(vmem_limit_bytes=VMEM_LIMIT),
        cost_estimate=cost,
    )(*args)


def struct(shape, dtype):
    return jax.ShapeDtypeStruct(shape, dtype)


def place_tiles(block_count, order, counts, tiles, dense, sems):
    tile = tiles.shape[-1]
    capacity = tiles.shape[2]
    cell = lax.axis_index("item")
    before = jnp.int32(0)
    for c in range(counts.shape[1]):
        before = before + jnp.where(c < cell, counts[0, c], 0)
    holding = counts[0, cell]
    dense[...] = jnp.zeros_like(dense)

    def copy(t):
        slot = order[0, jnp.minimum(before + t, order.shape[1] - 1)]
        row = pl.multiple_of((slot // block_count) * tile, tile)
        column = pl.multiple_of((slot % block_count) * tile, tile)
        return pltpu.make_async_copy(
            tiles.at[0, 0, t], dense.at[pl.ds(row, tile), pl.ds(column, tile)], sems.at[t]
        )

    for t in range(capacity):
        @pl.when(t < holding)
        def _():
            copy(t).start()
    for t in range(capacity):
        @pl.when(t < holding)
        def _():
            copy(t).wait()


def forward(chips, dense, weights, *refs):
    pieces = refs[: 2 * chips]
    aggregate, keep, send, features = refs[2 * chips:]
    core = lax.axis_index("item") % 2
    chip = lax.axis_index("item") // 2
    levels, width, hidden = weights.shape
    tile = pieces[0].shape[0]
    for k in range(chips):
        for other in range(2):
            block = 2 * (chip ^ k) + (core ^ other)
            features[pl.ds(pl.multiple_of(block * tile, tile), tile), :] = pieces[2 * k + other][...]
    group_rows = dense.shape[0] // levels
    share = keep.shape[1]
    step = min(256, group_rows)
    for first in range(0, group_rows, step):
        total = jnp.zeros((step, hidden), F32)
        for r in range(levels):
            rows = pl.ds(r * group_rows + first, step)
            block = jnp.dot(dense[rows, :], features[...], preferred_element_type=F32).astype(BF16)
            aggregate[rows, :] = block
            total = total + jnp.dot(block, weights[r], preferred_element_type=F32)
        for at in range(0, step, 2 * share):
            z = (first + at) // (2 * share)
            even = total[at:at + share]
            odd = total[at + share:at + 2 * share]
            keep[z] = jnp.where(core == 0, even, odd)
            send[z] = jnp.where(core == 0, odd, even).astype(BF16)


def pair_sum(chips, keep, got, own, *sends):
    chip = lax.axis_index("item") // 2
    own[...] = (keep[chip].astype(F32) + got[chip].astype(F32)).astype(own.dtype)
    for k in range(1, chips):
        sends[k - 1][...] = (keep[chip ^ k].astype(F32) + got[chip ^ k].astype(F32)).astype(BF16)


def activate(own, *refs):
    *parts, cotangent, hidden, slope = refs
    pre = own[...]
    for part in parts:
        pre = pre + part[...].astype(F32)
    sigmoid = 1.0 / (1.0 + jnp.exp(-pre))
    hidden[...] = (pre * sigmoid).astype(BF16)
    slope[...] = (cotangent[...].astype(F32) * (sigmoid * (1.0 + pre * (1.0 - sigmoid)))).astype(BF16)


def gather_slopes(chips, pieces, slopes):
    core = lax.axis_index("item") % 2
    chip = lax.axis_index("item") // 2
    share = pieces[0].shape[0]
    for k in range(chips):
        for other in range(2):
            block = 2 * (chip ^ k) + (core ^ other)
            slopes[pl.ds(pl.multiple_of(block * share, share), share), :] = pieces[2 * k + other][...]


def backward(chips, dense, weights, *refs):
    pieces = refs[: 2 * chips]
    slopes, keep, send, back = refs[2 * chips:]
    gather_slopes(chips, pieces, slopes)
    core = lax.axis_index("item") % 2
    levels, width, hidden = weights.shape
    group_rows = slopes.shape[0]
    for r in range(levels):
        back[pl.ds(r * group_rows, group_rows), :] = lax.dot_general(
            slopes[...], weights[r], (((1,), (1,)), ((), ())), preferred_element_type=F32
        ).astype(BF16)
    tile = keep.shape[1]
    for z in range(keep.shape[0]):
        both = lax.dot_general(
            dense[:, pl.ds(2 * z * tile, 2 * tile)], back[...],
            (((0,), (0,)), ((), ())), preferred_element_type=F32,
        )
        even, odd = both[:tile], both[tile:]
        keep[z] = jnp.where(core == 0, even, odd)
        send[z] = jnp.where(core == 0, odd, even).astype(BF16)


def weight_terms(aggregate, slopes, keep, send):
    core = lax.axis_index("item") % 2
    levels = keep.shape[1]
    group_rows = slopes.shape[0]
    half = aggregate.shape[1] // 2
    chips = keep.shape[0]
    part = half // chips
    for r in range(levels):
        both = lax.dot_general(
            aggregate[pl.ds(r * group_rows, group_rows), :], slopes[...],
            (((0,), (0,)), ((), ())), preferred_element_type=F32,
        )
        low, high = both[:half], both[half:]
        mine = jnp.where(core == 0, low, high)
        theirs = jnp.where(core == 0, high, low).astype(BF16)
        for z in range(chips):
            keep[z, r] = mine[z * part:(z + 1) * part]
            send[z, r] = theirs[z * part:(z + 1) * part]


def round_sum(*refs):
    *parts, out = refs
    total = parts[0][...].astype(F32)
    for part in parts[1:]:
        total = total + part[...].astype(F32)
    out[...] = total.astype(out.dtype)


def tree_round(*refs):
    *parts, out = refs
    out[...] = tree_sum([part[...].astype(F32) for part in parts]).astype(out.dtype)


def assemble(chips, scale, *refs):
    *pieces, out = refs
    core = lax.axis_index("item") % 2
    chip = lax.axis_index("item") // 2
    levels, part, hidden = pieces[0].shape
    half = out.shape[1] // 2
    for k in range(chips):
        for other in range(2):
            row = (core ^ other) * half + (chip ^ k) * part
            out[:, pl.ds(pl.multiple_of(row, part), part), :] = pieces[2 * k + other][...].astype(F32) * scale


def per_device(item_features, level_weights, tile_values, tile_order, tile_counts, cotangent):
    item_size = lax.axis_size("item")
    user_size = lax.axis_size("user")
    chips = item_size // 2
    levels, width, hidden_width = level_weights.shape
    tile = tile_values.shape[-1]
    capacity = tile_values.shape[2]
    local_items = item_features.shape[0]
    items = local_items * item_size
    block_count = items // tile
    user_blocks = tile_order.shape[1] // (levels * block_count)
    group_rows = user_blocks * tile
    share = group_rows // item_size
    vmem = pl.BlockSpec(memory_space=pltpu.VMEM)
    smem = pl.BlockSpec(memory_space=pltpu.SMEM)

    pieces = [item_features] + [swap(item_features, "item", 2 * k) for k in range(1, chips)]
    feature_pieces = []
    for piece in pieces:
        feature_pieces += [piece, swap(piece, "item", 1)]

    dense = call(
        functools.partial(place_tiles, block_count),
        struct((levels * group_rows, items), BF16),
        (tile_order, tile_counts, tile_values),
        scratch=[pltpu.SemaphoreType.DMA((capacity,))],
        specs=[smem, smem, pl.BlockSpec(memory_space=pl.ANY)],
    )
    aggregate, pre_keep, pre_send = call(
        functools.partial(forward, chips),
        (
            struct((levels * group_rows, width), BF16),
            struct((chips, share, hidden_width), F32),
            struct((chips, share, hidden_width), BF16),
        ),
        (dense, level_weights, *feature_pieces),
        scratch=[pltpu.VMEM((items, width), BF16)],
    )
    pre_got = swap(pre_send, "item", 1)
    pre_own, *pre_sends = call(
        functools.partial(pair_sum, chips),
        (struct((share, hidden_width), F32),) + (struct((share, hidden_width), BF16),) * (chips - 1),
        (pre_keep, pre_got),
    )
    pre_parts = [swap(pre_sends[k - 1], "item", 2 * k) for k in range(1, chips)]
    hidden, slope = call(
        activate,
        (struct((share, hidden_width), BF16),) * 2,
        (pre_own, *pre_parts, cotangent),
    )
    pieces = [slope] + [swap(slope, "item", 2 * k) for k in range(1, chips)]
    slope_pieces = []
    for piece in pieces:
        slope_pieces += [piece, swap(piece, "item", 1)]

    slopes, item_keep, item_send = call(
        functools.partial(backward, chips),
        (
            struct((group_rows, hidden_width), BF16),
            struct((chips, tile, width), F32),
            struct((chips, tile, width), BF16),
        ),
        (dense, level_weights, *slope_pieces),
        scratch=[pltpu.VMEM((levels * group_rows, width), BF16)],
    )
    item_got = swap(item_send, "item", 1)
    part = width // item_size
    grad_keep, grad_send = call(
        weight_terms,
        (
            struct((chips, levels, part, hidden_width), F32),
            struct((chips, levels, part, hidden_width), BF16),
        ),
        (aggregate, slopes),
    )
    item_own, *item_sends = call(
        functools.partial(pair_sum, chips),
        (struct((tile, width), F32),) + (struct((tile, width), BF16),) * (chips - 1),
        (item_keep, item_got),
    )
    item_parts = [swap(item_sends[k - 1], "item", 2 * k) for k in range(1, chips)]
    item_group = call(round_sum, struct((tile, width), BF16), (item_own, *item_parts))
    item_all = [item_group] + [swap(item_group, "user", k) for k in range(1, user_size)]
    item_grad = call(tree_round, struct((tile, width), F32), item_all)

    grad_got = swap(grad_send, "item", 1)
    grad_own, *grad_sends = call(
        functools.partial(pair_sum, chips),
        (struct((levels, part, hidden_width), F32),)
        + (struct((levels, part, hidden_width), BF16),) * (chips - 1),
        (grad_keep, grad_got),
    )
    grad_parts = [swap(grad_sends[k - 1], "item", 2 * k) for k in range(1, chips)]
    grad_group = call(round_sum, struct((levels, part, hidden_width), BF16), (grad_own, *grad_parts))
    grad_all = [grad_group] + [swap(grad_group, "user", k) for k in range(1, user_size)]
    grad_piece = call(tree_round, struct((levels, part, hidden_width), BF16), grad_all)
    pieces = [grad_piece] + [swap(grad_piece, "item", 2 * k) for k in range(1, chips)]
    grad_pieces = []
    for piece in pieces:
        grad_pieces += [piece, swap(piece, "item", 1)]
    weight_grad = call(
        functools.partial(assemble, chips, (group_rows * user_size) ** -0.5),
        struct((levels, width, hidden_width), F32),
        grad_pieces,
    )
    return hidden, item_grad, weight_grad


def solution(mesh):
    in_specs = (
        P("item", None),
        P(),
        P("user", "item", None, None, None),
        P("user", None),
        P("user", None),
        P(("user", "item"), None),
    )
    out_specs = (P(("user", "item"), None), P("item", None), P())
    return jax.shard_map(
        per_device, mesh=mesh, in_specs=in_specs, out_specs=out_specs, check_vma=False
    )
```

time: 324 us -> 85.1 us (0.26)
  waiting for transfers between devices: 239 us -> 32.9 us
  starting transfers between devices: 0.16 us -> 40.3 us
  blocking collectives: 31.9 us -> 0 us
  matrix products: 15.7 us -> 0 us
  between operations: 15.8 us -> 0.81 us
  local copies, waits for them, and re-layouts: 13.4 us -> 2.46 us
  Pallas kernels: 0 us -> 8.42 us
  other arithmetic: 7.17 us -> 0 us
    psum x2 -> x0, waiting for transfers between devices: 177 us -> none  [the longest x1 136 us: per_device(): lax.psum(grad_terms, ('user', 'item')) / jnp.sqrt(jnp.float32(users_total))]
    reduce_scatter x2 -> x0, waiting for transfers between devices: 62.1 us -> none  [the longest x1 33.5 us: per_device(): lax.psum_scatter(partial_pre, 'item', scatter_dimension=0, tiled=True)]
    ppermute x0 -> x39, starting transfers between devices: none -> 40.3 us  [swap(): return lax.ppermute(array, axis, partners(axis, step))]
    ppermute x0 -> x39, waiting for transfers between devices: none -> 32.9 us  [swap(): return lax.ppermute(array, axis, partners(axis, step))]
    all_gather x2 -> x0, blocking collectives: 31.9 us -> none  [the longest x1 16.9 us: per_device(): whole_rows = lax.all_gather(item_features, 'item', axis=0, tiled=True)]
    dot_general x7 -> x0, matrix products: 15.7 us -> none  [the longest x1 3.19 us: per_device(): jnp.dot(target_hot, products.reshape(capacity, tile_size * feature_width)...]
    pallas_call x0 -> x13, Pallas kernels: none -> 8.42 us  [call(): pl.pallas_call(body, out_shape=out_shapes, in_specs=specs if specs is not...]
    unnamed x13 -> x12, local copies, waits for them, and re-layouts: 9.16 us -> 2.46 us
  transfers between devices with their start and end apart: 4 -> 39, of which waited for: 4 -> 17; matrix products, arithmetic and copies ran while one was open for 1% -> 0% of each run, Pallas kernels for 0% -> 3%
where the time goes in v1:
time: 85.1 us; the launch traced here: 84.9 us
  starting transfers between devices  40.3 us (47%)
  waiting for transfers between devices  32.9 us (39%)
  Pallas kernels  8.42 us (10%)
  local copies, waits for them, and re-layouts  2.46 us (3%)
    ppermute x39, starting transfers between devices, swap(): return lax.ppermute(array, axis, partners(axis, step))  40.3 us
    ppermute x39, waiting for transfers between devices, swap(): return lax.ppermute(array, axis, partners(axis, step))  32.9 us
    pallas_call x13, Pallas kernels, call(): pl.pallas_call(body, out_shape=out_shapes, in_specs=specs if specs is not...  8.42 us
    unnamed x12, local copies, waits for them, and re-layouts  2.46 us
  transfers between devices with their start and end apart: 39, of which 17 were waited for; matrix products, arithmetic and copies ran while one was open for 0% of the time, Pallas kernels for 3%

profile of v1, /device:TPU:0, one launch (start us, length us, event | category | flops | bytes accessed | tf_op | source)
XLA Modules:
  0.0 84.9 jit_solution(566535614056741172)
XLA Ops:
  0.6 4.1 %collective-permute-start.3 = (bf16[128,256]{1,0:T(8,128)(2,1)}, bf16[128,256]{1,0:T(8,128)(2,1)S(1)}, u32[]{:S(2)}, u32[]{:S(2)}) collective-permute-start(bf16[128,256]{1,0:T(8,128)(2,1)} %refs_0_.1), channel_id=1, source_target_pairs={{0,4},{1,5},{2,6},{3,7},{4,0},{5,1},{6,2},{7,3},{8,12},{9,13},{10,... | collective-permute-start | bytes 196616 | tf_op jit(solution)/shard_map/ppermute | solution.py:19
  4.7 1.6 %collective-permute-start.1 = (bf16[128,256]{1,0:T(8,128)(2,1)}, bf16[128,256]{1,0:T(8,128)(2,1)S(1)}, u32[]{:S(2)}, u32[]{:S(2)}) collective-permute-start(bf16[128,256]{1,0:T(8,128)(2,1)} %refs_0_.1), channel_id=1, source_target_pairs={{0,2},{1,3},{2,0},{3,1},{4,6},{5,7},{6,4},{7,5},{8,10},{9,11},{10,... | collective-permute-start | bytes 196616 | tf_op jit(solution)/shard_map/ppermute | solution.py:19
  6.3 1.7 %collective-permute-done.3.refs_4_ = bf16[128,256]{1,0:T(8,128)(2,1)S(1)} collective-permute-done((bf16[128,256]{1,0:T(8,128)(2,1)}, bf16[128,256]{1,0:T(8,128)(2,1)S(1)}, u32[]{:S(2)}, u32[]{:S(2)}) %collective-permute-start.3) | collective-permute-done | bytes 65568 | tf_op jit(solution)/shard_map/ppermute | solution.py:19
  9.2 3.4 %collective-permute-done.5.refs_6_ = bf16[128,256]{1,0:T(8,128)(2,1)S(1)} collective-permute-done((bf16[128,256]{1,0:T(8,128)(2,1)}, bf16[128,256]{1,0:T(8,128)(2,1)S(1)}, u32[]{:S(2)}, u32[]{:S(2)}) %collective-permute-start.5) | collective-permute-done | bytes 65568 | tf_op jit(solution)/shard_map/ppermute | solution.py:19
  15.0 1.5 %shard_map.85.dense = bf16[1536,1024]{1,0:T(8,128)(2,1)S(1)} custom-call(s32[1,96]{1,0:T(1,128)S(1)} %copy-done.4, s32[1,8]{1,0:T(1,128)S(1)} %copy-done.5, bf16[1,1,24,128,128]{4,3,2,1,0:T(8,128)(2,1)S(1)} %copy-done.1), custom_call_target="tpu_custom_call" | custom-call | tf_op jit(solution)/shard_map/pallas_call | solution.py:30
  16.6 1.9 %shard_map.86 = (bf16[1536,256]{1,0:T(8,128)(2,1)S(1)}, f32[4,64,512]{2,1,0:T(8,128)S(1)}, bf16[4,64,512]{2,1,0:T(8,128)(2,1)S(1)}) custom-call(bf16[1536,1024]{1,0:T(8,128)(2,1)S(1)} %shard_map.85.dense, bf16[3,256,512]{2,1,0:T(8,128)(2,1)S(1)} %copy-done, bf16[128,256]{1,0:T(8,128)(2,1)S(1)} %copy-done.2, ...), custom_call_target="tpu_custom_call" | custom-call | tf_op jit(solution)/shard_map/pallas_call | solution.py:30
  20.3 2.1 %collective-permute-start.9 = (bf16[64,512]{1,0:T(8,128)(2,1)S(1)}, bf16[64,512]{1,0:T(8,128)(2,1)S(1)}, u32[]{:S(2)}, u32[]{:S(2)}) collective-permute-start(bf16[64,512]{1,0:T(8,128)(2,1)S(1)} %get-tuple-element.29), channel_id=1, source_target_pairs={{0,4},{1,5},{2,6},{3,7},{4,0},{5,1},{6,2},{7,3},{8,12},{9,13},{10,... | collective-permute-start | bytes 196616 | tf_op jit(solution)/shard_map/ppermute | solution.py:19
  22.4 2.3 %collective-permute-start.10 = (bf16[64,512]{1,0:T(8,128)(2,1)S(1)}, bf16[64,512]{1,0:T(8,128)(2,1)S(1)}, u32[]{:S(2)}, u32[]{:S(2)}) collective-permute-start(bf16[64,512]{1,0:T(8,128)(2,1)S(1)} %get-tuple-element.30), channel_id=1, source_target_pairs={{0,6},{1,7},{2,4},{3,5},{4,2},{5,3},{6,0},{7,1},{8,14},{9,15},{10,... | collective-permute-start | bytes 196616 | tf_op jit(solution)/shard_map/ppermute | solution.py:19
  25.7 3.0 %collective-permute-done.9.refs_1_ = bf16[64,512]{1,0:T(8,128)(2,1)S(1)} collective-permute-done((bf16[64,512]{1,0:T(8,128)(2,1)S(1)}, bf16[64,512]{1,0:T(8,128)(2,1)S(1)}, u32[]{:S(2)}, u32[]{:S(2)}) %collective-permute-start.9) | collective-permute-done | bytes 65568 | tf_op jit(solution)/shard_map/ppermute | solution.py:19
  29.4 2.5 %collective-permute-start.16 = (bf16[64,512]{1,0:T(8,128)(2,1)S(1)}, bf16[64,512]{1,0:T(8,128)(2,1)S(1)}, u32[]{:S(2)}, u32[]{:S(2)}) collective-permute-start(bf16[64,512]{1,0:T(8,128)(2,1)S(1)} %get-tuple-element.32.refs_0_), channel_id=1, source_target_pairs={{0,6},{1,7},{2,4},{3,5},{4,2},{5,3},{6,0},{7,1},{8,14},{9,15},{10,... | collective-permute-start | bytes 196616 | tf_op jit(solution)/shard_map/ppermute | solution.py:19
  33.8 2.2 %collective-permute-done.16.refs_6_ = bf16[64,512]{1,0:T(8,128)(2,1)S(1)} collective-permute-done((bf16[64,512]{1,0:T(8,128)(2,1)S(1)}, bf16[64,512]{1,0:T(8,128)(2,1)S(1)}, u32[]{:S(2)}, u32[]{:S(2)}) %collective-permute-start.16) | collective-permute-done | bytes 65568 | tf_op jit(solution)/shard_map/ppermute | solution.py:19
  35.9 2.2 %collective-permute-done.14.refs_4_ = bf16[64,512]{1,0:T(8,128)(2,1)S(1)} collective-permute-done((bf16[64,512]{1,0:T(8,128)(2,1)S(1)}, bf16[64,512]{1,0:T(8,128)(2,1)S(1)}, u32[]{:S(2)}, u32[]{:S(2)}) %collective-permute-start.14) | collective-permute-done | bytes 65568 | tf_op jit(solution)/shard_map/ppermute | solution.py:19
  43.6 3.1 %collective-permute-start.27 = (bf16[3,32,512]{2,1,0:T(8,128)(2,1)S(1)}, bf16[3,32,512]{2,1,0:T(8,128)(2,1)S(1)}, u32[]{:S(2)}, u32[]{:S(2)}) collective-permute-start(bf16[3,32,512]{2,1,0:T(8,128)(2,1)S(1)} %get-tuple-element.45), channel_id=1, source_target_pairs={{0,4},{1,5},{2,6},{3,7},{4,0},{5,1},{6,2},{7,3},{8,12},{9,13},{10,... | collective-permute-start | bytes 294920 | tf_op jit(solution)/shard_map/ppermute | solution.py:19
  47.9 2.4 %collective-permute-done.26.refs_1_ = bf16[3,32,512]{2,1,0:T(8,128)(2,1)S(1)} collective-permute-done((bf16[3,32,512]{2,1,0:T(8,128)(2,1)S(1)}, bf16[3,32,512]{2,1,0:T(8,128)(2,1)S(1)}, u32[]{:S(2)}, u32[]{:S(2)}) %collective-permute-start.26) | collective-permute-done | bytes 98336 | tf_op jit(solution)/shard_map/ppermute | solution.py:19
  50.3 4.2 %collective-permute-done.27.refs_2_ = bf16[3,32,512]{2,1,0:T(8,128)(2,1)S(1)} collective-permute-done((bf16[3,32,512]{2,1,0:T(8,128)(2,1)S(1)}, bf16[3,32,512]{2,1,0:T(8,128)(2,1)S(1)}, u32[]{:S(2)}, u32[]{:S(2)}) %collective-permute-start.27) | collective-permute-done | bytes 98336 | tf_op jit(solution)/shard_map/ppermute | solution.py:19
  54.5 2.5 %collective-permute-start.31 = (bf16[3,32,512]{2,1,0:T(8,128)(2,1)S(1)}, bf16[3,32,512]{2,1,0:T(8,128)(2,1)S(1)}, u32[]{:S(2)}, u32[]{:S(2)}) collective-permute-start(bf16[3,32,512]{2,1,0:T(8,128)(2,1)S(1)} %shard_map.95.refs_0_), channel_id=1, source_target_pairs={{0,24},{8,16},{16,8},{24,0},{1,25},{9,17},{17,9},{25,1},{2,26},{10... | collective-permute-start | bytes 294920 | tf_op jit(solution)/shard_map/ppermute | solution.py:19
  58.1 2.2 %collective-permute-start.19 = (bf16[128,256]{1,0:T(8,128)(2,1)S(1)}, bf16[128,256]{1,0:T(8,128)(2,1)S(1)}, u32[]{:S(2)}, u32[]{:S(2)}) collective-permute-start(bf16[128,256]{1,0:T(8,128)(2,1)S(1)} %get-tuple-element.36), channel_id=1, source_target_pairs={{0,2},{1,3},{2,0},{3,1},{4,6},{5,7},{6,4},{7,5},{8,10},{9,11},{10,... | collective-permute-start | bytes 196616 | tf_op jit(solution)/shard_map/ppermute | solution.py:19
  61.4 2.1 %collective-permute-start.21 = (bf16[128,256]{1,0:T(8,128)(2,1)S(1)}, bf16[128,256]{1,0:T(8,128)(2,1)S(1)}, u32[]{:S(2)}, u32[]{:S(2)}) collective-permute-start(bf16[128,256]{1,0:T(8,128)(2,1)S(1)} %get-tuple-element.38), channel_id=1, source_target_pairs={{0,6},{1,7},{2,4},{3,5},{4,2},{5,3},{6,0},{7,1},{8,14},{9,15},{10,... | collective-permute-start | bytes 196616 | tf_op jit(solution)/shard_map/ppermute | solution.py:19
  63.5 1.8 %collective-permute-start.37 = (bf16[3,32,512]{2,1,0:T(8,128)(2,1)S(1)}, bf16[3,32,512]{2,1,0:T(8,128)(2,1)S(1)}, u32[]{:S(2)}, u32[]{:S(2)}) collective-permute-start(bf16[3,32,512]{2,1,0:T(8,128)(2,1)S(1)} %shard_map.96.refs_0_), channel_id=1, source_target_pairs={{0,6},{1,7},{2,4},{3,5},{4,2},{5,3},{6,0},{7,1},{8,14},{9,15},{10,... | collective-permute-start | bytes 294920 | tf_op jit(solution)/shard_map/ppermute | solution.py:19
  66.1 1.9 %collective-permute-start.33 = (bf16[3,32,512]{2,1,0:T(8,128)(2,1)S(1)}, bf16[3,32,512]{2,1,0:T(8,128)(2,1)S(1)}, u32[]{:S(2)}, u32[]{:S(2)}) collective-permute-start(bf16[3,32,512]{2,1,0:T(8,128)(2,1)S(1)} %shard_map.96.refs_0_), channel_id=1, source_target_pairs={{0,2},{1,3},{2,0},{3,1},{4,6},{5,7},{6,4},{7,5},{8,10},{9,11},{10,... | collective-permute-start | bytes 294920 | tf_op jit(solution)/shard_map/ppermute | solution.py:19
  68.0 2.2 %collective-permute-done.20.refs_2_ = bf16[128,256]{1,0:T(8,128)(2,1)S(1)} collective-permute-done((bf16[128,256]{1,0:T(8,128)(2,1)S(1)}, bf16[128,256]{1,0:T(8,128)(2,1)S(1)}, u32[]{:S(2)}, u32[]{:S(2)}) %collective-permute-start.20) | collective-permute-done | bytes 65568 | tf_op jit(solution)/shard_map/ppermute | solution.py:19
  70.2 4.2 %collective-permute-start.24 = (bf16[128,256]{1,0:T(8,128)(2,1)S(1)}, bf16[128,256]{1,0:T(8,128)(2,1)S(1)}, u32[]{:S(2)}, u32[]{:S(2)}) collective-permute-start(bf16[128,256]{1,0:T(8,128)(2,1)S(1)} %shard_map.91.refs_0_), channel_id=1, source_target_pairs={{0,24},{8,16},{16,8},{24,0},{1,25},{9,17},{17,9},{25,1},{2,26},{10... | collective-permute-start | bytes 196616 | tf_op jit(solution)/shard_map/ppermute | solution.py:19
  74.9 1.7 %collective-permute-done.24.refs_3_ = bf16[128,256]{1,0:T(8,128)(2,1)S(1)} collective-permute-done((bf16[128,256]{1,0:T(8,128)(2,1)S(1)}, bf16[128,256]{1,0:T(8,128)(2,1)S(1)}, u32[]{:S(2)}, u32[]{:S(2)}) %collective-permute-start.24) | collective-permute-done | bytes 65568 | tf_op jit(solution)/shard_map/ppermute | solution.py:19
  79.6 3.3 %collective-permute-done.22.refs_1_ = bf16[128,256]{1,0:T(8,128)(2,1)S(1)} collective-permute-done((bf16[128,256]{1,0:T(8,128)(2,1)S(1)}, bf16[128,256]{1,0:T(8,128)(2,1)S(1)}, u32[]{:S(2)}, u32[]{:S(2)}) %collective-permute-start.22) | collective-permute-done | bytes 65568 | tf_op jit(solution)/shard_map/ppermute | solution.py:19
  (79 shorter events, 24.4 us)
Async XLA Ops:
  0.6 7.4 %collective-permute-start.3 = (bf16[128,256]{1,0:T(8,128)(2,1)}, bf16[128,256]{1,0:T(8,128)(2,1)S(1)}, u32[]{:S(2)}, u32[]{:S(2)}) collective-permute-start(bf16[128,256]{1,0:T(8,128)(2,1)} %refs_0_.1), channel_id=1, source_target_pairs={{0,4},{1,5},{2,6},{3,7},{4,0},{5,1},{6,2},{7,3},{8,12},{9,13},{10,... | collective-permute-start | bytes 196616 | tf_op jit(solution)/shard_map/ppermute | solution.py:19
  6.3 10.3 %collective-permute-start = (bf16[128,256]{1,0:T(8,128)(2,1)}, bf16[128,256]{1,0:T(8,128)(2,1)S(1)}, u32[]{:S(2)}, u32[]{:S(2)}) collective-permute-start(bf16[128,256]{1,0:T(8,128)(2,1)} %refs_0_.1), channel_id=1, source_target_pairs={{0,1},{1,0},{2,3},{3,2},{4,5},{5,4},{6,7},{7,6},{8,9},{9,8},{10,11... | collective-permute-start | bytes 196616 | tf_op jit(solution)/shard_map/ppermute | solution.py:19
  8.0 8.6 %collective-permute-start.4 = (bf16[128,256]{1,0:T(8,128)(2,1)S(1)}, bf16[128,256]{1,0:T(8,128)(2,1)S(1)}, u32[]{:S(2)}, u32[]{:S(2)}) collective-permute-start(bf16[128,256]{1,0:T(8,128)(2,1)S(1)} %collective-permute-done.3.refs_4_), channel_id=1, source_target_pairs={{0,1},{1,0},{2,3},{3,2},{4,5},{5,4},{6,7},{7,6},{8,9},{9,8},{10,11... | collective-permute-start | bytes 196616 | tf_op jit(solution)/shard_map/ppermute | solution.py:19
  9.2 7.4 %collective-permute-start.2 = (bf16[128,256]{1,0:T(8,128)(2,1)S(1)}, bf16[128,256]{1,0:T(8,128)(2,1)S(1)}, u32[]{:S(2)}, u32[]{:S(2)}) collective-permute-start(bf16[128,256]{1,0:T(8,128)(2,1)S(1)} %collective-permute-done.1.refs_2_), channel_id=1, source_target_pairs={{0,1},{1,0},{2,3},{3,2},{4,5},{5,4},{6,7},{7,6},{8,9},{9,8},{10,11... | collective-permute-start | bytes 196616 | tf_op jit(solution)/shard_map/ppermute | solution.py:19
  20.3 8.4 %collective-permute-start.9 = (bf16[64,512]{1,0:T(8,128)(2,1)S(1)}, bf16[64,512]{1,0:T(8,128)(2,1)S(1)}, u32[]{:S(2)}, u32[]{:S(2)}) collective-permute-start(bf16[64,512]{1,0:T(8,128)(2,1)S(1)} %get-tuple-element.29), channel_id=1, source_target_pairs={{0,4},{1,5},{2,6},{3,7},{4,0},{5,1},{6,2},{7,3},{8,12},{9,13},{10,... | collective-permute-start | bytes 196616 | tf_op jit(solution)/shard_map/ppermute | solution.py:19
  22.4 6.3 %collective-permute-start.10 = (bf16[64,512]{1,0:T(8,128)(2,1)S(1)}, bf16[64,512]{1,0:T(8,128)(2,1)S(1)}, u32[]{:S(2)}, u32[]{:S(2)}) collective-permute-start(bf16[64,512]{1,0:T(8,128)(2,1)S(1)} %get-tuple-element.30), channel_id=1, source_target_pairs={{0,6},{1,7},{2,4},{3,5},{4,2},{5,3},{6,0},{7,1},{8,14},{9,15},{10,... | collective-permute-start | bytes 196616 | tf_op jit(solution)/shard_map/ppermute | solution.py:19
  29.4 6.5 %collective-permute-start.16 = (bf16[64,512]{1,0:T(8,128)(2,1)S(1)}, bf16[64,512]{1,0:T(8,128)(2,1)S(1)}, u32[]{:S(2)}, u32[]{:S(2)}) collective-permute-start(bf16[64,512]{1,0:T(8,128)(2,1)S(1)} %get-tuple-element.32.refs_0_), channel_id=1, source_target_pairs={{0,6},{1,7},{2,4},{3,5},{4,2},{5,3},{6,0},{7,1},{8,14},{9,15},{10,... | collective-permute-start | bytes 196616 | tf_op jit(solution)/shard_map/ppermute | solution.py:19
  42.0 16.0 %collective-permute-start.18 = (bf16[4,128,256]{2,1,0:T(8,128)(2,1)S(1)}, bf16[4,128,256]{2,1,0:T(8,128)(2,1)S(1)}, u32[]{:S(2)}, u32[]{:S(2)}) collective-permute-start(bf16[4,128,256]{2,1,0:T(8,128)(2,1)S(1)} %get-tuple-element.34), channel_id=1, source_target_pairs={{0,1},{1,0},{2,3},{3,2},{4,5},{5,4},{6,7},{7,6},{8,9},{9,8},{10,11... | collective-permute-start | bytes 786440 | tf_op jit(solution)/shard_map/ppermute | solution.py:19
  43.5 6.8 %collective-permute-start.26 = (bf16[3,32,512]{2,1,0:T(8,128)(2,1)S(1)}, bf16[3,32,512]{2,1,0:T(8,128)(2,1)S(1)}, u32[]{:S(2)}, u32[]{:S(2)}) collective-permute-start(bf16[3,32,512]{2,1,0:T(8,128)(2,1)S(1)} %get-tuple-element.44), channel_id=1, source_target_pairs={{0,2},{1,3},{2,0},{3,1},{4,6},{5,7},{6,4},{7,5},{8,10},{9,11},{10,... | collective-permute-start | bytes 294920 | tf_op jit(solution)/shard_map/ppermute | solution.py:19
  43.6 10.9 %collective-permute-start.27 = (bf16[3,32,512]{2,1,0:T(8,128)(2,1)S(1)}, bf16[3,32,512]{2,1,0:T(8,128)(2,1)S(1)}, u32[]{:S(2)}, u32[]{:S(2)}) collective-permute-start(bf16[3,32,512]{2,1,0:T(8,128)(2,1)S(1)} %get-tuple-element.45), channel_id=1, source_target_pairs={{0,4},{1,5},{2,6},{3,7},{4,0},{5,1},{6,2},{7,3},{8,12},{9,13},{10,... | collective-permute-start | bytes 294920 | tf_op jit(solution)/shard_map/ppermute | solution.py:19
  46.6 7.8 %collective-permute-start.28 = (bf16[3,32,512]{2,1,0:T(8,128)(2,1)S(1)}, bf16[3,32,512]{2,1,0:T(8,128)(2,1)S(1)}, u32[]{:S(2)}, u32[]{:S(2)}) collective-permute-start(bf16[3,32,512]{2,1,0:T(8,128)(2,1)S(1)} %get-tuple-element.46), channel_id=1, source_target_pairs={{0,6},{1,7},{2,4},{3,5},{4,2},{5,3},{6,0},{7,1},{8,14},{9,15},{10,... | collective-permute-start | bytes 294920 | tf_op jit(solution)/shard_map/ppermute | solution.py:19
  54.5 6.8 %collective-permute-start.31 = (bf16[3,32,512]{2,1,0:T(8,128)(2,1)S(1)}, bf16[3,32,512]{2,1,0:T(8,128)(2,1)S(1)}, u32[]{:S(2)}, u32[]{:S(2)}) collective-permute-start(bf16[3,32,512]{2,1,0:T(8,128)(2,1)S(1)} %shard_map.95.refs_0_), channel_id=1, source_target_pairs={{0,24},{8,16},{16,8},{24,0},{1,25},{9,17},{17,9},{25,1},{2,26},{10... | collective-permute-start | bytes 294920 | tf_op jit(solution)/shard_map/ppermute | solution.py:19
  57.0 6.5 %collective-permute-start.30 = (bf16[3,32,512]{2,1,0:T(8,128)(2,1)S(1)}, bf16[3,32,512]{2,1,0:T(8,128)(2,1)S(1)}, u32[]{:S(2)}, u32[]{:S(2)}) collective-permute-start(bf16[3,32,512]{2,1,0:T(8,128)(2,1)S(1)} %shard_map.95.refs_0_), channel_id=1, source_target_pairs={{0,16},{8,24},{16,0},{24,8},{1,17},{9,25},{17,1},{25,9},{2,18},{10... | collective-permute-start | bytes 294920 | tf_op jit(solution)/shard_map/ppermute | solution.py:19
  58.1 8.0 %collective-permute-start.19 = (bf16[128,256]{1,0:T(8,128)(2,1)S(1)}, bf16[128,256]{1,0:T(8,128)(2,1)S(1)}, u32[]{:S(2)}, u32[]{:S(2)}) collective-permute-start(bf16[128,256]{1,0:T(8,128)(2,1)S(1)} %get-tuple-element.36), channel_id=1, source_target_pairs={{0,2},{1,3},{2,0},{3,1},{4,6},{5,7},{6,4},{7,5},{8,10},{9,11},{10,... | collective-permute-start | bytes 196616 | tf_op jit(solution)/shard_map/ppermute | solution.py:19
  60.3 9.8 %collective-permute-start.20 = (bf16[128,256]{1,0:T(8,128)(2,1)S(1)}, bf16[128,256]{1,0:T(8,128)(2,1)S(1)}, u32[]{:S(2)}, u32[]{:S(2)}) collective-permute-start(bf16[128,256]{1,0:T(8,128)(2,1)S(1)} %get-tuple-element.37), channel_id=1, source_target_pairs={{0,4},{1,5},{2,6},{3,7},{4,0},{5,1},{6,2},{7,3},{8,12},{9,13},{10,... | collective-permute-start | bytes 196616 | tf_op jit(solution)/shard_map/ppermute | solution.py:19
  61.4 8.8 %collective-permute-start.21 = (bf16[128,256]{1,0:T(8,128)(2,1)S(1)}, bf16[128,256]{1,0:T(8,128)(2,1)S(1)}, u32[]{:S(2)}, u32[]{:S(2)}) collective-permute-start(bf16[128,256]{1,0:T(8,128)(2,1)S(1)} %get-tuple-element.38), channel_id=1, source_target_pairs={{0,6},{1,7},{2,4},{3,5},{4,2},{5,3},{6,0},{7,1},{8,14},{9,15},{10,... | collective-permute-start | bytes 196616 | tf_op jit(solution)/shard_map/ppermute | solution.py:19
  63.5 13.1 %collective-permute-start.37 = (bf16[3,32,512]{2,1,0:T(8,128)(2,1)S(1)}, bf16[3,32,512]{2,1,0:T(8,128)(2,1)S(1)}, u32[]{:S(2)}, u32[]{:S(2)}) collective-permute-start(bf16[3,32,512]{2,1,0:T(8,128)(2,1)S(1)} %shard_map.96.refs_0_), channel_id=1, source_target_pairs={{0,6},{1,7},{2,4},{3,5},{4,2},{5,3},{6,0},{7,1},{8,14},{9,15},{10,... | collective-permute-start | bytes 294920 | tf_op jit(solution)/shard_map/ppermute | solution.py:19
  65.3 11.8 %collective-permute-start.35 = (bf16[3,32,512]{2,1,0:T(8,128)(2,1)S(1)}, bf16[3,32,512]{2,1,0:T(8,128)(2,1)S(1)}, u32[]{:S(2)}, u32[]{:S(2)}) collective-permute-start(bf16[3,32,512]{2,1,0:T(8,128)(2,1)S(1)} %shard_map.96.refs_0_), channel_id=1, source_target_pairs={{0,4},{1,5},{2,6},{3,7},{4,0},{5,1},{6,2},{7,3},{8,12},{9,13},{10,... | collective-permute-start | bytes 294920 | tf_op jit(solution)/shard_map/ppermute | solution.py:19
  66.1 11.1 %collective-permute-start.33 = (bf16[3,32,512]{2,1,0:T(8,128)(2,1)S(1)}, bf16[3,32,512]{2,1,0:T(8,128)(2,1)S(1)}, u32[]{:S(2)}, u32[]{:S(2)}) collective-permute-start(bf16[3,32,512]{2,1,0:T(8,128)(2,1)S(1)} %shard_map.96.refs_0_), channel_id=1, source_target_pairs={{0,2},{1,3},{2,0},{3,1},{4,6},{5,7},{6,4},{7,5},{8,10},{9,11},{10,... | collective-permute-start | bytes 294920 | tf_op jit(solution)/shard_map/ppermute | solution.py:19
  70.2 6.4 %collective-permute-start.24 = (bf16[128,256]{1,0:T(8,128)(2,1)S(1)}, bf16[128,256]{1,0:T(8,128)(2,1)S(1)}, u32[]{:S(2)}, u32[]{:S(2)}) collective-permute-start(bf16[128,256]{1,0:T(8,128)(2,1)S(1)} %shard_map.91.refs_0_), channel_id=1, source_target_pairs={{0,24},{8,16},{16,8},{24,0},{1,25},{9,17},{17,9},{25,1},{2,26},{10... | collective-permute-start | bytes 196616 | tf_op jit(solution)/shard_map/ppermute | solution.py:19
  76.6 7.0 %collective-permute-start.32 = (bf16[3,32,512]{2,1,0:T(8,128)(2,1)S(1)}, bf16[3,32,512]{2,1,0:T(8,128)(2,1)S(1)}, u32[]{:S(2)}, u32[]{:S(2)}) collective-permute-start(bf16[3,32,512]{2,1,0:T(8,128)(2,1)S(1)} %shard_map.96.refs_0_), channel_id=1, source_target_pairs={{0,1},{1,0},{2,3},{3,2},{4,5},{5,4},{6,7},{7,6},{8,9},{9,8},{10,11... | collective-permute-start | bytes 294920 | tf_op jit(solution)/shard_map/ppermute | solution.py:19
  76.6 7.0 %collective-permute-start.38 = (bf16[3,32,512]{2,1,0:T(8,128)(2,1)S(1)}, bf16[3,32,512]{2,1,0:T(8,128)(2,1)S(1)}, u32[]{:S(2)}, u32[]{:S(2)}) collective-permute-start(bf16[3,32,512]{2,1,0:T(8,128)(2,1)S(1)} %collective-permute-done.37.refs_6_), channel_id=1, source_target_pairs={{0,1},{1,0},{2,3},{3,2},{4,5},{5,4},{6,7},{7,6},{8,9},{9,8},{10,11... | collective-permute-start | bytes 294920 | tf_op jit(solution)/shard_map/ppermute | solution.py:19
  77.1 6.5 %collective-permute-start.36 = (bf16[3,32,512]{2,1,0:T(8,128)(2,1)S(1)}, bf16[3,32,512]{2,1,0:T(8,128)(2,1)S(1)}, u32[]{:S(2)}, u32[]{:S(2)}) collective-permute-start(bf16[3,32,512]{2,1,0:T(8,128)(2,1)S(1)} %collective-permute-done.35.refs_4_), channel_id=1, source_target_pairs={{0,1},{1,0},{2,3},{3,2},{4,5},{5,4},{6,7},{7,6},{8,9},{9,8},{10,11... | collective-permute-start | bytes 294920 | tf_op jit(solution)/shard_map/ppermute | solution.py:19
  77.2 6.4 %collective-permute-start.34 = (bf16[3,32,512]{2,1,0:T(8,128)(2,1)S(1)}, bf16[3,32,512]{2,1,0:T(8,128)(2,1)S(1)}, u32[]{:S(2)}, u32[]{:S(2)}) collective-permute-start(bf16[3,32,512]{2,1,0:T(8,128)(2,1)S(1)} %collective-permute-done.33.refs_2_), channel_id=1, source_target_pairs={{0,1},{1,0},{2,3},{3,2},{4,5},{5,4},{6,7},{7,6},{8,9},{9,8},{10,11... | collective-permute-start | bytes 294920 | tf_op jit(solution)/shard_map/ppermute | solution.py:19
  (21 other events, 92.5 us)

commit v2 on v1

--- a/solution.py
+++ b/solution.py
@@ -36,6 +36,12 @@
         compiler_params=pltpu.CompilerParams(vmem_limit_bytes=VMEM_LIMIT),
         cost_estimate=cost,
     )(*args)
+
+
+def cost(microseconds):
+    return pl.CostEstimate(
+        flops=int(microseconds * 1e9), bytes_accessed=int(microseconds * 3e6), transcendentals=0
+    )
 
 
 def struct(shape, dtype):
@@ -106,6 +112,14 @@
         sends[k - 1][...] = (keep[chip ^ k].astype(F32) + got[chip ^ k].astype(F32)).astype(BF16)
 
 
+def halve(keep, got, own, send):
+    chip = lax.axis_index("item") // 2
+    for k in range(0, keep.shape[0], 2):
+        own[k // 2] = keep[chip ^ k].astype(F32) + got[chip ^ k].astype(F32)
+        k += 1
+        send[k // 2] = (keep[chip ^ k].astype(F32) + got[chip ^ k].astype(F32)).astype(BF16)
+
+
 def activate(own, *refs):
     *parts, cotangent, hidden, slope = refs
     pre = own[...]
@@ -137,60 +151,152 @@
         back[pl.ds(r * group_rows, group_rows), :] = lax.dot_general(
             slopes[...], weights[r], (((1,), (1,)), ((), ())), preferred_element_type=F32
         ).astype(BF16)
-    tile = keep.shape[1]
-    for z in range(keep.shape[0]):
+    users, chips_, few, _ = keep.shape
+    tile = users * few
+    for z in range(chips_):
         both = lax.dot_general(
             dense[:, pl.ds(2 * z * tile, 2 * tile)], back[...],
             (((0,), (0,)), ((), ())), preferred_element_type=F32,
         )
         even, odd = both[:tile], both[tile:]
-        keep[z] = jnp.where(core == 0, even, odd)
-        send[z] = jnp.where(core == 0, odd, even).astype(BF16)
-
-
-def weight_terms(aggregate, slopes, keep, send):
+        mine = jnp.where(core == 0, even, odd)
+        theirs = jnp.where(core == 0, odd, even).astype(BF16)
+        for u in range(users):
+            keep[u, z] = mine[u * few:(u + 1) * few]
+            send[u, z] = theirs[u * few:(u + 1) * few]
+
+
+def transpose_terms(levels, aggregate, keep, send):
     core = lax.axis_index("item") % 2
-    levels = keep.shape[1]
+    chips, part, _ = keep.shape
+    half = chips * part
+    step = keep.shape[2] // levels
+    for r in range(levels):
+        columns = pl.ds(r * step, step)
+        turned = aggregate[columns, :].T
+        low, high = turned[:half], turned[half:]
+        mine = jnp.where(core == 0, low, high)
+        theirs = jnp.where(core == 0, high, low)
+        for z in range(chips):
+            keep[z, :, columns] = mine[z * part:(z + 1) * part]
+            send[z, :, columns] = theirs[z * part:(z + 1) * part]
+
+
+def weight_rows(slopes, keep, got, out, turned):
     group_rows = slopes.shape[0]
-    half = aggregate.shape[1] // 2
-    chips = keep.shape[0]
-    part = half // chips
-    for r in range(levels):
-        both = lax.dot_general(
-            aggregate[pl.ds(r * group_rows, group_rows), :], slopes[...],
-            (((0,), (0,)), ((), ())), preferred_element_type=F32,
-        )
-        low, high = both[:half], both[half:]
-        mine = jnp.where(core == 0, low, high)
-        theirs = jnp.where(core == 0, high, low).astype(BF16)
+    kept, part, columns = keep.shape
+    levels = columns // group_rows
+    for k in range(kept):
+        total = (keep[k] + got[k].astype(F32)).astype(BF16)
+        for r in range(levels):
+            at = (k * levels + r) * part
+            turned[at:at + part, :] = total[:, r * group_rows:(r + 1) * group_rows]
+    rows = jnp.dot(turned[...], slopes[...], preferred_element_type=F32)
+    users, _, few, lanes = out.shape
+    groups = part // few
+    for u in range(users):
+        for block in range(kept * levels):
+            first = block * part + (u % groups) * few
+            column = (u // groups) * lanes
+            out[u, block] = rows[first:first + few, column:column + lanes]
+
+
+def user_pieces(keep, got, rows, *outs):
+    user = lax.axis_index("user")
+    _, chips, few, width = keep.shape
+    _, levels, part, lanes = rows.shape
+    for k, out in enumerate(outs):
+        items = keep[user ^ k] + got[user ^ k].astype(F32)
+        at = 0
+        for column in range(0, width, lanes):
+            for z in range(chips):
+                out[at:at + few] = items[z, :, column:column + lanes].astype(out.dtype)
+                at += few
+        for r in range(levels):
+            out[at:at + part] = rows[user ^ k, r].astype(out.dtype)
+            at += part
+        if at < out.shape[0]:
+            out[at:] = jnp.zeros((out.shape[0] - at, lanes), out.dtype)
+
+
+def chip_pieces(chips, few, blocks, rows, *refs):
+    count = len(refs) - chips - 1
+    parts, outs, total = refs[:count], refs[count:-1], refs[-1]
+    chip = lax.axis_index("item") // 2
+    summed = parts[0][...]
+    for part in parts[1:]:
+        summed = summed + part[...].astype(F32)
+    for block in range(blocks):
         for z in range(chips):
-            keep[z, r] = mine[z * part:(z + 1) * part]
-            send[z, r] = theirs[z * part:(z + 1) * part]
-
-
-def round_sum(*refs):
+            at = (block * chips + z) * few
+            total[z, block * few:(block + 1) * few] = summed[at:at + few]
+    first = blocks * chips * few
+    weight = summed[first:first + rows].astype(BF16)
+    for k, out in enumerate(outs):
+        out[:blocks * few] = total[chip ^ k].astype(out.dtype)
+        out[blocks * few:blocks * few + rows] = weight.astype(out.dtype)
+        if blocks * few + rows < out.shape[0]:
+            out[blocks * few + rows:] = jnp.zeros((out.shape[0] - blocks * few - rows, out.shape[1]), out.dtype)
+
+
+def user_rows(items, rows, *refs):
     *parts, out = refs
-    total = parts[0][...].astype(F32)
+    total = parts[0][:items]
     for part in parts[1:]:
-        total = total + part[...].astype(F32)
-    out[...] = total.astype(out.dtype)
-
-
-def tree_round(*refs):
+        total = total + part[:items].astype(F32)
+    out[:items] = total.astype(BF16)
+    for k in range(len(parts)):
+        terms = []
+        for j in range(k % 2, len(parts), 2):
+            at = items + ((j ^ k) // 2) * rows
+            terms.append(parts[j][at:at + rows].astype(BF16).astype(F32))
+        out[items + k * rows:items + (k + 1) * rows] = tree_sum(terms).astype(BF16)
+    if items + len(parts) * rows < out.shape[0]:
+        out[items + len(parts) * rows:] = jnp.zeros((out.shape[0] - items - len(parts) * rows, out.shape[1]), BF16)
+
+
+def item_rows(few, *refs):
     *parts, out = refs
-    out[...] = tree_sum([part[...].astype(F32) for part in parts]).astype(out.dtype)
-
-
-def assemble(chips, scale, *refs):
-    *pieces, out = refs
+    user = lax.axis_index("user")
+    lanes = parts[0].shape[1]
+    for k, part in enumerate(parts):
+        row = pl.multiple_of((user ^ k) * few, few)
+        for block in range(out.shape[1] // lanes):
+            out[pl.ds(row, few), block * lanes:(block + 1) * lanes] = part[block * few:(block + 1) * few].astype(F32)
+
+
+def weight_out(chips, items, few, scale, *refs):
+    *pieces, out, wide = refs
     core = lax.axis_index("item") % 2
     chip = lax.axis_index("item") // 2
-    levels, part, hidden = pieces[0].shape
-    half = out.shape[1] // 2
-    for k in range(chips):
-        for other in range(2):
-            row = (core ^ other) * half + (chip ^ k) * part
-            out[:, pl.ds(pl.multiple_of(row, part), part), :] = pieces[2 * k + other][...].astype(F32) * scale
+    user = lax.axis_index("user")
+    levels, width, _ = out.shape
+    lanes = pieces[0].shape[1]
+    users = len(pieces) // 2
+    part = width // (2 * chips)
+    groups = part // few
+    for other in range(2):
+        for j in range(users):
+            piece = pieces[users * other + j]
+            for k in range(chips):
+                at = items + k * levels * few
+                for r in range(levels):
+                    block = piece[at + r * few:at + (r + 1) * few].astype(F32) * scale
+                    if groups == 1 and few % 8 == 0:
+                        row = (core ^ other) * (width // 2) + (chip ^ k) * part
+                        column = (user ^ j) * lanes
+                        out[r, pl.ds(pl.multiple_of(row, few), few),
+                            pl.ds(pl.multiple_of(column, lanes), lanes)] = block
+                    else:
+                        wide[core ^ other, chip ^ k, user ^ j, r] = block
+    if not (groups == 1 and few % 8 == 0):
+        for c in range(2):
+            for z in range(chips):
+                for u in range(users):
+                    row = c * (width // 2) + z * part + (u % groups) * few
+                    column = (u // groups) * lanes
+                    for r in range(levels):
+                        out[r, row:row + few, column:column + lanes] = wide[c, z, u, r]
 
 
 def per_device(item_features, level_weights, tile_values, tile_order, tile_counts, cotangent):
@@ -209,18 +315,20 @@
     vmem = pl.BlockSpec(memory_space=pltpu.VMEM)
     smem = pl.BlockSpec(memory_space=pltpu.SMEM)
 
-    pieces = [item_features] + [swap(item_features, "item", 2 * k) for k in range(1, chips)]
-    feature_pieces = []
-    for piece in pieces:
-        feature_pieces += [piece, swap(piece, "item", 1)]
-
+    far = [swap(item_features, "item", 2 * k) for k in range(chips - 1, 0, -1)][::-1]
     dense = call(
         functools.partial(place_tiles, block_count),
         struct((levels * group_rows, items), BF16),
         (tile_order, tile_counts, tile_values),
         scratch=[pltpu.SemaphoreType.DMA((capacity,))],
         specs=[smem, smem, pl.BlockSpec(memory_space=pl.ANY)],
-    )
+        cost=cost(4),
+    )
+    *far, dense = lax.optimization_barrier((*far, dense))
+    feature_pieces = []
+    for piece in [item_features, *far]:
+        feature_pieces += [piece, swap(piece, "item", 1)]
+
     aggregate, pre_keep, pre_send = call(
         functools.partial(forward, chips),
         (
@@ -230,73 +338,111 @@
         ),
         (dense, level_weights, *feature_pieces),
         scratch=[pltpu.VMEM((items, width), BF16)],
+        cost=cost(2),
     )
     pre_got = swap(pre_send, "item", 1)
     pre_own, *pre_sends = call(
         functools.partial(pair_sum, chips),
         (struct((share, hidden_width), F32),) + (struct((share, hidden_width), BF16),) * (chips - 1),
         (pre_keep, pre_got),
-    )
-    pre_parts = [swap(pre_sends[k - 1], "item", 2 * k) for k in range(1, chips)]
+        cost=cost(0.1),
+    )
+    aggregate, *pre_sends = lax.optimization_barrier((aggregate, *pre_sends))
+    pre_parts = [swap(pre_sends[k - 1], "item", 2 * k) for k in range(chips - 1, 0, -1)][::-1]
+
+    part = width // item_size
+    turned = struct((chips, part, levels * group_rows), BF16)
+
+    turned_keep, turned_send = call(
+        functools.partial(transpose_terms, levels), (turned, turned), (aggregate,), cost=cost(1)
+    )
+    turned_got = swap(turned_send, "item", 1)
+    turned_own, turned_send = call(
+        halve,
+        (struct((chips // 2,) + turned.shape[1:], F32), struct((chips // 2,) + turned.shape[1:], BF16)),
+        (turned_keep, turned_got),
+        cost=cost(0.1),
+    )
+    turned_got = swap(turned_send, "item", 2)
+
     hidden, slope = call(
         activate,
         (struct((share, hidden_width), BF16),) * 2,
         (pre_own, *pre_parts, cotangent),
-    )
-    pieces = [slope] + [swap(slope, "item", 2 * k) for k in range(1, chips)]
+        cost=cost(0.7),
+    )
+    far = [swap(slope, "item", 2 * k) for k in range(chips - 1, 0, -1)][::-1]
+    *far, turned_got = lax.optimization_barrier((*far, turned_got))
     slope_pieces = []
-    for piece in pieces:
+    for piece in [slope, *far]:
         slope_pieces += [piece, swap(piece, "item", 1)]
 
+    user_few = tile // user_size
     slopes, item_keep, item_send = call(
         functools.partial(backward, chips),
         (
             struct((group_rows, hidden_width), BF16),
-            struct((chips, tile, width), F32),
-            struct((chips, tile, width), BF16),
+            struct((user_size, chips, user_few, width), F32),
+            struct((user_size, chips, user_few, width), BF16),
         ),
         (dense, level_weights, *slope_pieces),
         scratch=[pltpu.VMEM((levels * group_rows, width), BF16)],
+        cost=cost(1.5),
     )
     item_got = swap(item_send, "item", 1)
-    part = width // item_size
-    grad_keep, grad_send = call(
-        weight_terms,
-        (
-            struct((chips, levels, part, hidden_width), F32),
-            struct((chips, levels, part, hidden_width), BF16),
+
+    lanes = 128
+    lane_blocks = min(hidden_width // lanes, user_size)
+    few = part * lane_blocks // user_size
+    rows = call(
+        weight_rows,
+        struct((user_size, chips // 2 * levels, few, lanes), F32),
+        (slopes, turned_own, turned_got),
+        scratch=[pltpu.VMEM((chips // 2 * levels * part, group_rows), BF16)],
+        cost=cost(0.6),
+    )
+
+    def padded(amount):
+        return -(-amount // 16) * 16
+
+    blocks = width // lanes
+    amount = padded(blocks * chips * user_few + chips // 2 * levels * few)
+    mine, *sends = call(
+        user_pieces,
+        (struct((amount, lanes), F32),) + (struct((amount, lanes), BF16),) * (user_size - 1),
+        (item_keep, item_got, rows),
+        cost=cost(0.2),
+    )
+    parts = [swap(sends[k - 1], "user", k) for k in range(user_size - 1, 0, -1)][::-1]
+    amount = padded(blocks * user_few + chips // 2 * levels * few)
+    mine, *sends = call(
+        functools.partial(chip_pieces, chips, user_few, blocks, chips // 2 * levels * few),
+        (struct((amount, lanes), F32),) + (struct((amount, lanes), BF16),) * (chips - 1),
+        (mine, *parts),
+        scratch=[pltpu.VMEM((chips, blocks * user_few, lanes), F32)],
+        cost=cost(0.1),
+    )
+    parts = [swap(sends[k - 1], "item", 2 * k) for k in range(chips - 1, 0, -1)][::-1]
+    amount = padded(blocks * user_few + chips * levels * few)
+    gathered = call(
+        functools.partial(user_rows, blocks * user_few, levels * few),
+        struct((amount, lanes), BF16),
+        (mine, *parts),
+        cost=cost(0.1),
+    )
+    gathered = [gathered] + [swap(gathered, "user", k) for k in range(user_size - 1, 0, -1)][::-1]
+    others = [swap(piece, "item", 1) for piece in gathered]
+    item_grad = call(
+        functools.partial(item_rows, user_few), struct((tile, width), F32), gathered, cost=cost(0.7)
+    )
+    weight_grad = call(
+        functools.partial(
+            weight_out, chips, blocks * user_few, few, (group_rows * user_size) ** -0.5
         ),
-        (aggregate, slopes),
-    )
-    item_own, *item_sends = call(
-        functools.partial(pair_sum, chips),
-        (struct((tile, width), F32),) + (struct((tile, width), BF16),) * (chips - 1),
-        (item_keep, item_got),
-    )
-    item_parts = [swap(item_sends[k - 1], "item", 2 * k) for k in range(1, chips)]
-    item_group = call(round_sum, struct((tile, width), BF16), (item_own, *item_parts))
-    item_all = [item_group] + [swap(item_group, "user", k) for k in range(1, user_size)]
-    item_grad = call(tree_round, struct((tile, width), F32), item_all)
-
-    grad_got = swap(grad_send, "item", 1)
-    grad_own, *grad_sends = call(
-        functools.partial(pair_sum, chips),
-        (struct((levels, part, hidden_width), F32),)
-        + (struct((levels, part, hidden_width), BF16),) * (chips - 1),
-        (grad_keep, grad_got),
-    )
-    grad_parts = [swap(grad_sends[k - 1], "item", 2 * k) for k in range(1, chips)]
-    grad_group = call(round_sum, struct((levels, part, hidden_width), BF16), (grad_own, *grad_parts))
-    grad_all = [grad_group] + [swap(grad_group, "user", k) for k in range(1, user_size)]
-    grad_piece = call(tree_round, struct((levels, part, hidden_width), BF16), grad_all)
-    pieces = [grad_piece] + [swap(grad_piece, "item", 2 * k) for k in range(1, chips)]
-    grad_pieces = []
-    for piece in pieces:
-        grad_pieces += [piece, swap(piece, "item", 1)]
-    weight_grad = call(
-        functools.partial(assemble, chips, (group_rows * user_size) ** -0.5),
         struct((levels, width, hidden_width), F32),
-        grad_pieces,
+        (*gathered, *others),
+        scratch=[pltpu.VMEM((2, chips, user_size, levels, few, lanes), F32)],
+        cost=cost(1.3),
     )
     return hidden, item_grad, weight_grad
 

time: 85.1 us -> 68.8 us (0.81)
  starting transfers between devices: 40.3 us -> 28.1 us
  waiting for transfers between devices: 32.9 us -> 29 us
    ppermute x39 -> x34, starting transfers between devices: 40.3 us -> 28.1 us  [swap(): return lax.ppermute(array, axis, partners(axis, step))]
    ppermute x39 -> x34, waiting for transfers between devices: 32.9 us -> 29 us  [swap(): return lax.ppermute(array, axis, partners(axis, step))]
  transfers between devices with their start and end apart: 39 -> 34, of which waited for: 17 -> 22; matrix products, arithmetic and copies ran while one was open for 0% -> 0% of each run, Pallas kernels for 3% -> 4%
where the time goes in v2:
time: 68.8 us; the launch traced here: 68.6 us
  waiting for transfers between devices  29 us (42%)
  starting transfers between devices  28.1 us (41%)
  Pallas kernels  8.26 us (12%)
  local copies, waits for them, and re-layouts  2.46 us (4%)
  between operations  0.75 us (1%)
    ppermute x34, waiting for transfers between devices, swap(): return lax.ppermute(array, axis, partners(axis, step))  29 us
    ppermute x34, starting transfers between devices, swap(): return lax.ppermute(array, axis, partners(axis, step))  28.1 us
    pallas_call x13, Pallas kernels, call(): pl.pallas_call(body, out_shape=out_shapes, in_specs=specs if specs is not...  8.26 us
    unnamed x12, local copies, waits for them, and re-layouts  2.46 us
  transfers between devices with their start and end apart: 34, of which 22 were waited for; matrix products, arithmetic and copies ran while one was open for 0% of the time, Pallas kernels for 4%

profile of v2, /device:TPU:0, one launch (start us, length us, event | category | flops | bytes accessed | tf_op | source)
XLA Modules:
  0.0 68.6 jit_solution(9276731162399592774)
XLA Ops:
  0.6 5.1 %collective-permute-start.2 = (bf16[128,256]{1,0:T(8,128)(2,1)}, bf16[128,256]{1,0:T(8,128)(2,1)S(1)}, u32[]{:S(2)}, u32[]{:S(2)}) collective-permute-start(bf16[128,256]{1,0:T(8,128)(2,1)} %refs_0_.1), channel_id=1, source_target_pairs={{0,6},{1,7},{2,4},{3,5},{4,2},{5,3},{6,0},{7,1},{8,14},{9,15},{10,... | collective-permute-start | bytes 196616 | tf_op jit(solution)/shard_map/ppermute | solution.py:19
  8.8 1.3 %shard_map.85.dense = bf16[1536,1024]{1,0:T(8,128)(2,1)S(1)} custom-call(s32[1,96]{1,0:T(1,128)S(1)} %copy-done.4, s32[1,8]{1,0:T(1,128)S(1)} %copy-done.5, bf16[1,1,24,128,128]{4,3,2,1,0:T(8,128)(2,1)S(1)} %copy-done), custom_call_target="tpu_custom_call" | custom-call | flops 4000000000 | bytes 12000000 | tf_op jit(solution)/shard_map/pallas_call | solution.py:30
  10.2 1.4 %collective-permute-done.1.refs_4_ = bf16[128,256]{1,0:T(8,128)(2,1)S(1)} collective-permute-done((bf16[128,256]{1,0:T(8,128)(2,1)}, bf16[128,256]{1,0:T(8,128)(2,1)S(1)}, u32[]{:S(2)}, u32[]{:S(2)}) %collective-permute-start.1) | collective-permute-done | bytes 65568 | tf_op jit(solution)/shard_map/ppermute | solution.py:19
  13.3 1.9 %shard_map.86 = (bf16[1536,256]{1,0:T(8,128)(2,1)S(1)}, f32[4,64,512]{2,1,0:T(8,128)S(1)}, bf16[4,64,512]{2,1,0:T(8,128)(2,1)S(1)}) custom-call(bf16[1536,1024]{1,0:T(8,128)(2,1)S(1)} %shard_map.85.dense, bf16[3,256,512]{2,1,0:T(8,128)(2,1)S(1)} %copy-done.1, bf16[128,256]{1,0:T(8,128)(2,1)S(1)} %copy-done.2, ...), custom_call_target="tpu_custom_call" | custom-call | flops 2000000000 | bytes 6000000 | tf_op jit(solution)/shard_map/pallas_call | solution.py:30
  15.5 1.4 %collective-permute-done.7.got = bf16[4,64,512]{2,1,0:T(8,128)(2,1)S(1)} collective-permute-done((bf16[4,64,512]{2,1,0:T(8,128)(2,1)S(1)}, bf16[4,64,512]{2,1,0:T(8,128)(2,1)S(1)}, u32[]{:S(2)}, u32[]{:S(2)}) %collective-permute-start.7) | collective-permute-done | bytes 262176 | tf_op jit(solution)/shard_map/ppermute | solution.py:19
  18.5 2.2 %collective-permute-start.9 = (bf16[64,512]{1,0:T(8,128)(2,1)S(1)}, bf16[64,512]{1,0:T(8,128)(2,1)S(1)}, u32[]{:S(2)}, u32[]{:S(2)}) collective-permute-start(bf16[64,512]{1,0:T(8,128)(2,1)S(1)} %get-tuple-element.51), channel_id=1, source_target_pairs={{0,4},{1,5},{2,6},{3,7},{4,0},{5,1},{6,2},{7,3},{8,12},{9,13},{10,... | collective-permute-start | bytes 196616 | tf_op jit(solution)/shard_map/ppermute | solution.py:19
  22.1 4.0 %collective-permute-done.9.refs_1_ = bf16[64,512]{1,0:T(8,128)(2,1)S(1)} collective-permute-done((bf16[64,512]{1,0:T(8,128)(2,1)S(1)}, bf16[64,512]{1,0:T(8,128)(2,1)S(1)}, u32[]{:S(2)}, u32[]{:S(2)}) %collective-permute-start.9) | collective-permute-done | bytes 65568 | tf_op jit(solution)/shard_map/ppermute | solution.py:19
  26.2 1.3 %collective-permute-done.10.refs_2_ = bf16[64,512]{1,0:T(8,128)(2,1)S(1)} collective-permute-done((bf16[64,512]{1,0:T(8,128)(2,1)S(1)}, bf16[64,512]{1,0:T(8,128)(2,1)S(1)}, u32[]{:S(2)}, u32[]{:S(2)}) %collective-permute-start.10) | collective-permute-done | bytes 65568 | tf_op jit(solution)/shard_map/ppermute | solution.py:19
  28.2 1.5 %collective-permute-start.14 = (bf16[64,512]{1,0:T(8,128)(2,1)S(1)}, bf16[64,512]{1,0:T(8,128)(2,1)S(1)}, u32[]{:S(2)}, u32[]{:S(2)}) collective-permute-start(bf16[64,512]{1,0:T(8,128)(2,1)S(1)} %get-tuple-element.54.refs_0_), channel_id=1, source_target_pairs={{0,6},{1,7},{2,4},{3,5},{4,2},{5,3},{6,0},{7,1},{8,14},{9,15},{10,... | collective-permute-start | bytes 196616 | tf_op jit(solution)/shard_map/ppermute | solution.py:19
  30.4 2.2 %collective-permute-start.12 = (bf16[64,512]{1,0:T(8,128)(2,1)S(1)}, bf16[64,512]{1,0:T(8,128)(2,1)S(1)}, u32[]{:S(2)}, u32[]{:S(2)}) collective-permute-start(bf16[64,512]{1,0:T(8,128)(2,1)S(1)} %get-tuple-element.54.refs_0_), channel_id=1, source_target_pairs={{0,2},{1,3},{2,0},{3,1},{4,6},{5,7},{6,4},{7,5},{8,10},{9,11},{10,... | collective-permute-start | bytes 196616 | tf_op jit(solution)/shard_map/ppermute | solution.py:19
  32.6 1.7 %collective-permute-done.14.refs_6_ = bf16[64,512]{1,0:T(8,128)(2,1)S(1)} collective-permute-done((bf16[64,512]{1,0:T(8,128)(2,1)S(1)}, bf16[64,512]{1,0:T(8,128)(2,1)S(1)}, u32[]{:S(2)}, u32[]{:S(2)}) %collective-permute-start.14) | collective-permute-done | bytes 65568 | tf_op jit(solution)/shard_map/ppermute | solution.py:19
  34.3 1.4 %collective-permute-done.13.refs_4_ = bf16[64,512]{1,0:T(8,128)(2,1)S(1)} collective-permute-done((bf16[64,512]{1,0:T(8,128)(2,1)S(1)}, bf16[64,512]{1,0:T(8,128)(2,1)S(1)}, u32[]{:S(2)}, u32[]{:S(2)}) %collective-permute-start.13) | collective-permute-done | bytes 65568 | tf_op jit(solution)/shard_map/ppermute | solution.py:19
  37.5 1.4 %shard_map.91 = (bf16[512,512]{1,0:T(8,128)(2,1)S(1)}, f32[4,4,32,256]{3,2,1,0:T(8,128)S(1)}, bf16[4,4,32,256]{3,2,1,0:T(8,128)(2,1)S(1)}) custom-call(bf16[1536,1024]{1,0:T(8,128)(2,1)S(1)} %shard_map.85.dense, bf16[3,256,512]{2,1,0:T(8,128)(2,1)S(1)} %copy-done.1, bf16[64,512]{1,0:T(8,128)(2,1)S(1)} %get-tuple-element.54.refs_0_, ...), custom_call_target="tpu_custom_call" | custom-call | flops 1500000000 | bytes 4500000 | tf_op jit(solution)/shard_map/pallas_call | solution.py:30
  40.6 1.6 %collective-permute-start.21 = (bf16[448,128]{1,0:T(8,128)(2,1)S(1)}, bf16[448,128]{1,0:T(8,128)(2,1)S(1)}, u32[]{:S(2)}, u32[]{:S(2)}) collective-permute-start(bf16[448,128]{1,0:T(8,128)(2,1)S(1)} %get-tuple-element.68), channel_id=1, source_target_pairs={{0,8},{8,0},{16,24},{24,16},{1,9},{9,1},{17,25},{25,17},{2,10},{10... | collective-permute-start | bytes 344072 | tf_op jit(solution)/shard_map/ppermute | solution.py:19
  42.2 1.5 %collective-permute-start.22 = (bf16[448,128]{1,0:T(8,128)(2,1)S(1)}, bf16[448,128]{1,0:T(8,128)(2,1)S(1)}, u32[]{:S(2)}, u32[]{:S(2)}) collective-permute-start(bf16[448,128]{1,0:T(8,128)(2,1)S(1)} %get-tuple-element.69), channel_id=1, source_target_pairs={{0,16},{8,24},{16,0},{24,8},{1,17},{9,25},{17,1},{25,9},{2,18},{10... | collective-permute-start | bytes 344072 | tf_op jit(solution)/shard_map/ppermute | solution.py:19
  44.2 1.7 %collective-permute-done.21.refs_1_ = bf16[448,128]{1,0:T(8,128)(2,1)S(1)} collective-permute-done((bf16[448,128]{1,0:T(8,128)(2,1)S(1)}, bf16[448,128]{1,0:T(8,128)(2,1)S(1)}, u32[]{:S(2)}, u32[]{:S(2)}) %collective-permute-start.21) | collective-permute-done | bytes 114720 | tf_op jit(solution)/shard_map/ppermute | solution.py:19
  45.9 3.7 %collective-permute-done.22.refs_2_ = bf16[448,128]{1,0:T(8,128)(2,1)S(1)} collective-permute-done((bf16[448,128]{1,0:T(8,128)(2,1)S(1)}, bf16[448,128]{1,0:T(8,128)(2,1)S(1)}, u32[]{:S(2)}, u32[]{:S(2)}) %collective-permute-start.22) | collective-permute-done | bytes 114720 | tf_op jit(solution)/shard_map/ppermute | solution.py:19
  52.0 2.0 %collective-permute-start.26 = (bf16[256,128]{1,0:T(8,128)(2,1)S(1)}, bf16[256,128]{1,0:T(8,128)(2,1)S(1)}, u32[]{:S(2)}, u32[]{:S(2)}) collective-permute-start(bf16[256,128]{1,0:T(8,128)(2,1)S(1)} %get-tuple-element.74), channel_id=1, source_target_pairs={{0,6},{1,7},{2,4},{3,5},{4,2},{5,3},{6,0},{7,1},{8,14},{9,15},{10,... | collective-permute-start | bytes 196616 | tf_op jit(solution)/shard_map/ppermute | solution.py:19
  54.3 2.4 %collective-permute-done.25.refs_2_ = bf16[256,128]{1,0:T(8,128)(2,1)S(1)} collective-permute-done((bf16[256,128]{1,0:T(8,128)(2,1)S(1)}, bf16[256,128]{1,0:T(8,128)(2,1)S(1)}, u32[]{:S(2)}, u32[]{:S(2)}) %collective-permute-start.25) | collective-permute-done | bytes 65568 | tf_op jit(solution)/shard_map/ppermute | solution.py:19
  56.7 1.4 %collective-permute-done.26.refs_3_ = bf16[256,128]{1,0:T(8,128)(2,1)S(1)} collective-permute-done((bf16[256,128]{1,0:T(8,128)(2,1)S(1)}, bf16[256,128]{1,0:T(8,128)(2,1)S(1)}, u32[]{:S(2)}, u32[]{:S(2)}) %collective-permute-start.26) | collective-permute-done | bytes 65568 | tf_op jit(solution)/shard_map/ppermute | solution.py:19
  58.1 1.7 %collective-permute-start.29 = (bf16[448,128]{1,0:T(8,128)(2,1)S(1)}, bf16[448,128]{1,0:T(8,128)(2,1)S(1)}, u32[]{:S(2)}, u32[]{:S(2)}) collective-permute-start(bf16[448,128]{1,0:T(8,128)(2,1)S(1)} %shard_map.95.refs_0_), channel_id=1, source_target_pairs={{0,24},{8,16},{16,8},{24,0},{1,25},{9,17},{17,9},{25,1},{2,26},{10... | collective-permute-start | bytes 344072 | tf_op jit(solution)/shard_map/ppermute | solution.py:19
  59.8 1.3 %collective-permute-start.28 = (bf16[448,128]{1,0:T(8,128)(2,1)S(1)}, bf16[448,128]{1,0:T(8,128)(2,1)S(1)}, u32[]{:S(2)}, u32[]{:S(2)}) collective-permute-start(bf16[448,128]{1,0:T(8,128)(2,1)S(1)} %shard_map.95.refs_0_), channel_id=1, source_target_pairs={{0,16},{8,24},{16,0},{24,8},{1,17},{9,25},{17,1},{25,9},{2,18},{10... | collective-permute-start | bytes 344072 | tf_op jit(solution)/shard_map/ppermute | solution.py:19
  61.7 2.3 %collective-permute-done.29.refs_3_ = bf16[448,128]{1,0:T(8,128)(2,1)S(1)} collective-permute-done((bf16[448,128]{1,0:T(8,128)(2,1)S(1)}, bf16[448,128]{1,0:T(8,128)(2,1)S(1)}, u32[]{:S(2)}, u32[]{:S(2)}) %collective-permute-start.29) | collective-permute-done | bytes 114720 | tf_op jit(solution)/shard_map/ppermute | solution.py:19
  67.2 1.4 %shard_map.97 = f32[3,256,512]{2,1,0:T(8,128)} custom-call(bf16[448,128]{1,0:T(8,128)(2,1)S(1)} %shard_map.95.refs_0_, bf16[448,128]{1,0:T(8,128)(2,1)S(1)} %collective-permute-done.27.refs_1_, bf16[448,128]{1,0:T(8,128)(2,1)S(1)} %collective-permute-done.28.refs_2_, bf16[448,128]{1,0:T(8,128)(2,1)S(1)} %collective-permute-done.29.refs_3_, ...), custom_call_target="tpu_custom_call" | custom-call | flops 1300000000 | bytes 3900000 | tf_op jit(solution)/shard_map/pallas_call | solution.py:30
  (69 shorter events, 20.0 us)
Async XLA Ops:
  0.6 9.5 %collective-permute-start.2 = (bf16[128,256]{1,0:T(8,128)(2,1)}, bf16[128,256]{1,0:T(8,128)(2,1)S(1)}, u32[]{:S(2)}, u32[]{:S(2)}) collective-permute-start(bf16[128,256]{1,0:T(8,128)(2,1)} %refs_0_.1), channel_id=1, source_target_pairs={{0,6},{1,7},{2,4},{3,5},{4,2},{5,3},{6,0},{7,1},{8,14},{9,15},{10,... | collective-permute-start | bytes 196616 | tf_op jit(solution)/shard_map/ppermute | solution.py:19
  5.7 5.8 %collective-permute-start.1 = (bf16[128,256]{1,0:T(8,128)(2,1)}, bf16[128,256]{1,0:T(8,128)(2,1)S(1)}, u32[]{:S(2)}, u32[]{:S(2)}) collective-permute-start(bf16[128,256]{1,0:T(8,128)(2,1)} %refs_0_.1), channel_id=1, source_target_pairs={{0,4},{1,5},{2,6},{3,7},{4,0},{5,1},{6,2},{7,3},{8,12},{9,13},{10,... | collective-permute-start | bytes 196616 | tf_op jit(solution)/shard_map/ppermute | solution.py:19
  5.7 5.8 %collective-permute-start = (bf16[128,256]{1,0:T(8,128)(2,1)}, bf16[128,256]{1,0:T(8,128)(2,1)S(1)}, u32[]{:S(2)}, u32[]{:S(2)}) collective-permute-start(bf16[128,256]{1,0:T(8,128)(2,1)} %refs_0_.1), channel_id=1, source_target_pairs={{0,2},{1,3},{2,0},{3,1},{4,6},{5,7},{6,4},{7,5},{8,10},{9,11},{10,... | collective-permute-start | bytes 196616 | tf_op jit(solution)/shard_map/ppermute | solution.py:19
  6.4 5.7 %collective-permute-start.3 = (bf16[128,256]{1,0:T(8,128)(2,1)}, bf16[128,256]{1,0:T(8,128)(2,1)S(1)}, u32[]{:S(2)}, u32[]{:S(2)}) collective-permute-start(bf16[128,256]{1,0:T(8,128)(2,1)} %refs_0_.1), channel_id=1, source_target_pairs={{0,1},{1,0},{2,3},{3,2},{4,5},{5,4},{6,7},{7,6},{8,9},{9,8},{10,11... | collective-permute-start | bytes 196616 | tf_op jit(solution)/shard_map/ppermute | solution.py:19
  17.2 4.6 %collective-permute-start.15 = (bf16[4,32,1536]{2,1,0:T(8,128)(2,1)S(1)}, bf16[4,32,1536]{2,1,0:T(8,128)(2,1)S(1)}, u32[]{:S(2)}, u32[]{:S(2)}) collective-permute-start(bf16[4,32,1536]{2,1,0:T(8,128)(2,1)S(1)} %get-tuple-element.57), channel_id=1, source_target_pairs={{0,1},{1,0},{2,3},{3,2},{4,5},{5,4},{6,7},{7,6},{8,9},{9,8},{10,11... | collective-permute-start | bytes 1179656 | tf_op jit(solution)/shard_map/ppermute | solution.py:19
  17.4 4.7 %collective-permute-start.8 = (bf16[64,512]{1,0:T(8,128)(2,1)S(1)}, bf16[64,512]{1,0:T(8,128)(2,1)S(1)}, u32[]{:S(2)}, u32[]{:S(2)}) collective-permute-start(bf16[64,512]{1,0:T(8,128)(2,1)S(1)} %get-tuple-element.50), channel_id=1, source_target_pairs={{0,2},{1,3},{2,0},{3,1},{4,6},{5,7},{6,4},{7,5},{8,10},{9,11},{10,... | collective-permute-start | bytes 196616 | tf_op jit(solution)/shard_map/ppermute | solution.py:19
  18.5 7.7 %collective-permute-start.9 = (bf16[64,512]{1,0:T(8,128)(2,1)S(1)}, bf16[64,512]{1,0:T(8,128)(2,1)S(1)}, u32[]{:S(2)}, u32[]{:S(2)}) collective-permute-start(bf16[64,512]{1,0:T(8,128)(2,1)S(1)} %get-tuple-element.51), channel_id=1, source_target_pairs={{0,4},{1,5},{2,6},{3,7},{4,0},{5,1},{6,2},{7,3},{8,12},{9,13},{10,... | collective-permute-start | bytes 196616 | tf_op jit(solution)/shard_map/ppermute | solution.py:19
  20.7 6.8 %collective-permute-start.10 = (bf16[64,512]{1,0:T(8,128)(2,1)S(1)}, bf16[64,512]{1,0:T(8,128)(2,1)S(1)}, u32[]{:S(2)}, u32[]{:S(2)}) collective-permute-start(bf16[64,512]{1,0:T(8,128)(2,1)S(1)} %get-tuple-element.52), channel_id=1, source_target_pairs={{0,6},{1,7},{2,4},{3,5},{4,2},{5,3},{6,0},{7,1},{8,14},{9,15},{10,... | collective-permute-start | bytes 196616 | tf_op jit(solution)/shard_map/ppermute | solution.py:19
  21.9 13.8 %collective-permute-start.16 = (bf16[2,32,1536]{2,1,0:T(8,128)(2,1)S(1)}, bf16[2,32,1536]{2,1,0:T(8,128)(2,1)S(1)}, u32[]{:S(2)}, u32[]{:S(2)}) collective-permute-start(bf16[2,32,1536]{2,1,0:T(8,128)(2,1)S(1)} %get-tuple-element.58), channel_id=1, source_target_pairs={{0,2},{1,3},{2,0},{3,1},{4,6},{5,7},{6,4},{7,5},{8,10},{9,11},{10,... | collective-permute-start | bytes 589832 | tf_op jit(solution)/shard_map/ppermute | solution.py:19
  28.2 6.1 %collective-permute-start.14 = (bf16[64,512]{1,0:T(8,128)(2,1)S(1)}, bf16[64,512]{1,0:T(8,128)(2,1)S(1)}, u32[]{:S(2)}, u32[]{:S(2)}) collective-permute-start(bf16[64,512]{1,0:T(8,128)(2,1)S(1)} %get-tuple-element.54.refs_0_), channel_id=1, source_target_pairs={{0,6},{1,7},{2,4},{3,5},{4,2},{5,3},{6,0},{7,1},{8,14},{9,15},{10,... | collective-permute-start | bytes 196616 | tf_op jit(solution)/shard_map/ppermute | solution.py:19
  29.7 6.0 %collective-permute-start.13 = (bf16[64,512]{1,0:T(8,128)(2,1)S(1)}, bf16[64,512]{1,0:T(8,128)(2,1)S(1)}, u32[]{:S(2)}, u32[]{:S(2)}) collective-permute-start(bf16[64,512]{1,0:T(8,128)(2,1)S(1)} %get-tuple-element.54.refs_0_), channel_id=1, source_target_pairs={{0,4},{1,5},{2,6},{3,7},{4,0},{5,1},{6,2},{7,3},{8,12},{9,13},{10,... | collective-permute-start | bytes 196616 | tf_op jit(solution)/shard_map/ppermute | solution.py:19
  30.4 5.3 %collective-permute-start.12 = (bf16[64,512]{1,0:T(8,128)(2,1)S(1)}, bf16[64,512]{1,0:T(8,128)(2,1)S(1)}, u32[]{:S(2)}, u32[]{:S(2)}) collective-permute-start(bf16[64,512]{1,0:T(8,128)(2,1)S(1)} %get-tuple-element.54.refs_0_), channel_id=1, source_target_pairs={{0,2},{1,3},{2,0},{3,1},{4,6},{5,7},{6,4},{7,5},{8,10},{9,11},{10,... | collective-permute-start | bytes 196616 | tf_op jit(solution)/shard_map/ppermute | solution.py:19
  32.6 3.7 %collective-permute-start.11 = (bf16[64,512]{1,0:T(8,128)(2,1)S(1)}, bf16[64,512]{1,0:T(8,128)(2,1)S(1)}, u32[]{:S(2)}, u32[]{:S(2)}) collective-permute-start(bf16[64,512]{1,0:T(8,128)(2,1)S(1)} %get-tuple-element.54.refs_0_), channel_id=1, source_target_pairs={{0,1},{1,0},{2,3},{3,2},{4,5},{5,4},{6,7},{7,6},{8,9},{9,8},{10,11... | collective-permute-start | bytes 196616 | tf_op jit(solution)/shard_map/ppermute | solution.py:19
  40.6 5.3 %collective-permute-start.21 = (bf16[448,128]{1,0:T(8,128)(2,1)S(1)}, bf16[448,128]{1,0:T(8,128)(2,1)S(1)}, u32[]{:S(2)}, u32[]{:S(2)}) collective-permute-start(bf16[448,128]{1,0:T(8,128)(2,1)S(1)} %get-tuple-element.68), channel_id=1, source_target_pairs={{0,8},{8,0},{16,24},{24,16},{1,9},{9,1},{17,25},{25,17},{2,10},{10... | collective-permute-start | bytes 344072 | tf_op jit(solution)/shard_map/ppermute | solution.py:19
  42.2 7.4 %collective-permute-start.22 = (bf16[448,128]{1,0:T(8,128)(2,1)S(1)}, bf16[448,128]{1,0:T(8,128)(2,1)S(1)}, u32[]{:S(2)}, u32[]{:S(2)}) collective-permute-start(bf16[448,128]{1,0:T(8,128)(2,1)S(1)} %get-tuple-element.69), channel_id=1, source_target_pairs={{0,16},{8,24},{16,0},{24,8},{1,17},{9,25},{17,1},{25,9},{2,18},{10... | collective-permute-start | bytes 344072 | tf_op jit(solution)/shard_map/ppermute | solution.py:19
  43.7 5.8 %collective-permute-start.23 = (bf16[448,128]{1,0:T(8,128)(2,1)S(1)}, bf16[448,128]{1,0:T(8,128)(2,1)S(1)}, u32[]{:S(2)}, u32[]{:S(2)}) collective-permute-start(bf16[448,128]{1,0:T(8,128)(2,1)S(1)} %get-tuple-element.70), channel_id=1, source_target_pairs={{0,24},{8,16},{16,8},{24,0},{1,25},{9,17},{17,9},{25,1},{2,26},{10... | collective-permute-start | bytes 344072 | tf_op jit(solution)/shard_map/ppermute | solution.py:19
  49.6 4.6 %collective-permute-start.24 = (bf16[256,128]{1,0:T(8,128)(2,1)S(1)}, bf16[256,128]{1,0:T(8,128)(2,1)S(1)}, u32[]{:S(2)}, u32[]{:S(2)}) collective-permute-start(bf16[256,128]{1,0:T(8,128)(2,1)S(1)} %get-tuple-element.72), channel_id=1, source_target_pairs={{0,2},{1,3},{2,0},{3,1},{4,6},{5,7},{6,4},{7,5},{8,10},{9,11},{10,... | collective-permute-start | bytes 196616 | tf_op jit(solution)/shard_map/ppermute | solution.py:19
  50.8 5.9 %collective-permute-start.25 = (bf16[256,128]{1,0:T(8,128)(2,1)S(1)}, bf16[256,128]{1,0:T(8,128)(2,1)S(1)}, u32[]{:S(2)}, u32[]{:S(2)}) collective-permute-start(bf16[256,128]{1,0:T(8,128)(2,1)S(1)} %get-tuple-element.73), channel_id=1, source_target_pairs={{0,4},{1,5},{2,6},{3,7},{4,0},{5,1},{6,2},{7,3},{8,12},{9,13},{10,... | collective-permute-start | bytes 196616 | tf_op jit(solution)/shard_map/ppermute | solution.py:19
  52.0 6.1 %collective-permute-start.26 = (bf16[256,128]{1,0:T(8,128)(2,1)S(1)}, bf16[256,128]{1,0:T(8,128)(2,1)S(1)}, u32[]{:S(2)}, u32[]{:S(2)}) collective-permute-start(bf16[256,128]{1,0:T(8,128)(2,1)S(1)} %get-tuple-element.74), channel_id=1, source_target_pairs={{0,6},{1,7},{2,4},{3,5},{4,2},{5,3},{6,0},{7,1},{8,14},{9,15},{10,... | collective-permute-start | bytes 196616 | tf_op jit(solution)/shard_map/ppermute | solution.py:19
  58.1 5.8 %collective-permute-start.29 = (bf16[448,128]{1,0:T(8,128)(2,1)S(1)}, bf16[448,128]{1,0:T(8,128)(2,1)S(1)}, u32[]{:S(2)}, u32[]{:S(2)}) collective-permute-start(bf16[448,128]{1,0:T(8,128)(2,1)S(1)} %shard_map.95.refs_0_), channel_id=1, source_target_pairs={{0,24},{8,16},{16,8},{24,0},{1,25},{9,17},{17,9},{25,1},{2,26},{10... | collective-permute-start | bytes 344072 | tf_op jit(solution)/shard_map/ppermute | solution.py:19
  59.8 5.3 %collective-permute-start.28 = (bf16[448,128]{1,0:T(8,128)(2,1)S(1)}, bf16[448,128]{1,0:T(8,128)(2,1)S(1)}, u32[]{:S(2)}, u32[]{:S(2)}) collective-permute-start(bf16[448,128]{1,0:T(8,128)(2,1)S(1)} %shard_map.95.refs_0_), channel_id=1, source_target_pairs={{0,16},{8,24},{16,0},{24,8},{1,17},{9,25},{17,1},{25,9},{2,18},{10... | collective-permute-start | bytes 344072 | tf_op jit(solution)/shard_map/ppermute | solution.py:19
  61.1 4.8 %collective-permute-start.27 = (bf16[448,128]{1,0:T(8,128)(2,1)S(1)}, bf16[448,128]{1,0:T(8,128)(2,1)S(1)}, u32[]{:S(2)}, u32[]{:S(2)}) collective-permute-start(bf16[448,128]{1,0:T(8,128)(2,1)S(1)} %shard_map.95.refs_0_), channel_id=1, source_target_pairs={{0,8},{8,0},{16,24},{24,16},{1,9},{9,1},{17,25},{25,17},{2,10},{10... | collective-permute-start | bytes 344072 | tf_op jit(solution)/shard_map/ppermute | solution.py:19
  61.7 4.8 %collective-permute-start.30 = (bf16[448,128]{1,0:T(8,128)(2,1)S(1)}, bf16[448,128]{1,0:T(8,128)(2,1)S(1)}, u32[]{:S(2)}, u32[]{:S(2)}) collective-permute-start(bf16[448,128]{1,0:T(8,128)(2,1)S(1)} %shard_map.95.refs_0_), channel_id=1, source_target_pairs={{0,1},{1,0},{2,3},{3,2},{4,5},{5,4},{6,7},{7,6},{8,9},{9,8},{10,11... | collective-permute-start | bytes 344072 | tf_op jit(solution)/shard_map/ppermute | solution.py:19
  64.0 2.6 %collective-permute-start.33 = (bf16[448,128]{1,0:T(8,128)(2,1)S(1)}, bf16[448,128]{1,0:T(8,128)(2,1)S(1)}, u32[]{:S(2)}, u32[]{:S(2)}) collective-permute-start(bf16[448,128]{1,0:T(8,128)(2,1)S(1)} %collective-permute-done.29.refs_3_), channel_id=1, source_target_pairs={{0,1},{1,0},{2,3},{3,2},{4,5},{5,4},{6,7},{7,6},{8,9},{9,8},{10,11... | collective-permute-start | bytes 344072 | tf_op jit(solution)/shard_map/ppermute | solution.py:19
  (16 other events, 37.5 us)

commit v3 on v2

v3 whole, which is shorter than its diff:
```python
import functools
import jax
import jax.numpy as jnp
from jax import lax
from jax.experimental import pallas as pl
from jax.experimental.pallas import tpu as pltpu
from jax.sharding import PartitionSpec as P

BF16 = jnp.bfloat16
F32 = jnp.float32
VMEM_LIMIT = 24 * 1024 * 1024


def partners(axis, step):
    return [(i, i ^ step) for i in range(lax.axis_size(axis))]


def swap(array, axis, step):
    return lax.ppermute(array, axis, partners(axis, step))


def tree_sum(parts):
    while len(parts) > 1:
        parts = [parts[i] + parts[i + 1] for i in range(0, len(parts), 2)]
    return parts[0]


def call(body, out_shapes, args, scratch=(), specs=None, cost=None):
    vmem = pl.BlockSpec(memory_space=pltpu.VMEM)
    return pl.pallas_call(
        body,
        out_shape=out_shapes,
        in_specs=specs if specs is not None else [vmem] * len(args),
        out_specs=jax.tree.map(lambda _: vmem, out_shapes),
        scratch_shapes=list(scratch),
        compiler_params=pltpu.CompilerParams(vmem_limit_bytes=VMEM_LIMIT),
        cost_estimate=cost,
    )(*args)


def cost(microseconds):
    return pl.CostEstimate(
        flops=int(microseconds * 1e9), bytes_accessed=int(microseconds * 3e6), transcendentals=0
    )


def struct(shape, dtype):
    return jax.ShapeDtypeStruct(shape, dtype)


def place_tiles(block_count, order, counts, mine, theirs, dense, sems):
    tile = mine.shape[-1]
    capacity, strips, _, share = mine.shape[1:5]
    chips = counts.shape[1] // 2
    user_blocks = chips // strips
    cell = lax.axis_index("item")
    dense[...] = jnp.zeros_like(dense)
    copies = []
    for other, tiles in enumerate((mine, theirs)):
        before = jnp.int32(0)
        for c in range(counts.shape[1]):
            before = before + jnp.where(c < (cell ^ other), counts[0, c], 0)
        holding = counts[0, cell ^ other]
        for t in range(capacity):
            copies.append((other, tiles, t, before, holding))

    def copy(number, strip):
        other, tiles, t, before, _ = copies[number]
        slot = order[0, jnp.minimum(before + t, order.shape[1] - 1)]
        target, block = slot // block_count, slot % block_count
        level, user_block = target // user_blocks, target % user_blocks
        row = (level * chips + user_block * strips + strip) * share
        column = ((block % 2) * chips + block // 2) * tile
        return pltpu.make_async_copy(
            tiles.at[0, t, strip],
            dense.at[:, pl.ds(pl.multiple_of(row, share), share),
                     pl.ds(pl.multiple_of(column, tile), tile)],
            sems.at[number * strips + strip],
        )

    for number, (_, _, t, _, holding) in enumerate(copies):
        @pl.when(t < holding)
        def _():
            for strip in range(strips):
                copy(number, strip).start()
    for number, (_, _, t, _, holding) in enumerate(copies):
        @pl.when(t < holding)
        def _():
            for strip in range(strips):
                copy(number, strip).wait()


def forward(chips, dense, weights, *refs):
    pieces = refs[: 2 * chips]
    features, own, *sends, pre = refs[2 * chips:]
    core = lax.axis_index("item") % 2
    chip = lax.axis_index("item") // 2
    levels, _, hidden = weights.shape
    tile = pieces[0].shape[0]
    for k in range(chips):
        for other in range(2):
            row = ((core ^ other) * chips + (chip ^ k)) * tile
            features[pl.ds(pl.multiple_of(row, tile), tile), :] = pieces[2 * k + other][...]
    rows = dense.shape[1] // levels
    total = jnp.zeros((rows, hidden), F32)
    for r in range(levels):
        block = jnp.dot(
            dense[core, r * rows:(r + 1) * rows, :], features[...], preferred_element_type=F32
        )
        total = total + jnp.dot(block.astype(BF16), weights[r], preferred_element_type=F32)
    pre[...] = total.reshape(pre.shape)
    own[...] = pre[chip]
    for k in range(1, chips):
        sends[k - 1][...] = pre[chip ^ k].astype(BF16)


def turn(levels, dense, features, own, send, turned):
    core = lax.axis_index("item") % 2
    chip = lax.axis_index("item") // 2
    chips, part, _ = turned.shape
    half = chips * part
    rows = dense.shape[1] // levels
    columns = features[:, pl.ds(pl.multiple_of(core * half, half), half)]
    for p in range(2):
        for r in range(levels):
            block = jnp.dot(
                dense[p, r * rows:(r + 1) * rows, :], columns, preferred_element_type=F32
            )
            at = (p * levels + r) * rows
            turned[:, :, at:at + rows] = block.T.reshape(chips, part, rows)
    for k in range(0, chips, 2):
        own[k // 2] = turned[chip ^ k]
        send[k // 2] = turned[chip ^ (k + 1)].astype(BF16)


def slopes_of(own, *refs):
    *parts, cotangent, pre_out, slope = refs
    pre = own[...]
    for part in parts:
        pre = pre + part[...].astype(F32)
    sigmoid = 1.0 / (1.0 + jnp.exp(-pre))
    pre_out[...] = pre
    slope[...] = (cotangent[...].astype(F32) * (sigmoid * (1.0 + pre * (1.0 - sigmoid)))).astype(BF16)


def activate(pre, hidden):
    hidden[...] = (pre[...] / (1.0 + jnp.exp(-pre[...]))).astype(BF16)


def backward(chips, other, dense, weights, *refs):
    pieces = refs[:chips]
    *before, slopes, items = refs[chips:]
    core = lax.axis_index("item") % 2
    chip = lax.axis_index("item") // 2
    levels, width, _ = weights.shape
    share = pieces[0].shape[0]
    for k in range(chips):
        slopes[pl.ds(pl.multiple_of((chip ^ k) * share, share), share), :] = pieces[k][...]
    rows = chips * share
    half = dense.shape[2] // 2
    columns = pl.ds(pl.multiple_of(core * half, half), half)
    total = jnp.zeros((half, width), F32)
    for r in range(levels):
        back = lax.dot_general(
            slopes[...], weights[r], (((1,), (1,)), ((), ())), preferred_element_type=F32
        ).astype(BF16)
        total = total + lax.dot_general(
            dense[core ^ other, r * rows:(r + 1) * rows, columns], back,
            (((0,), (0,)), ((), ())), preferred_element_type=F32,
        )
    total = total.reshape(items.shape)
    if before:
        total = total + before[0][...]
    items[...] = total


def weight_rows(levels, mine, theirs, keep, got, out, turned):
    core = lax.axis_index("item") % 2
    kept, part, columns = keep.shape
    rows = columns // (2 * levels)
    for k in range(kept):
        total = (keep[k] + got[k].astype(F32)).astype(BF16)
        for p in range(2):
            for r in range(levels):
                at, column = (k * levels + r) * part, (p * levels + r) * rows
                turned[p, at:at + part, :] = total[:, column:column + rows]
    terms = jnp.dot(turned[core], mine[...], preferred_element_type=F32)
    terms = terms + jnp.dot(turned[1 - core], theirs[...], preferred_element_type=F32)
    users, _, few, lanes = out.shape
    groups = part // few
    for u in range(users):
        for block in range(kept * levels):
            first = block * part + (u % groups) * few
            column = (u // groups) * lanes
            out[u, block] = terms[first:first + few, column:column + lanes]


def user_pieces(items, rows, *outs):
    user = lax.axis_index("user")
    chips, tile, width = items.shape
    users, blocks, part, lanes = rows.shape
    few = tile // users
    for k, out in enumerate(outs):
        first = pl.multiple_of((user ^ k) * few, few)
        at = 0
        for column in range(0, width, lanes):
            for z in range(chips):
                out[at:at + few] = items[z, pl.ds(first, few), column:column + lanes].astype(out.dtype)
                at += few
        for block in range(blocks):
            out[at:at + part] = rows[user ^ k, block].astype(out.dtype)
            at += part
        if at < out.shape[0]:
            out[at:] = jnp.zeros((out.shape[0] - at, lanes), out.dtype)


def chip_pieces(chips, few, blocks, rows, *refs):
    count = len(refs) - chips - 1
    parts, outs, total = refs[:count], refs[count:-1], refs[-1]
    chip = lax.axis_index("item") // 2
    summed = parts[0][...]
    for part in parts[1:]:
        summed = summed + part[...].astype(F32)
    for block in range(blocks):
        for z in range(chips):
            at = (block * chips + z) * few
            total[z, block * few:(block + 1) * few] = summed[at:at + few]
    first = blocks * chips * few
    weight = summed[first:first + rows].astype(BF16)
    for k, out in enumerate(outs):
        out[:blocks * few] = total[chip ^ k].astype(out.dtype)
        out[blocks * few:blocks * few + rows] = weight.astype(out.dtype)
        if blocks * few + rows < out.shape[0]:
            out[blocks * few + rows:] = jnp.zeros((out.shape[0] - blocks * few - rows, out.shape[1]), out.dtype)


def user_rows(items, rows, *refs):
    own, *parts, out = refs
    parts = [own, *parts[::-1]]
    total = parts[0][:items]
    for part in parts[1:]:
        total = total + part[:items].astype(F32)
    out[:items] = total.astype(BF16)
    for k in range(len(parts)):
        terms = []
        for j in range(k % 2, len(parts), 2):
            at = items + ((j ^ k) // 2) * rows
            terms.append(parts[j][at:at + rows].astype(BF16).astype(F32))
        out[items + k * rows:items + (k + 1) * rows] = tree_sum(terms).astype(BF16)
    if items + len(parts) * rows < out.shape[0]:
        out[items + len(parts) * rows:] = jnp.zeros((out.shape[0] - items - len(parts) * rows, out.shape[1]), BF16)


def item_rows(few, *refs):
    *parts, out = refs
    user = lax.axis_index("user")
    lanes = parts[0].shape[1]
    for k, part in enumerate(parts):
        row = pl.multiple_of((user ^ k) * few, few)
        for block in range(out.shape[1] // lanes):
            out[pl.ds(row, few), block * lanes:(block + 1) * lanes] = part[block * few:(block + 1) * few].astype(F32)


def weight_out(chips, items, few, scale, *refs):
    *pieces, out, wide = refs
    core = lax.axis_index("item") % 2
    chip = lax.axis_index("item") // 2
    user = lax.axis_index("user")
    levels, width, _ = out.shape
    lanes = pieces[0].shape[1]
    users = len(pieces) // 2
    part = width // (2 * chips)
    groups = part // few
    for other in range(2):
        for j in range(users):
            piece = pieces[users * other + j]
            for k in range(chips):
                at = items + k * levels * few
                for r in range(levels):
                    block = piece[at + r * few:at + (r + 1) * few].astype(F32) * scale
                    if groups == 1 and few % 8 == 0:
                        row = (core ^ other) * (width // 2) + (chip ^ k) * part
                        column = (user ^ j) * lanes
                        out[r, pl.ds(pl.multiple_of(row, few), few),
                            pl.ds(pl.multiple_of(column, lanes), lanes)] = block
                    else:
                        wide[core ^ other, chip ^ k, user ^ j, r] = block
    if not (groups == 1 and few % 8 == 0):
        for c in range(2):
            for z in range(chips):
                for u in range(users):
                    row = c * (width // 2) + z * part + (u % groups) * few
                    column = (u // groups) * lanes
                    for r in range(levels):
                        out[r, row:row + few, column:column + lanes] = wide[c, z, u, r]


def per_device(item_features, level_weights, tile_values, tile_order, tile_counts, cotangent):
    item_size = lax.axis_size("item")
    user_size = lax.axis_size("user")
    chips = item_size // 2
    levels, width, hidden_width = level_weights.shape
    tile = tile_values.shape[-1]
    capacity = tile_values.shape[2]
    local_items = item_features.shape[0]
    items = local_items * item_size
    block_count = items // tile
    user_blocks = tile_order.shape[1] // (levels * block_count)
    group_rows = user_blocks * tile
    share = group_rows // item_size
    smem = pl.BlockSpec(memory_space=pltpu.SMEM)

    strips = tile // (2 * share)
    tiles = tile_values.reshape(1, capacity, strips, 2, share, tile)
    other_tiles = swap(tiles, "item", 1)
    far = [swap(item_features, "item", 2 * k) for k in range(chips - 1, 0, -1)][::-1]
    rows = levels * chips * share
    dense = call(
        functools.partial(place_tiles, block_count),
        struct((2, rows, items), BF16),
        (tile_order, tile_counts, tiles, other_tiles),
        scratch=[pltpu.SemaphoreType.DMA((2 * capacity * strips,))],
        specs=[smem, smem, pl.BlockSpec(memory_space=pl.ANY), pl.BlockSpec(memory_space=pl.ANY)],
        cost=cost(4),
    )
    *far, dense = lax.optimization_barrier((*far, dense))
    feature_pieces = []
    for piece in [item_features, *far]:
        feature_pieces += [piece, swap(piece, "item", 1)]

    features, pre_own, *pre_sends = call(
        functools.partial(forward, chips),
        (struct((items, width), BF16), struct((share, hidden_width), F32))
        + (struct((share, hidden_width), BF16),) * (chips - 1),
        (dense, level_weights, *feature_pieces),
        scratch=[pltpu.VMEM((chips, share, hidden_width), F32)],
        cost=cost(1.5),
    )
    pre_parts = [swap(pre_sends[k - 1], "item", 2 * k) for k in range(1, chips)]

    part = width // item_size
    kept = chips // 2
    turned_own, turned_send = call(
        functools.partial(turn, levels),
        (struct((kept, part, 2 * rows), F32), struct((kept, part, 2 * rows), BF16)),
        (dense, features),
        scratch=[pltpu.VMEM((chips, part, 2 * rows), F32)],
        cost=cost(3),
    )
    turned_got = swap(turned_send, "item", 2)

    pre, slope = call(
        slopes_of,
        (struct((share, hidden_width), F32), struct((share, hidden_width), BF16)),
        (pre_own, *pre_parts[::-1], cotangent),
        cost=cost(0.1),
    )
    far = [swap(slope, "item", 2 * k) for k in range(chips - 1, 0, -1)][::-1]
    hidden = call(activate, struct((share, hidden_width), BF16), (pre,), cost=cost(0.7))
    mine = [slope, *far]
    theirs = [swap(piece, "item", 1) for piece in mine]
    *theirs, turned_got = lax.optimization_barrier((*theirs, turned_got))

    item_terms = struct((chips, tile, width), F32)
    half_slopes = struct((group_rows // 2, hidden_width), BF16)
    my_slopes, item_part = call(
        functools.partial(backward, chips, 0),
        (half_slopes, item_terms),
        (dense, level_weights, *mine),
        cost=cost(1),
    )
    their_slopes, item_part = call(
        functools.partial(backward, chips, 1),
        (half_slopes, item_terms),
        (dense, level_weights, *theirs, item_part),
        cost=cost(1),
    )

    user_few = tile // user_size
    lanes = 128
    lane_blocks = min(hidden_width // lanes, user_size)
    few = part * lane_blocks // user_size
    weight_part = call(
        functools.partial(weight_rows, levels),
        struct((user_size, kept * levels, few, lanes), F32),
        (my_slopes, their_slopes, turned_own, turned_got),
        scratch=[pltpu.VMEM((2, kept * levels * part, group_rows // 2), BF16)],
        cost=cost(0.6),
    )

    def padded(amount):
        return -(-amount // 16) * 16

    blocks = width // lanes
    amount = padded(blocks * chips * user_few + chips // 2 * levels * few)
    mine, *sends = call(
        user_pieces,
        (struct((amount, lanes), F32),) + (struct((amount, lanes), BF16),) * (user_size - 1),
        (item_part, weight_part),
        cost=cost(0.2),
    )
    parts = [swap(sends[k - 1], "user", k) for k in range(user_size - 1, 0, -1)][::-1]
    amount = padded(blocks * user_few + chips // 2 * levels * few)
    mine, *sends = call(
        functools.partial(chip_pieces, chips, user_few, blocks, chips // 2 * levels * few),
        (struct((amount, lanes), F32),) + (struct((amount, lanes), BF16),) * (chips - 1),
        (mine, *parts[::-1]),
        scratch=[pltpu.VMEM((chips, blocks * user_few, lanes), F32)],
        cost=cost(0.1),
    )
    parts = [swap(sends[k - 1], "item", 2 * k) for k in range(chips - 1, 0, -1)][::-1]
    amount = padded(blocks * user_few + chips * levels * few)
    gathered = call(
        functools.partial(user_rows, blocks * user_few, levels * few),
        struct((amount, lanes), BF16),
        (mine, *parts[::-1]),
        cost=cost(0.1),
    )
    gathered = [gathered] + [swap(gathered, "user", k) for k in range(user_size - 1, 0, -1)][::-1]
    others = [swap(piece, "item", 1) for piece in gathered]
    item_grad = call(
        functools.partial(item_rows, user_few), struct((tile, width), F32), gathered, cost=cost(0.7)
    )
    weight_grad = call(
        functools.partial(
            weight_out, chips, blocks * user_few, few, (group_rows * user_size) ** -0.5
        ),
        struct((levels, width, hidden_width), F32),
        (*gathered, *others),
        scratch=[pltpu.VMEM((2, chips, user_size, levels, few, lanes), F32)],
        cost=cost(1.3),
    )
    return hidden, item_grad, weight_grad


def solution(mesh):
    in_specs = (
        P("item", None),
        P(),
        P("user", "item", None, None, None),
        P("user", None),
        P("user", None),
        P(("user", "item"), None),
    )
    out_specs = (P(("user", "item"), None), P("item", None), P())
    return jax.shard_map(
        per_device, mesh=mesh, in_specs=in_specs, out_specs=out_specs, check_vma=False
    )
```

time: 68.8 us -> 66.3 us (0.964)
  waiting for transfers between devices: 29 us -> 24.6 us
  Pallas kernels: 8.26 us -> 9.9 us
    ppermute x34 -> x32, waiting for transfers between devices: 29 us -> 24.6 us  [swap(): return lax.ppermute(array, axis, partners(axis, step))]
    pallas_call x13, Pallas kernels: 8.26 us -> 9.9 us  [call(): pl.pallas_call(body, out_shape=out_shapes, in_specs=specs if specs is not...]
    ppermute x34 -> x32, starting transfers between devices: 28.1 us -> 28.3 us  [swap(): return lax.ppermute(array, axis, partners(axis, step))]
  transfers between devices with their start and end apart: 34 -> 32, of which waited for: 22 -> 14; matrix products, arithmetic and copies ran while one was open for 0% -> 0% of each run, Pallas kernels for 4% -> 9%
where the time goes in v3:
time: 66.3 us; the launch traced here: 66 us
  starting transfers between devices  28.3 us (43%)
  waiting for transfers between devices  24.6 us (37%)
  Pallas kernels  9.9 us (15%)
  local copies, waits for them, and re-layouts  2.45 us (4%)
  between operations  0.8 us (1%)
    ppermute x32, starting transfers between devices, swap(): return lax.ppermute(array, axis, partners(axis, step))  28.3 us
    ppermute x32, waiting for transfers between devices, swap(): return lax.ppermute(array, axis, partners(axis, step))  24.6 us
    pallas_call x13, Pallas kernels, call(): pl.pallas_call(body, out_shape=out_shapes, in_specs=specs if specs is not...  9.9 us
    unnamed x12, local copies, waits for them, and re-layouts  2.45 us
  transfers between devices with their start and end apart: 32, of which 14 were waited for; matrix products, arithmetic and copies ran while one was open for 0% of the time, Pallas kernels for 9%

profile of v3, /device:TPU:0, one launch (start us, length us, event | category | flops | bytes accessed | tf_op | source)
XLA Modules:
  0.0 66.0 jit_solution(11837934314474989627)
XLA Ops:
  1.2 4.7 %collective-permute-start.2 = (bf16[128,256]{1,0:T(8,128)(2,1)}, bf16[128,256]{1,0:T(8,128)(2,1)S(1)}, u32[]{:S(2)}, u32[]{:S(2)}) collective-permute-start(bf16[128,256]{1,0:T(8,128)(2,1)} %refs_0_.1), channel_id=1, source_target_pairs={{0,6},{1,7},{2,4},{3,5},{4,2},{5,3},{6,0},{7,1},{8,14},{9,15},{10,... | collective-permute-start | bytes 196616 | tf_op jit(solution)/shard_map/ppermute | solution.py:19
  6.5 1.1 %copy-done.2 = bf16[1,1,24,128,128]{4,3,2,1,0:T(8,128)(2,1)S(1)} copy-done((bf16[1,1,24,128,128]{4,3,2,1,0:T(8,128)(2,1)S(1)}, bf16[1,1,24,128,128]{4,3,2,1,0:T(8,128)(2,1)}, u32[]{:S(2)}) %copy-start.2) | copy-done | bytes 786456
  8.9 2.3 %shard_map.85.dense = bf16[2,768,1024]{2,1,0:T(8,128)(2,1)S(1)} custom-call(s32[1,96]{1,0:T(1,128)S(1)} %copy-done.4, s32[1,8]{1,0:T(1,128)S(1)} %copy-done.5, bf16[1,24,1,2,64,128]{5,4,3,2,1,0:T(8,128)(2,1)S(1)} %bitcast.2, bf16[1,24,1,2,64,128]{5,4,3,2,1,0:T(8,128)(2,1)S(1)} %collective-permute-done.3.theirs), custom_call_target="tpu_custom_call" | custom-call | flops 4000000000 | bytes 12000000 | tf_op jit(solution)/shard_map/pallas_call | solution.py:30
  13.9 1.3 %shard_map.86 = (bf16[1024,256]{1,0:T(8,128)(2,1)S(1)}, f32[64,512]{1,0:T(8,128)S(1)}, bf16[64,512]{1,0:T(8,128)(2,1)S(1)}, bf16[64,512]{1,0:T(8,128)(2,1)S(1)}, bf16[64,512]{1,0:T(8,128)(2,1)S(1)}) custom-call(bf16[2,768,1024]{2,1,0:T(8,128)(2,1)S(1)} %shard_map.85.dense, bf16[3,256,512]{2,1,0:T(8,128)(2,1)S(1)} %copy-done, bf16[128,256]{1,0:T(8,128)(2,1)S(1)} %copy-done.3, ...), custom_call_target="tpu_custom_call" | custom-call | flops 1500000000 | bytes 4500000 | tf_op jit(solution)/shard_map/pallas_call | solution.py:30
  15.2 2.7 %collective-permute-start.8 = (bf16[64,512]{1,0:T(8,128)(2,1)S(1)}, bf16[64,512]{1,0:T(8,128)(2,1)S(1)}, u32[]{:S(2)}, u32[]{:S(2)}) collective-permute-start(bf16[64,512]{1,0:T(8,128)(2,1)S(1)} %get-tuple-element.38), channel_id=1, source_target_pairs={{0,6},{1,7},{2,4},{3,5},{4,2},{5,3},{6,0},{7,1},{8,14},{9,15},{10,... | collective-permute-start | bytes 196616 | tf_op jit(solution)/shard_map/ppermute | solution.py:19
  17.9 1.7 %collective-permute-start.10 = (bf16[64,512]{1,0:T(8,128)(2,1)S(1)}, bf16[64,512]{1,0:T(8,128)(2,1)S(1)}, u32[]{:S(2)}, u32[]{:S(2)}) collective-permute-start(bf16[64,512]{1,0:T(8,128)(2,1)S(1)} %get-tuple-element.40), channel_id=1, source_target_pairs={{0,2},{1,3},{2,0},{3,1},{4,6},{5,7},{6,4},{7,5},{8,10},{9,11},{10,... | collective-permute-start | bytes 196616 | tf_op jit(solution)/shard_map/ppermute | solution.py:19
  19.6 1.1 %shard_map.89 = (f32[2,32,1536]{2,1,0:T(8,128)S(1)}, bf16[2,32,1536]{2,1,0:T(8,128)(2,1)S(1)}) custom-call(bf16[2,768,1024]{2,1,0:T(8,128)(2,1)S(1)} %shard_map.85.dense, bf16[1024,256]{1,0:T(8,128)(2,1)S(1)} %get-tuple-element.43.features), custom_call_target="tpu_custom_call" | custom-call | flops 3000000000 | bytes 9000000 | tf_op jit(solution)/shard_map/pallas_call | solution.py:30
  22.0 2.4 %collective-permute-done.9.refs_1_ = bf16[64,512]{1,0:T(8,128)(2,1)S(1)} collective-permute-done((bf16[64,512]{1,0:T(8,128)(2,1)S(1)}, bf16[64,512]{1,0:T(8,128)(2,1)S(1)}, u32[]{:S(2)}, u32[]{:S(2)}) %collective-permute-start.9) | collective-permute-done | bytes 65568 | tf_op jit(solution)/shard_map/ppermute | solution.py:19
  24.6 2.3 %collective-permute-start.16 = (bf16[64,512]{1,0:T(8,128)(2,1)S(1)}, bf16[64,512]{1,0:T(8,128)(2,1)S(1)}, u32[]{:S(2)}, u32[]{:S(2)}) collective-permute-start(bf16[64,512]{1,0:T(8,128)(2,1)S(1)} %get-tuple-element.42.refs_0_), channel_id=1, source_target_pairs={{0,6},{1,7},{2,4},{3,5},{4,2},{5,3},{6,0},{7,1},{8,14},{9,15},{10,... | collective-permute-start | bytes 196616 | tf_op jit(solution)/shard_map/ppermute | solution.py:19
  27.3 1.8 %collective-permute-start.12 = (bf16[64,512]{1,0:T(8,128)(2,1)S(1)}, bf16[64,512]{1,0:T(8,128)(2,1)S(1)}, u32[]{:S(2)}, u32[]{:S(2)}) collective-permute-start(bf16[64,512]{1,0:T(8,128)(2,1)S(1)} %get-tuple-element.42.refs_0_), channel_id=1, source_target_pairs={{0,2},{1,3},{2,0},{3,1},{4,6},{5,7},{6,4},{7,5},{8,10},{9,11},{10,... | collective-permute-start | bytes 196616 | tf_op jit(solution)/shard_map/ppermute | solution.py:19
  29.0 2.1 %collective-permute-done.16.refs_3_ = bf16[64,512]{1,0:T(8,128)(2,1)S(1)} collective-permute-done((bf16[64,512]{1,0:T(8,128)(2,1)S(1)}, bf16[64,512]{1,0:T(8,128)(2,1)S(1)}, u32[]{:S(2)}, u32[]{:S(2)}) %collective-permute-start.16) | collective-permute-done | bytes 65568 | tf_op jit(solution)/shard_map/ppermute | solution.py:19
  31.2 2.5 %collective-permute-done.14.refs_2_ = bf16[64,512]{1,0:T(8,128)(2,1)S(1)} collective-permute-done((bf16[64,512]{1,0:T(8,128)(2,1)S(1)}, bf16[64,512]{1,0:T(8,128)(2,1)S(1)}, u32[]{:S(2)}, u32[]{:S(2)}) %collective-permute-start.14) | collective-permute-done | bytes 65568 | tf_op jit(solution)/shard_map/ppermute | solution.py:19
  36.6 2.8 %collective-permute-start.19 = (bf16[448,128]{1,0:T(8,128)(2,1)S(1)}, bf16[448,128]{1,0:T(8,128)(2,1)S(1)}, u32[]{:S(2)}, u32[]{:S(2)}) collective-permute-start(bf16[448,128]{1,0:T(8,128)(2,1)S(1)} %get-tuple-element.56), channel_id=1, source_target_pairs={{0,24},{8,16},{16,8},{24,0},{1,25},{9,17},{17,9},{25,1},{2,26},{10... | collective-permute-start | bytes 344072 | tf_op jit(solution)/shard_map/ppermute | solution.py:19
  40.2 2.9 %collective-permute-done.19.refs_1_ = bf16[448,128]{1,0:T(8,128)(2,1)S(1)} collective-permute-done((bf16[448,128]{1,0:T(8,128)(2,1)S(1)}, bf16[448,128]{1,0:T(8,128)(2,1)S(1)}, u32[]{:S(2)}, u32[]{:S(2)}) %collective-permute-start.19) | collective-permute-done | bytes 114720 | tf_op jit(solution)/shard_map/ppermute | solution.py:19
  43.1 2.4 %collective-permute-done.20.refs_2_ = bf16[448,128]{1,0:T(8,128)(2,1)S(1)} collective-permute-done((bf16[448,128]{1,0:T(8,128)(2,1)S(1)}, bf16[448,128]{1,0:T(8,128)(2,1)S(1)}, u32[]{:S(2)}, u32[]{:S(2)}) %collective-permute-start.20) | collective-permute-done | bytes 114720 | tf_op jit(solution)/shard_map/ppermute | solution.py:19
  45.5 1.8 %collective-permute-start.22 = (bf16[256,128]{1,0:T(8,128)(2,1)S(1)}, bf16[256,128]{1,0:T(8,128)(2,1)S(1)}, u32[]{:S(2)}, u32[]{:S(2)}) collective-permute-start(bf16[256,128]{1,0:T(8,128)(2,1)S(1)} %get-tuple-element.60), channel_id=1, source_target_pairs={{0,6},{1,7},{2,4},{3,5},{4,2},{5,3},{6,0},{7,1},{8,14},{9,15},{10,... | collective-permute-start | bytes 196616 | tf_op jit(solution)/shard_map/ppermute | solution.py:19
  47.4 2.6 %collective-permute-start.24 = (bf16[256,128]{1,0:T(8,128)(2,1)S(1)}, bf16[256,128]{1,0:T(8,128)(2,1)S(1)}, u32[]{:S(2)}, u32[]{:S(2)}) collective-permute-start(bf16[256,128]{1,0:T(8,128)(2,1)S(1)} %get-tuple-element.62), channel_id=1, source_target_pairs={{0,2},{1,3},{2,0},{3,1},{4,6},{5,7},{6,4},{7,5},{8,10},{9,11},{10,... | collective-permute-start | bytes 196616 | tf_op jit(solution)/shard_map/ppermute | solution.py:19
  50.0 2.4 %collective-permute-done.22.refs_1_ = bf16[256,128]{1,0:T(8,128)(2,1)S(1)} collective-permute-done((bf16[256,128]{1,0:T(8,128)(2,1)S(1)}, bf16[256,128]{1,0:T(8,128)(2,1)S(1)}, u32[]{:S(2)}, u32[]{:S(2)}) %collective-permute-start.22) | collective-permute-done | bytes 65568 | tf_op jit(solution)/shard_map/ppermute | solution.py:19
  52.4 1.8 %collective-permute-done.23.refs_2_ = bf16[256,128]{1,0:T(8,128)(2,1)S(1)} collective-permute-done((bf16[256,128]{1,0:T(8,128)(2,1)S(1)}, bf16[256,128]{1,0:T(8,128)(2,1)S(1)}, u32[]{:S(2)}, u32[]{:S(2)}) %collective-permute-start.23) | collective-permute-done | bytes 65568 | tf_op jit(solution)/shard_map/ppermute | solution.py:19
  54.3 1.2 %collective-permute-start.27 = (bf16[448,128]{1,0:T(8,128)(2,1)S(1)}, bf16[448,128]{1,0:T(8,128)(2,1)S(1)}, u32[]{:S(2)}, u32[]{:S(2)}) collective-permute-start(bf16[448,128]{1,0:T(8,128)(2,1)S(1)} %shard_map.95.refs_0_), channel_id=1, source_target_pairs={{0,24},{8,16},{16,8},{24,0},{1,25},{9,17},{17,9},{25,1},{2,26},{10... | collective-permute-start | bytes 344072 | tf_op jit(solution)/shard_map/ppermute | solution.py:19
  55.5 2.0 %collective-permute-start.26 = (bf16[448,128]{1,0:T(8,128)(2,1)S(1)}, bf16[448,128]{1,0:T(8,128)(2,1)S(1)}, u32[]{:S(2)}, u32[]{:S(2)}) collective-permute-start(bf16[448,128]{1,0:T(8,128)(2,1)S(1)} %shard_map.95.refs_0_), channel_id=1, source_target_pairs={{0,16},{8,24},{16,0},{24,8},{1,17},{9,25},{17,1},{25,9},{2,18},{10... | collective-permute-start | bytes 344072 | tf_op jit(solution)/shard_map/ppermute | solution.py:19
  57.8 3.4 %collective-permute-done.27.refs_3_ = bf16[448,128]{1,0:T(8,128)(2,1)S(1)} collective-permute-done((bf16[448,128]{1,0:T(8,128)(2,1)S(1)}, bf16[448,128]{1,0:T(8,128)(2,1)S(1)}, u32[]{:S(2)}, u32[]{:S(2)}) %collective-permute-start.27) | collective-permute-done | bytes 114720 | tf_op jit(solution)/shard_map/ppermute | solution.py:19
  61.2 1.5 %collective-permute-done.26.refs_2_ = bf16[448,128]{1,0:T(8,128)(2,1)S(1)} collective-permute-done((bf16[448,128]{1,0:T(8,128)(2,1)S(1)}, bf16[448,128]{1,0:T(8,128)(2,1)S(1)}, u32[]{:S(2)}, u32[]{:S(2)}) %collective-permute-start.26) | collective-permute-done | bytes 114720 | tf_op jit(solution)/shard_map/ppermute | solution.py:19
  64.6 1.4 %shard_map.97 = f32[3,256,512]{2,1,0:T(8,128)} custom-call(bf16[448,128]{1,0:T(8,128)(2,1)S(1)} %shard_map.95.refs_0_, bf16[448,128]{1,0:T(8,128)(2,1)S(1)} %collective-permute-done.25.refs_1_, bf16[448,128]{1,0:T(8,128)(2,1)S(1)} %collective-permute-done.26.refs_2_, bf16[448,128]{1,0:T(8,128)(2,1)S(1)} %collective-permute-done.27.refs_3_, ...), custom_call_target="tpu_custom_call" | custom-call | flops 1300000000 | bytes 3900000 | tf_op jit(solution)/shard_map/pallas_call | solution.py:30
  (65 shorter events, 12.8 us)
Async XLA Ops:
  0.6 5.9 %collective-permute-start.3 = (bf16[1,24,1,2,64,128]{5,4,3,2,1,0:T(8,128)(2,1)}, bf16[1,24,1,2,64,128]{5,4,3,2,1,0:T(8,128)(2,1)S(1)}, u32[]{:S(2)}, u32[]{:S(2)}) collective-permute-start(bf16[1,24,1,2,64,128]{5,4,3,2,1,0:T(8,128)(2,1)} %bitcast.1), channel_id=1, source_target_pairs={{0,1},{1,0},{2,3},{3,2},{4,5},{5,4},{6,7},{7,6},{8,9},{9,8},{10,11... | collective-permute-start | bytes 2359304 | tf_op jit(solution)/shard_map/ppermute | solution.py:19
  1.2 10.1 %collective-permute-start.2 = (bf16[128,256]{1,0:T(8,128)(2,1)}, bf16[128,256]{1,0:T(8,128)(2,1)S(1)}, u32[]{:S(2)}, u32[]{:S(2)}) collective-permute-start(bf16[128,256]{1,0:T(8,128)(2,1)} %refs_0_.1), channel_id=1, source_target_pairs={{0,6},{1,7},{2,4},{3,5},{4,2},{5,3},{6,0},{7,1},{8,14},{9,15},{10,... | collective-permute-start | bytes 196616 | tf_op jit(solution)/shard_map/ppermute | solution.py:19
  5.8 6.3 %collective-permute-start.1 = (bf16[128,256]{1,0:T(8,128)(2,1)}, bf16[128,256]{1,0:T(8,128)(2,1)S(1)}, u32[]{:S(2)}, u32[]{:S(2)}) collective-permute-start(bf16[128,256]{1,0:T(8,128)(2,1)} %refs_0_.1), channel_id=1, source_target_pairs={{0,4},{1,5},{2,6},{3,7},{4,0},{5,1},{6,2},{7,3},{8,12},{9,13},{10,... | collective-permute-start | bytes 196616 | tf_op jit(solution)/shard_map/ppermute | solution.py:19
  5.8 6.3 %collective-permute-start = (bf16[128,256]{1,0:T(8,128)(2,1)}, bf16[128,256]{1,0:T(8,128)(2,1)S(1)}, u32[]{:S(2)}, u32[]{:S(2)}) collective-permute-start(bf16[128,256]{1,0:T(8,128)(2,1)} %refs_0_.1), channel_id=1, source_target_pairs={{0,2},{1,3},{2,0},{3,1},{4,6},{5,7},{6,4},{7,5},{8,10},{9,11},{10,... | collective-permute-start | bytes 196616 | tf_op jit(solution)/shard_map/ppermute | solution.py:19
  6.5 6.1 %collective-permute-start.4 = (bf16[128,256]{1,0:T(8,128)(2,1)}, bf16[128,256]{1,0:T(8,128)(2,1)S(1)}, u32[]{:S(2)}, u32[]{:S(2)}) collective-permute-start(bf16[128,256]{1,0:T(8,128)(2,1)} %refs_0_.1), channel_id=1, source_target_pairs={{0,1},{1,0},{2,3},{3,2},{4,5},{5,4},{6,7},{7,6},{8,9},{9,8},{10,11... | collective-permute-start | bytes 196616 | tf_op jit(solution)/shard_map/ppermute | solution.py:19
  15.2 6.9 %collective-permute-start.8 = (bf16[64,512]{1,0:T(8,128)(2,1)S(1)}, bf16[64,512]{1,0:T(8,128)(2,1)S(1)}, u32[]{:S(2)}, u32[]{:S(2)}) collective-permute-start(bf16[64,512]{1,0:T(8,128)(2,1)S(1)} %get-tuple-element.38), channel_id=1, source_target_pairs={{0,6},{1,7},{2,4},{3,5},{4,2},{5,3},{6,0},{7,1},{8,14},{9,15},{10,... | collective-permute-start | bytes 196616 | tf_op jit(solution)/shard_map/ppermute | solution.py:19
  17.9 6.6 %collective-permute-start.9 = (bf16[64,512]{1,0:T(8,128)(2,1)S(1)}, bf16[64,512]{1,0:T(8,128)(2,1)S(1)}, u32[]{:S(2)}, u32[]{:S(2)}) collective-permute-start(bf16[64,512]{1,0:T(8,128)(2,1)S(1)} %get-tuple-element.39), channel_id=1, source_target_pairs={{0,4},{1,5},{2,6},{3,7},{4,0},{5,1},{6,2},{7,3},{8,12},{9,13},{10,... | collective-permute-start | bytes 196616 | tf_op jit(solution)/shard_map/ppermute | solution.py:19
  17.9 6.6 %collective-permute-start.10 = (bf16[64,512]{1,0:T(8,128)(2,1)S(1)}, bf16[64,512]{1,0:T(8,128)(2,1)S(1)}, u32[]{:S(2)}, u32[]{:S(2)}) collective-permute-start(bf16[64,512]{1,0:T(8,128)(2,1)S(1)} %get-tuple-element.40), channel_id=1, source_target_pairs={{0,2},{1,3},{2,0},{3,1},{4,6},{5,7},{6,4},{7,5},{8,10},{9,11},{10,... | collective-permute-start | bytes 196616 | tf_op jit(solution)/shard_map/ppermute | solution.py:19
  20.8 14.5 %collective-permute-start.18 = (bf16[2,32,1536]{2,1,0:T(8,128)(2,1)S(1)}, bf16[2,32,1536]{2,1,0:T(8,128)(2,1)S(1)}, u32[]{:S(2)}, u32[]{:S(2)}) collective-permute-start(bf16[2,32,1536]{2,1,0:T(8,128)(2,1)S(1)} %get-tuple-element.44), channel_id=1, source_target_pairs={{0,2},{1,3},{2,0},{3,1},{4,6},{5,7},{6,4},{7,5},{8,10},{9,11},{10,... | collective-permute-start | bytes 589832 | tf_op jit(solution)/shard_map/ppermute | solution.py:19
  24.6 6.6 %collective-permute-start.16 = (bf16[64,512]{1,0:T(8,128)(2,1)S(1)}, bf16[64,512]{1,0:T(8,128)(2,1)S(1)}, u32[]{:S(2)}, u32[]{:S(2)}) collective-permute-start(bf16[64,512]{1,0:T(8,128)(2,1)S(1)} %get-tuple-element.42.refs_0_), channel_id=1, source_target_pairs={{0,6},{1,7},{2,4},{3,5},{4,2},{5,3},{6,0},{7,1},{8,14},{9,15},{10,... | collective-permute-start | bytes 196616 | tf_op jit(solution)/shard_map/ppermute | solution.py:19
  26.9 6.8 %collective-permute-start.14 = (bf16[64,512]{1,0:T(8,128)(2,1)S(1)}, bf16[64,512]{1,0:T(8,128)(2,1)S(1)}, u32[]{:S(2)}, u32[]{:S(2)}) collective-permute-start(bf16[64,512]{1,0:T(8,128)(2,1)S(1)} %get-tuple-element.42.refs_0_), channel_id=1, source_target_pairs={{0,4},{1,5},{2,6},{3,7},{4,0},{5,1},{6,2},{7,3},{8,12},{9,13},{10,... | collective-permute-start | bytes 196616 | tf_op jit(solution)/shard_map/ppermute | solution.py:19
  27.3 6.5 %collective-permute-start.12 = (bf16[64,512]{1,0:T(8,128)(2,1)S(1)}, bf16[64,512]{1,0:T(8,128)(2,1)S(1)}, u32[]{:S(2)}, u32[]{:S(2)}) collective-permute-start(bf16[64,512]{1,0:T(8,128)(2,1)S(1)} %get-tuple-element.42.refs_0_), channel_id=1, source_target_pairs={{0,2},{1,3},{2,0},{3,1},{4,6},{5,7},{6,4},{7,5},{8,10},{9,11},{10,... | collective-permute-start | bytes 196616 | tf_op jit(solution)/shard_map/ppermute | solution.py:19
  29.0 6.2 %collective-permute-start.11 = (bf16[64,512]{1,0:T(8,128)(2,1)S(1)}, bf16[64,512]{1,0:T(8,128)(2,1)S(1)}, u32[]{:S(2)}, u32[]{:S(2)}) collective-permute-start(bf16[64,512]{1,0:T(8,128)(2,1)S(1)} %get-tuple-element.42.refs_0_), channel_id=1, source_target_pairs={{0,1},{1,0},{2,3},{3,2},{4,5},{5,4},{6,7},{7,6},{8,9},{9,8},{10,11... | collective-permute-start | bytes 196616 | tf_op jit(solution)/shard_map/ppermute | solution.py:19
  31.2 4.1 %collective-permute-start.17 = (bf16[64,512]{1,0:T(8,128)(2,1)S(1)}, bf16[64,512]{1,0:T(8,128)(2,1)S(1)}, u32[]{:S(2)}, u32[]{:S(2)}) collective-permute-start(bf16[64,512]{1,0:T(8,128)(2,1)S(1)} %collective-permute-done.16.refs_3_), channel_id=1, source_target_pairs={{0,1},{1,0},{2,3},{3,2},{4,5},{5,4},{6,7},{7,6},{8,9},{9,8},{10,11... | collective-permute-start | bytes 196616 | tf_op jit(solution)/shard_map/ppermute | solution.py:19
  36.6 6.5 %collective-permute-start.19 = (bf16[448,128]{1,0:T(8,128)(2,1)S(1)}, bf16[448,128]{1,0:T(8,128)(2,1)S(1)}, u32[]{:S(2)}, u32[]{:S(2)}) collective-permute-start(bf16[448,128]{1,0:T(8,128)(2,1)S(1)} %get-tuple-element.56), channel_id=1, source_target_pairs={{0,24},{8,16},{16,8},{24,0},{1,25},{9,17},{17,9},{25,1},{2,26},{10... | collective-permute-start | bytes 344072 | tf_op jit(solution)/shard_map/ppermute | solution.py:19
  39.4 6.0 %collective-permute-start.20 = (bf16[448,128]{1,0:T(8,128)(2,1)S(1)}, bf16[448,128]{1,0:T(8,128)(2,1)S(1)}, u32[]{:S(2)}, u32[]{:S(2)}) collective-permute-start(bf16[448,128]{1,0:T(8,128)(2,1)S(1)} %get-tuple-element.57), channel_id=1, source_target_pairs={{0,16},{8,24},{16,0},{24,8},{1,17},{9,25},{17,1},{25,9},{2,18},{10... | collective-permute-start | bytes 344072 | tf_op jit(solution)/shard_map/ppermute | solution.py:19
  40.0 5.4 %collective-permute-start.21 = (bf16[448,128]{1,0:T(8,128)(2,1)S(1)}, bf16[448,128]{1,0:T(8,128)(2,1)S(1)}, u32[]{:S(2)}, u32[]{:S(2)}) collective-permute-start(bf16[448,128]{1,0:T(8,128)(2,1)S(1)} %get-tuple-element.58), channel_id=1, source_target_pairs={{0,8},{8,0},{16,24},{24,16},{1,9},{9,1},{17,25},{25,17},{2,10},{10... | collective-permute-start | bytes 344072 | tf_op jit(solution)/shard_map/ppermute | solution.py:19
  45.5 6.9 %collective-permute-start.22 = (bf16[256,128]{1,0:T(8,128)(2,1)S(1)}, bf16[256,128]{1,0:T(8,128)(2,1)S(1)}, u32[]{:S(2)}, u32[]{:S(2)}) collective-permute-start(bf16[256,128]{1,0:T(8,128)(2,1)S(1)} %get-tuple-element.60), channel_id=1, source_target_pairs={{0,6},{1,7},{2,4},{3,5},{4,2},{5,3},{6,0},{7,1},{8,14},{9,15},{10,... | collective-permute-start | bytes 196616 | tf_op jit(solution)/shard_map/ppermute | solution.py:19
  47.3 6.9 %collective-permute-start.23 = (bf16[256,128]{1,0:T(8,128)(2,1)S(1)}, bf16[256,128]{1,0:T(8,128)(2,1)S(1)}, u32[]{:S(2)}, u32[]{:S(2)}) collective-permute-start(bf16[256,128]{1,0:T(8,128)(2,1)S(1)} %get-tuple-element.61), channel_id=1, source_target_pairs={{0,4},{1,5},{2,6},{3,7},{4,0},{5,1},{6,2},{7,3},{8,12},{9,13},{10,... | collective-permute-start | bytes 196616 | tf_op jit(solution)/shard_map/ppermute | solution.py:19
  47.4 6.9 %collective-permute-start.24 = (bf16[256,128]{1,0:T(8,128)(2,1)S(1)}, bf16[256,128]{1,0:T(8,128)(2,1)S(1)}, u32[]{:S(2)}, u32[]{:S(2)}) collective-permute-start(bf16[256,128]{1,0:T(8,128)(2,1)S(1)} %get-tuple-element.62), channel_id=1, source_target_pairs={{0,2},{1,3},{2,0},{3,1},{4,6},{5,7},{6,4},{7,5},{8,10},{9,11},{10,... | collective-permute-start | bytes 196616 | tf_op jit(solution)/shard_map/ppermute | solution.py:19
  54.3 7.0 %collective-permute-start.27 = (bf16[448,128]{1,0:T(8,128)(2,1)S(1)}, bf16[448,128]{1,0:T(8,128)(2,1)S(1)}, u32[]{:S(2)}, u32[]{:S(2)}) collective-permute-start(bf16[448,128]{1,0:T(8,128)(2,1)S(1)} %shard_map.95.refs_0_), channel_id=1, source_target_pairs={{0,24},{8,16},{16,8},{24,0},{1,25},{9,17},{17,9},{25,1},{2,26},{10... | collective-permute-start | bytes 344072 | tf_op jit(solution)/shard_map/ppermute | solution.py:19
  55.5 7.3 %collective-permute-start.26 = (bf16[448,128]{1,0:T(8,128)(2,1)S(1)}, bf16[448,128]{1,0:T(8,128)(2,1)S(1)}, u32[]{:S(2)}, u32[]{:S(2)}) collective-permute-start(bf16[448,128]{1,0:T(8,128)(2,1)S(1)} %shard_map.95.refs_0_), channel_id=1, source_target_pairs={{0,16},{8,24},{16,0},{24,8},{1,17},{9,25},{17,1},{25,9},{2,18},{10... | collective-permute-start | bytes 344072 | tf_op jit(solution)/shard_map/ppermute | solution.py:19
  57.5 5.2 %collective-permute-start.25 = (bf16[448,128]{1,0:T(8,128)(2,1)S(1)}, bf16[448,128]{1,0:T(8,128)(2,1)S(1)}, u32[]{:S(2)}, u32[]{:S(2)}) collective-permute-start(bf16[448,128]{1,0:T(8,128)(2,1)S(1)} %shard_map.95.refs_0_), channel_id=1, source_target_pairs={{0,8},{8,0},{16,24},{24,16},{1,9},{9,1},{17,25},{25,17},{2,10},{10... | collective-permute-start | bytes 344072 | tf_op jit(solution)/shard_map/ppermute | solution.py:19
  57.8 6.8 %collective-permute-start.28 = (bf16[448,128]{1,0:T(8,128)(2,1)S(1)}, bf16[448,128]{1,0:T(8,128)(2,1)S(1)}, u32[]{:S(2)}, u32[]{:S(2)}) collective-permute-start(bf16[448,128]{1,0:T(8,128)(2,1)S(1)} %shard_map.95.refs_0_), channel_id=1, source_target_pairs={{0,1},{1,0},{2,3},{3,2},{4,5},{5,4},{6,7},{7,6},{8,9},{9,8},{10,11... | collective-permute-start | bytes 344072 | tf_op jit(solution)/shard_map/ppermute | solution.py:19
  (14 other events, 39.6 us)

commit v4 on v3

v4 whole, which is shorter than its diff:
```python
import functools
import jax
import jax.numpy as jnp
from jax import lax
from jax.experimental import pallas as pl
from jax.experimental.pallas import tpu as pltpu
from jax.sharding import PartitionSpec as P

BF16 = jnp.bfloat16
F32 = jnp.float32
VMEM_LIMIT = 24 * 1024 * 1024
LANES = 128


def swap(array, axis, step):
    return lax.ppermute(array, axis, [(i, i ^ step) for i in range(lax.axis_size(axis))])


def swap_each(arrays, axis, unit):
    return [swap(array, axis, (k + 1) * unit) for k, array in enumerate(arrays)]


def by_reach(parts):
    return [parts[k - 1] for k in reach(len(parts))]


def reach(count):
    return sorted(range(1, count + 1), reverse=True)


def together(parts, *others):
    ks = reach(len(parts))[::-1]
    out = lax.optimization_barrier((*[parts[k - 1] for k in ks], *others))
    made = dict(zip(ks, out))
    return [made[k] for k in sorted(made)], *out[len(ks):]


def tree_sum(parts):
    while len(parts) > 1:
        parts = [parts[i] + parts[i + 1] for i in range(0, len(parts), 2)]
    return parts[0]


def cost(microseconds):
    return pl.CostEstimate(
        flops=int(microseconds * 1e9), bytes_accessed=int(microseconds * 3e6), transcendentals=0
    )


def struct(shape, dtype):
    return jax.ShapeDtypeStruct(shape, dtype)


def space(memory_space):
    return pl.BlockSpec(memory_space=memory_space)


def call(body, outs, args, time, scratch=(), specs=None, out_specs=None, aliases=None):
    vmem = space(pltpu.VMEM)
    return pl.pallas_call(
        body,
        out_shape=outs,
        in_specs=specs or [vmem] * len(args),
        out_specs=out_specs or jax.tree.map(lambda _: vmem, outs),
        scratch_shapes=list(scratch),
        compiler_params=pltpu.CompilerParams(vmem_limit_bytes=VMEM_LIMIT),
        cost_estimate=cost(time),
        input_output_aliases=aliases or {},
    )(*args)


def here():
    item = lax.axis_index("item")
    return item // 2, item % 2


def place_tiles(block_count, order, counts, mine, theirs, dense, order_s, counts_s, sems):
    tile = mine.shape[-1]
    capacity, strips, _, share = mine.shape[1:5]
    chips = counts.shape[1] // 2
    user_blocks = chips // strips
    scalars = [
        pltpu.make_async_copy(order, order_s, sems.at[2 * capacity * strips]),
        pltpu.make_async_copy(counts, counts_s, sems.at[2 * capacity * strips + 1]),
    ]
    for scalar in scalars:
        scalar.start()
    dense[...] = jnp.zeros_like(dense)
    for scalar in scalars:
        scalar.wait()
    copies = []
    for other, tiles in enumerate((mine, theirs)):
        cell = lax.axis_index("item") ^ other
        before = jnp.int32(0)
        for c in range(counts.shape[1]):
            before = before + jnp.where(c < cell, counts_s[0, c], 0)
        holding = counts_s[0, cell]
        for t in range(capacity):
            copies.append((other * capacity + t, tiles, t, before, holding))

    def copy(number, tiles, t, before, strip):
        slot = order_s[0, jnp.minimum(before + t, order.shape[1] - 1)]
        target, block = slot // block_count, slot % block_count
        level, user_block = target // user_blocks, target % user_blocks
        row = (level * chips + user_block * strips + strip) * share
        column = ((block % 2) * chips + block // 2) * tile
        return pltpu.make_async_copy(
            tiles.at[0, t, strip],
            dense.at[:, pl.ds(pl.multiple_of(row, share), share),
                     pl.ds(pl.multiple_of(column, tile), tile)],
            sems.at[number * strips + strip],
        )

    for number, tiles, t, before, holding in copies:
        @pl.when(t < holding)
        def _():
            for strip in range(strips):
                copy(number, tiles, t, before, strip).start()
    for number, tiles, t, before, holding in copies:
        @pl.when(t < holding)
        def _():
            for strip in range(strips):
                copy(number, tiles, t, before, strip).wait()


def forward(chips, dense, weights, *refs):
    pieces = refs[: 2 * chips]
    features, own, *sends, pre = refs[2 * chips:]
    chip, core = here()
    levels, _, hidden = weights.shape
    tile = pieces[0].shape[0]
    for k in range(chips):
        for other in range(2):
            row = ((core ^ other) * chips + (chip ^ k)) * tile
            features[pl.ds(pl.multiple_of(row, tile), tile), :] = pieces[2 * k + other][...]
    rows = dense.shape[1] // levels
    total = jnp.zeros((rows, hidden), F32)
    for r in range(levels):
        block = jnp.dot(
            dense[core, r * rows:(r + 1) * rows, :], features[...], preferred_element_type=F32
        )
        total = total + jnp.dot(block.astype(BF16), weights[r], preferred_element_type=F32)
    pre[...] = total.reshape(pre.shape)
    own[...] = pre[chip]
    for k in range(1, chips):
        sends[k - 1][...] = pre[chip ^ k].astype(BF16)


def turn(levels, dense, features, own, send, turned):
    chip, core = here()
    chips, part, _ = turned.shape
    half = chips * part
    rows = dense.shape[1] // levels
    columns = features[:, pl.ds(pl.multiple_of(core * half, half), half)]
    for p in range(2):
        for r in range(levels):
            block = jnp.dot(
                dense[p, r * rows:(r + 1) * rows, :], columns, preferred_element_type=F32
            )
            at = (p * levels + r) * rows
            turned[:, :, at:at + rows] = block.T.reshape(chips, part, rows)
    for k in range(0, chips, 2):
        own[k // 2] = turned[chip ^ k]
        send[k // 2] = turned[chip ^ (k + 1)].astype(BF16)


def slopes_of(own, *refs):
    *parts, cotangent, pre_out, slope = refs
    pre = own[...]
    for part in parts:
        pre = pre + part[...].astype(F32)
    sigmoid = 1.0 / (1.0 + jnp.exp(-pre))
    pre_out[...] = pre
    slope[...] = (cotangent[...].astype(F32) * (sigmoid * (1.0 + pre * (1.0 - sigmoid)))).astype(BF16)


def activate(pre, hidden):
    hidden[...] = (pre[...] / (1.0 + jnp.exp(-pre[...]))).astype(BF16)


def item_terms(chips, other, dense, weights, pieces, slopes):
    chip, core = here()
    levels, width, _ = weights.shape
    share = pieces[0].shape[0]
    for k in range(chips):
        slopes[pl.ds(pl.multiple_of((chip ^ k) * share, share), share), :] = pieces[k][...]
    rows = chips * share
    half = dense.shape[2] // 2
    columns = pl.ds(pl.multiple_of(core * half, half), half)
    total = jnp.zeros((half, width), F32)
    for r in range(levels):
        back = lax.dot_general(
            slopes[...], weights[r], (((1,), (1,)), ((), ())), preferred_element_type=F32
        ).astype(BF16)
        total = total + lax.dot_general(
            dense[core ^ other, r * rows:(r + 1) * rows, columns], back,
            (((0,), (0,)), ((), ())), preferred_element_type=F32,
        )
    return total


def backward_mine(chips, dense, weights, *refs):
    *pieces, out, slopes = refs
    out[...] = item_terms(chips, 0, dense, weights, pieces, slopes).reshape(out.shape)


def backward_theirs(chips, few, dense, weights, *refs):
    mine, theirs = refs[:chips], refs[chips:2 * chips]
    before, keep, got, *outs, their_slopes, items, turned, slopes, chunks = refs[2 * chips:]
    chip, core = here()
    user = lax.axis_index("user")
    levels = weights.shape[0]
    terms = item_terms(chips, 1, dense, weights, theirs, their_slopes)
    items[...] = before[...] + terms.reshape(items.shape)

    share = mine[0].shape[0]
    kept, part, columns = keep.shape
    rows = columns // (2 * levels)
    for k in range(chips):
        for other, pieces in enumerate((mine, theirs)):
            row = ((core ^ other) * chips + (chip ^ k)) * share
            slopes[pl.ds(pl.multiple_of(row, share), share), :] = pieces[k][...]
    for k in range(kept):
        total = (keep[k] + got[k].astype(F32)).astype(BF16)
        for p in range(2):
            for r in range(levels):
                at, column = (k * levels + r) * part, (p * levels + r) * rows
                turned[at:at + part, p * rows:(p + 1) * rows] = total[:, column:column + rows]
    terms = jnp.dot(turned[...], slopes[...], preferred_element_type=F32)
    users = chunks.shape[0]
    groups = part // few
    for u in range(users):
        for block in range(kept * levels):
            first = block * part + (u % groups) * few
            column = (u // groups) * LANES
            chunks[u, block * few:(block + 1) * few] = terms[first:first + few, column:column + LANES]

    _, tile, width = items.shape
    item_few = tile // users
    for k, out in enumerate(outs):
        first = pl.multiple_of((user ^ k) * item_few, item_few)
        blocks = [
            items[z, pl.ds(first, item_few), column:column + LANES]
            for column in range(0, width, LANES)
            for z in range(chips)
        ]
        fill(out, *blocks, chunks[user ^ k])


def fill(out, *blocks):
    at = 0
    for block in blocks:
        out[at:at + block.shape[0]] = block.astype(out.dtype)
        at += block.shape[0]
    if at < out.shape[0]:
        out[at:] = jnp.zeros((out.shape[0] - at,) + out.shape[1:], out.dtype)


def user_sum(chips, few, blocks, rows, *refs):
    count = len(refs) - chips - 1
    parts, outs, total = refs[:count], refs[count:-1], refs[-1]
    chip, _ = here()
    summed = parts[0][...]
    for part in parts[1:]:
        summed = summed + part[...].astype(F32)
    for block in range(blocks):
        for z in range(chips):
            at = (block * chips + z) * few
            total[z, block * few:(block + 1) * few] = summed[at:at + few]
    first = blocks * chips * few
    weight = summed[first:first + rows].astype(BF16)
    for k, out in enumerate(outs):
        fill(out, total[chip ^ k], weight)


def line_sum(items, rows, stride, own, *refs):
    *parts, out = refs
    made = dict(zip(reach(len(parts)), parts))
    parts = [own] + [made[k] for k in sorted(made)]
    total = own[:items]
    for part in parts[1:]:
        total = total + part[:items].astype(F32)
    blocks = [total]
    for k in range(len(parts)):
        terms = []
        for j in range(k % stride, len(parts), stride):
            at = items + ((j ^ k) // stride) * rows
            terms.append(parts[j][at:at + rows].astype(BF16).astype(F32))
        blocks.append(tree_sum(terms))
    fill(out, *blocks)


def weight_out(chips, items, few, other, scale, *refs):
    *pieces, out, wide, loose, item_rows, sems = refs
    if other:
        pieces = pieces[:-1]
    else:
        *pieces, item_grad = pieces
    chip, core = here()
    user = lax.axis_index("user")
    levels, half, _ = wide.shape
    users = len(pieces)
    part = half // chips
    groups = part // few
    copies = []
    if not other:
        item_few = item_rows.shape[0] // users
        for j in range(users):
            row = pl.multiple_of((user ^ j) * item_few, item_few)
            for block in range(items // item_few):
                item_rows[pl.ds(row, item_few), block * LANES:(block + 1) * LANES] = (
                    pieces[j][block * item_few:(block + 1) * item_few].astype(F32)
                )
        copies.append(pltpu.make_async_copy(item_rows, item_grad, sems.at[levels]))
        copies[-1].start()
    for r in range(levels):
        for j in range(users):
            for k in range(chips):
                at = items + (k * levels + r) * few
                block = pieces[j][at:at + few].astype(F32) * scale
                if groups == 1:
                    row = pl.multiple_of((chip ^ k) * part, part)
                    column = pl.multiple_of((user ^ j) * LANES, LANES)
                    wide[r, pl.ds(row, part), pl.ds(column, LANES)] = block
                else:
                    loose[chip ^ k, user ^ j] = block
        if groups > 1:
            for z in range(chips):
                for u in range(users):
                    row, column = z * part + (u % groups) * few, (u // groups) * LANES
                    wide[r, row:row + few, column:column + LANES] = loose[z, u]
        first = pl.multiple_of((core ^ other) * half, half)
        copies.append(pltpu.make_async_copy(wide.at[r], out.at[r, pl.ds(first, half), :], sems.at[r]))
        copies[-1].start()
    for copy in copies:
        copy.wait()


def per_device(item_features, level_weights, tile_values, tile_order, tile_counts, cotangent):
    item_size = lax.axis_size("item")
    user_size = lax.axis_size("user")
    chips = item_size // 2
    levels, width, hidden_width = level_weights.shape
    tile = tile_values.shape[-1]
    capacity = tile_values.shape[2]
    items = item_features.shape[0] * item_size
    block_count = items // tile
    user_blocks = tile_order.shape[1] // (levels * block_count)
    group_rows = user_blocks * tile
    share = group_rows // item_size
    rows = levels * chips * share
    vmem, anywhere = space(pltpu.VMEM), space(pl.ANY)

    strips = tile // (2 * share)
    tiles = tile_values.reshape(1, capacity, strips, 2, share, tile)
    other_tiles = swap(tiles, "item", 1)
    far = swap_each([item_features] * (chips - 1), "item", 2)
    dense = call(
        functools.partial(place_tiles, block_count),
        struct((2, rows, items), BF16),
        (tile_order, tile_counts, tiles, other_tiles),
        4,
        scratch=[
            pltpu.SMEM(tile_order.shape, jnp.int32),
            pltpu.SMEM(tile_counts.shape, jnp.int32),
            pltpu.SemaphoreType.DMA((2 * capacity * strips + 2,)),
        ],
        specs=[space(pltpu.HBM)] * 3 + [anywhere],
    )
    far, dense = together(far, dense)
    feature_pieces = []
    for piece in [item_features, *far]:
        feature_pieces += [piece, swap(piece, "item", 1)]

    piece = struct((share, hidden_width), BF16)
    features, pre_own, *pre_sends = call(
        functools.partial(forward, chips),
        (struct((items, width), BF16), struct((share, hidden_width), F32)) + (piece,) * (chips - 1),
        (dense, level_weights, *feature_pieces),
        1.5,
        scratch=[pltpu.VMEM((chips, share, hidden_width), F32)],
    )
    pre_parts = swap_each(pre_sends, "item", 2)

    part = width // item_size
    kept = chips // 2
    turned_own, turned_send = call(
        functools.partial(turn, levels),
        (struct((kept, part, 2 * rows), F32), struct((kept, part, 2 * rows), BF16)),
        (dense, features),
        3,
        scratch=[pltpu.VMEM((chips, part, 2 * rows), F32)],
    )
    turned_got = swap(turned_send, "item", 2)

    pre, slope = call(
        slopes_of,
        (struct((share, hidden_width), F32), piece),
        (pre_own, *by_reach(pre_parts), cotangent),
        0.1,
    )
    far = swap_each([slope] * (chips - 1), "item", 2)
    hidden = call(activate, piece, (pre,), 0.7)
    mine = [slope, *far]
    theirs = [swap(piece, "item", 1) for piece in mine]
    *theirs, turned_got = lax.optimization_barrier((*theirs, turned_got))

    item_part = call(
        functools.partial(backward_mine, chips),
        struct((chips, tile, width), F32),
        (dense, level_weights, *mine),
        1,
        scratch=[pltpu.VMEM((chips * share, hidden_width), BF16)],
    )

    def padded(amount):
        return -(-amount // 16) * 16

    few = part * min(hidden_width // LANES, user_size) // user_size
    item_few = tile // user_size
    blocks = width // LANES
    count = kept * levels * few
    amount = padded(blocks * chips * item_few + count)
    own, *sends = call(
        functools.partial(backward_theirs, chips, few),
        (struct((amount, LANES), F32),) + (struct((amount, LANES), BF16),) * (user_size - 1),
        (dense, level_weights, *mine, *theirs, item_part, turned_own, turned_got),
        1.3,
        scratch=[
            pltpu.VMEM((chips * share, hidden_width), BF16),
            pltpu.VMEM((chips, tile, width), F32),
            pltpu.VMEM((kept * levels * part, group_rows), BF16),
            pltpu.VMEM((group_rows, hidden_width), BF16),
            pltpu.VMEM((user_size, count, LANES), F32),
        ],
    )
    parts = swap_each(sends, "user", 1)
    parts, hidden = together(parts, hidden)
    amount = padded(blocks * item_few + count)
    own, *sends = call(
        functools.partial(user_sum, chips, item_few, blocks, count),
        (struct((amount, LANES), F32),) + (struct((amount, LANES), BF16),) * (chips - 1),
        (own, *parts[::-1]),
        0.1,
        scratch=[pltpu.VMEM((chips, blocks * item_few, LANES), F32)],
    )
    parts = swap_each(sends, "item", 2)
    amount = padded(blocks * item_few + chips * levels * few)
    gathered = call(
        functools.partial(line_sum, blocks * item_few, levels * few, chips // kept),
        struct((amount, LANES), BF16),
        (own, *by_reach(parts)),
        0.1,
    )
    gathered = [gathered] + swap_each([gathered] * (user_size - 1), "user", 1)
    others = [swap(piece, "item", 1) for piece in gathered]
    weight_grad = struct((levels, width, hidden_width), F32)
    scratch = [
        pltpu.VMEM((levels, width // 2, hidden_width), F32),
        pltpu.VMEM((chips, user_size, few, LANES), F32),
        pltpu.VMEM((tile, width), F32),
        pltpu.SemaphoreType.DMA((levels + 1,)),
    ]
    scale = (group_rows * user_size) ** -0.5
    item_grad, half_grad = call(
        functools.partial(weight_out, chips, blocks * item_few, few, 0, scale),
        (struct((tile, width), F32), weight_grad),
        gathered,
        0.9,
        scratch=scratch,
        out_specs=(anywhere, anywhere),
    )
    weight_grad = call(
        functools.partial(weight_out, chips, blocks * item_few, few, 1, scale),
        weight_grad,
        (*others, half_grad),
        0.9,
        scratch=scratch,
        specs=[vmem] * user_size + [anywhere],
        out_specs=anywhere,
        aliases={user_size: 0},
    )
    return hidden, item_grad, weight_grad


def solution(mesh):
    in_specs = (
        P("item", None),
        P(),
        P("user", "item", None, None, None),
        P("user", None),
        P("user", None),
        P(("user", "item"), None),
    )
    out_specs = (P(("user", "item"), None), P("item", None), P())
    return jax.shard_map(
        per_device, mesh=mesh, in_specs=in_specs, out_specs=out_specs, check_vma=False
    )
```

time: 66.3 us -> 63.5 us (0.958)
  waiting for transfers between devices: 24.6 us -> 22.9 us
  Pallas kernels: 9.9 us -> 9.04 us
    ppermute x32, waiting for transfers between devices: 24.6 us -> 22.9 us  [swap(): lax.ppermute(array, axis, [(i, i ^ step) for i in range(lax.axis_size(axi...]
    pallas_call x13 -> x11, Pallas kernels: 9.9 us -> 9.04 us  [call(): pl.pallas_call(body, out_shape=outs, in_specs=specs or [vmem] * len(args)...]
  transfers between devices with their start and end apart: 32 -> 32, of which waited for: 14 -> 15; matrix products, arithmetic and copies ran while one was open for 0% -> 0% of each run, Pallas kernels for 9% -> 9%
where the time goes in v4:
time: 63.5 us; the launch traced here: 63.4 us
  starting transfers between devices  28.2 us (44%)
  waiting for transfers between devices  22.9 us (36%)
  Pallas kernels  9.04 us (14%)
  local copies, waits for them, and re-layouts  2.45 us (4%)
  between operations  0.82 us (1%)
    ppermute x32, starting transfers between devices, swap(): lax.ppermute(array, axis, [(i, i ^ step) for i in range(lax.axis_size(axi...  28.2 us
    ppermute x32, waiting for transfers between devices, swap(): lax.ppermute(array, axis, [(i, i ^ step) for i in range(lax.axis_size(axi...  22.9 us
    pallas_call x11, Pallas kernels, call(): pl.pallas_call(body, out_shape=outs, in_specs=specs or [vmem] * len(args)...  9.04 us
    unnamed x12, local copies, waits for them, and re-layouts  2.45 us
  transfers between devices with their start and end apart: 32, of which 15 were waited for; matrix products, arithmetic and copies ran while one was open for 0% of the time, Pallas kernels for 9%

profile of v4, /device:TPU:0, one launch (start us, length us, event | category | flops | bytes accessed | tf_op | source)
XLA Modules:
  0.0 63.4 jit_solution(2388097863018963340)
XLA Ops:
  1.2 4.7 %collective-permute-start.2 = (bf16[128,256]{1,0:T(8,128)(2,1)}, bf16[128,256]{1,0:T(8,128)(2,1)S(1)}, u32[]{:S(2)}, u32[]{:S(2)}) collective-permute-start(bf16[128,256]{1,0:T(8,128)(2,1)} %refs_0_.1), channel_id=1, source_target_pairs={{0,6},{1,7},{2,4},{3,5},{4,2},{5,3},{6,0},{7,1},{8,14},{9,15},{10,... | collective-permute-start | bytes 196616 | tf_op jit(solution)/shard_map/ppermute | solution.py:16
  6.5 1.1 %copy-done.2 = bf16[1,1,24,128,128]{4,3,2,1,0:T(8,128)(2,1)S(1)} copy-done((bf16[1,1,24,128,128]{4,3,2,1,0:T(8,128)(2,1)S(1)}, bf16[1,1,24,128,128]{4,3,2,1,0:T(8,128)(2,1)}, u32[]{:S(2)}) %copy-start.2) | copy-done | bytes 786456
  8.9 2.0 %shard_map.85.dense = bf16[2,768,1024]{2,1,0:T(8,128)(2,1)S(1)} custom-call(s32[1,96]{1,0:T(1,128)S(1)} %copy-done.4, s32[1,8]{1,0:T(1,128)S(1)} %copy-done.5, bf16[1,24,1,2,64,128]{5,4,3,2,1,0:T(8,128)(2,1)S(1)} %bitcast.2, bf16[1,24,1,2,64,128]{5,4,3,2,1,0:T(8,128)(2,1)S(1)} %collective-permute-done.3.theirs), custom_call_target="tpu_custom_call" | custom-call | flops 4000000000 | bytes 12000000 | tf_op jit(solution)/shard_map/pallas_call | solution.py:60
  10.9 1.2 %collective-permute-done.1.refs_4_ = bf16[128,256]{1,0:T(8,128)(2,1)S(1)} collective-permute-done((bf16[128,256]{1,0:T(8,128)(2,1)}, bf16[128,256]{1,0:T(8,128)(2,1)S(1)}, u32[]{:S(2)}, u32[]{:S(2)}) %collective-permute-start.1) | collective-permute-done | bytes 65568 | tf_op jit(solution)/shard_map/ppermute | solution.py:16
  13.9 1.3 %shard_map.86 = (bf16[1024,256]{1,0:T(8,128)(2,1)S(1)}, f32[64,512]{1,0:T(8,128)S(1)}, bf16[64,512]{1,0:T(8,128)(2,1)S(1)}, bf16[64,512]{1,0:T(8,128)(2,1)S(1)}, bf16[64,512]{1,0:T(8,128)(2,1)S(1)}) custom-call(bf16[2,768,1024]{2,1,0:T(8,128)(2,1)S(1)} %shard_map.85.dense, bf16[3,256,512]{2,1,0:T(8,128)(2,1)S(1)} %copy-done, bf16[128,256]{1,0:T(8,128)(2,1)S(1)} %copy-done.3, ...), custom_call_target="tpu_custom_call" | custom-call | flops 1500000000 | bytes 4500000 | tf_op jit(solution)/shard_map/pallas_call | solution.py:60
  15.2 2.7 %collective-permute-start.8 = (bf16[64,512]{1,0:T(8,128)(2,1)S(1)}, bf16[64,512]{1,0:T(8,128)(2,1)S(1)}, u32[]{:S(2)}, u32[]{:S(2)}) collective-permute-start(bf16[64,512]{1,0:T(8,128)(2,1)S(1)} %get-tuple-element.40), channel_id=1, source_target_pairs={{0,6},{1,7},{2,4},{3,5},{4,2},{5,3},{6,0},{7,1},{8,14},{9,15},{10,... | collective-permute-start | bytes 196616 | tf_op jit(solution)/shard_map/ppermute | solution.py:16
  17.9 1.7 %collective-permute-start.10 = (bf16[64,512]{1,0:T(8,128)(2,1)S(1)}, bf16[64,512]{1,0:T(8,128)(2,1)S(1)}, u32[]{:S(2)}, u32[]{:S(2)}) collective-permute-start(bf16[64,512]{1,0:T(8,128)(2,1)S(1)} %get-tuple-element.42), channel_id=1, source_target_pairs={{0,2},{1,3},{2,0},{3,1},{4,6},{5,7},{6,4},{7,5},{8,10},{9,11},{10,... | collective-permute-start | bytes 196616 | tf_op jit(solution)/shard_map/ppermute | solution.py:16
  19.6 1.1 %shard_map.88 = (f32[2,32,1536]{2,1,0:T(8,128)S(1)}, bf16[2,32,1536]{2,1,0:T(8,128)(2,1)S(1)}) custom-call(bf16[2,768,1024]{2,1,0:T(8,128)(2,1)S(1)} %shard_map.85.dense, bf16[1024,256]{1,0:T(8,128)(2,1)S(1)} %get-tuple-element.44.features), custom_call_target="tpu_custom_call" | custom-call | flops 3000000000 | bytes 9000000 | tf_op jit(solution)/shard_map/pallas_call | solution.py:60
  22.0 2.5 %collective-permute-done.9.refs_1_ = bf16[64,512]{1,0:T(8,128)(2,1)S(1)} collective-permute-done((bf16[64,512]{1,0:T(8,128)(2,1)S(1)}, bf16[64,512]{1,0:T(8,128)(2,1)S(1)}, u32[]{:S(2)}, u32[]{:S(2)}) %collective-permute-start.9) | collective-permute-done | bytes 65568 | tf_op jit(solution)/shard_map/ppermute | solution.py:16
  24.6 2.3 %collective-permute-start.13 = (bf16[64,512]{1,0:T(8,128)(2,1)S(1)}, bf16[64,512]{1,0:T(8,128)(2,1)S(1)}, u32[]{:S(2)}, u32[]{:S(2)}) collective-permute-start(bf16[64,512]{1,0:T(8,128)(2,1)S(1)} %get-tuple-element.43.refs_0_), channel_id=1, source_target_pairs={{0,6},{1,7},{2,4},{3,5},{4,2},{5,3},{6,0},{7,1},{8,14},{9,15},{10,... | collective-permute-start | bytes 196616 | tf_op jit(solution)/shard_map/ppermute | solution.py:16
  27.2 1.8 %collective-permute-start.11 = (bf16[64,512]{1,0:T(8,128)(2,1)S(1)}, bf16[64,512]{1,0:T(8,128)(2,1)S(1)}, u32[]{:S(2)}, u32[]{:S(2)}) collective-permute-start(bf16[64,512]{1,0:T(8,128)(2,1)S(1)} %get-tuple-element.43.refs_0_), channel_id=1, source_target_pairs={{0,2},{1,3},{2,0},{3,1},{4,6},{5,7},{6,4},{7,5},{8,10},{9,11},{10,... | collective-permute-start | bytes 196616 | tf_op jit(solution)/shard_map/ppermute | solution.py:16
  29.0 2.1 %collective-permute-done.13.refs_3_ = bf16[64,512]{1,0:T(8,128)(2,1)S(1)} collective-permute-done((bf16[64,512]{1,0:T(8,128)(2,1)S(1)}, bf16[64,512]{1,0:T(8,128)(2,1)S(1)}, u32[]{:S(2)}, u32[]{:S(2)}) %collective-permute-start.13) | collective-permute-done | bytes 65568 | tf_op jit(solution)/shard_map/ppermute | solution.py:16
  31.1 2.6 %collective-permute-done.12.refs_2_ = bf16[64,512]{1,0:T(8,128)(2,1)S(1)} collective-permute-done((bf16[64,512]{1,0:T(8,128)(2,1)S(1)}, bf16[64,512]{1,0:T(8,128)(2,1)S(1)}, u32[]{:S(2)}, u32[]{:S(2)}) %collective-permute-start.12) | collective-permute-done | bytes 65568 | tf_op jit(solution)/shard_map/ppermute | solution.py:16
  36.1 1.8 %collective-permute-start.19 = (bf16[448,128]{1,0:T(8,128)(2,1)S(1)}, bf16[448,128]{1,0:T(8,128)(2,1)S(1)}, u32[]{:S(2)}, u32[]{:S(2)}) collective-permute-start(bf16[448,128]{1,0:T(8,128)(2,1)S(1)} %get-tuple-element.52), channel_id=1, source_target_pairs={{0,8},{8,0},{16,24},{24,16},{1,9},{9,1},{17,25},{25,17},{2,10},{10... | collective-permute-start | bytes 344072 | tf_op jit(solution)/shard_map/ppermute | solution.py:16
  37.9 1.4 %collective-permute-start.20 = (bf16[448,128]{1,0:T(8,128)(2,1)S(1)}, bf16[448,128]{1,0:T(8,128)(2,1)S(1)}, u32[]{:S(2)}, u32[]{:S(2)}) collective-permute-start(bf16[448,128]{1,0:T(8,128)(2,1)S(1)} %get-tuple-element.53), channel_id=1, source_target_pairs={{0,16},{8,24},{16,0},{24,8},{1,17},{9,25},{17,1},{25,9},{2,18},{10... | collective-permute-start | bytes 344072 | tf_op jit(solution)/shard_map/ppermute | solution.py:16
  40.3 1.1 %collective-permute-done.19.refs_3_ = bf16[448,128]{1,0:T(8,128)(2,1)S(1)} collective-permute-done((bf16[448,128]{1,0:T(8,128)(2,1)S(1)}, bf16[448,128]{1,0:T(8,128)(2,1)S(1)}, u32[]{:S(2)}, u32[]{:S(2)}) %collective-permute-start.19) | collective-permute-done | bytes 114720 | tf_op jit(solution)/shard_map/ppermute | solution.py:16
  41.4 3.9 %collective-permute-done.20.refs_2_ = bf16[448,128]{1,0:T(8,128)(2,1)S(1)} collective-permute-done((bf16[448,128]{1,0:T(8,128)(2,1)S(1)}, bf16[448,128]{1,0:T(8,128)(2,1)S(1)}, u32[]{:S(2)}, u32[]{:S(2)}) %collective-permute-start.20) | collective-permute-done | bytes 114720 | tf_op jit(solution)/shard_map/ppermute | solution.py:16
  45.4 1.7 %collective-permute-start.22 = (bf16[256,128]{1,0:T(8,128)(2,1)S(1)}, bf16[256,128]{1,0:T(8,128)(2,1)S(1)}, u32[]{:S(2)}, u32[]{:S(2)}) collective-permute-start(bf16[256,128]{1,0:T(8,128)(2,1)S(1)} %get-tuple-element.62), channel_id=1, source_target_pairs={{0,6},{1,7},{2,4},{3,5},{4,2},{5,3},{6,0},{7,1},{8,14},{9,15},{10,... | collective-permute-start | bytes 196616 | tf_op jit(solution)/shard_map/ppermute | solution.py:16
  47.2 2.7 %collective-permute-start.24 = (bf16[256,128]{1,0:T(8,128)(2,1)S(1)}, bf16[256,128]{1,0:T(8,128)(2,1)S(1)}, u32[]{:S(2)}, u32[]{:S(2)}) collective-permute-start(bf16[256,128]{1,0:T(8,128)(2,1)S(1)} %get-tuple-element.64), channel_id=1, source_target_pairs={{0,2},{1,3},{2,0},{3,1},{4,6},{5,7},{6,4},{7,5},{8,10},{9,11},{10,... | collective-permute-start | bytes 196616 | tf_op jit(solution)/shard_map/ppermute | solution.py:16
  49.9 2.3 %collective-permute-done.22.refs_0_ = bf16[256,128]{1,0:T(8,128)(2,1)S(1)} collective-permute-done((bf16[256,128]{1,0:T(8,128)(2,1)S(1)}, bf16[256,128]{1,0:T(8,128)(2,1)S(1)}, u32[]{:S(2)}, u32[]{:S(2)}) %collective-permute-start.22) | collective-permute-done | bytes 65568 | tf_op jit(solution)/shard_map/ppermute | solution.py:16
  52.2 1.3 %collective-permute-done.23.refs_1_ = bf16[256,128]{1,0:T(8,128)(2,1)S(1)} collective-permute-done((bf16[256,128]{1,0:T(8,128)(2,1)S(1)}, bf16[256,128]{1,0:T(8,128)(2,1)S(1)}, u32[]{:S(2)}, u32[]{:S(2)}) %collective-permute-start.23) | collective-permute-done | bytes 65568 | tf_op jit(solution)/shard_map/ppermute | solution.py:16
  53.5 1.6 %collective-permute-start.27 = (bf16[448,128]{1,0:T(8,128)(2,1)S(1)}, bf16[448,128]{1,0:T(8,128)(2,1)S(1)}, u32[]{:S(2)}, u32[]{:S(2)}) collective-permute-start(bf16[448,128]{1,0:T(8,128)(2,1)S(1)} %shard_map.93.refs_0_), channel_id=1, source_target_pairs={{0,24},{8,16},{16,8},{24,0},{1,25},{9,17},{17,9},{25,1},{2,26},{10... | collective-permute-start | bytes 344072 | tf_op jit(solution)/shard_map/ppermute | solution.py:16
  55.1 1.1 %collective-permute-start.26 = (bf16[448,128]{1,0:T(8,128)(2,1)S(1)}, bf16[448,128]{1,0:T(8,128)(2,1)S(1)}, u32[]{:S(2)}, u32[]{:S(2)}) collective-permute-start(bf16[448,128]{1,0:T(8,128)(2,1)S(1)} %shard_map.93.refs_0_), channel_id=1, source_target_pairs={{0,16},{8,24},{16,0},{24,8},{1,17},{9,25},{17,1},{25,9},{2,18},{10... | collective-permute-start | bytes 344072 | tf_op jit(solution)/shard_map/ppermute | solution.py:16
  57.1 3.3 %collective-permute-done.27.refs_3_ = bf16[448,128]{1,0:T(8,128)(2,1)S(1)} collective-permute-done((bf16[448,128]{1,0:T(8,128)(2,1)S(1)}, bf16[448,128]{1,0:T(8,128)(2,1)S(1)}, u32[]{:S(2)}, u32[]{:S(2)}) %collective-permute-start.27) | collective-permute-done | bytes 114720 | tf_op jit(solution)/shard_map/ppermute | solution.py:16
  (63 shorter events, 13.5 us)
Async XLA Ops:
  0.6 5.9 %collective-permute-start.3 = (bf16[1,24,1,2,64,128]{5,4,3,2,1,0:T(8,128)(2,1)}, bf16[1,24,1,2,64,128]{5,4,3,2,1,0:T(8,128)(2,1)S(1)}, u32[]{:S(2)}, u32[]{:S(2)}) collective-permute-start(bf16[1,24,1,2,64,128]{5,4,3,2,1,0:T(8,128)(2,1)} %bitcast.1), channel_id=1, source_target_pairs={{0,1},{1,0},{2,3},{3,2},{4,5},{5,4},{6,7},{7,6},{8,9},{9,8},{10,11... | collective-permute-start | bytes 2359304 | tf_op jit(solution)/shard_map/ppermute | solution.py:16
  1.2 9.8 %collective-permute-start.2 = (bf16[128,256]{1,0:T(8,128)(2,1)}, bf16[128,256]{1,0:T(8,128)(2,1)S(1)}, u32[]{:S(2)}, u32[]{:S(2)}) collective-permute-start(bf16[128,256]{1,0:T(8,128)(2,1)} %refs_0_.1), channel_id=1, source_target_pairs={{0,6},{1,7},{2,4},{3,5},{4,2},{5,3},{6,0},{7,1},{8,14},{9,15},{10,... | collective-permute-start | bytes 196616 | tf_op jit(solution)/shard_map/ppermute | solution.py:16
  5.8 6.3 %collective-permute-start.1 = (bf16[128,256]{1,0:T(8,128)(2,1)}, bf16[128,256]{1,0:T(8,128)(2,1)S(1)}, u32[]{:S(2)}, u32[]{:S(2)}) collective-permute-start(bf16[128,256]{1,0:T(8,128)(2,1)} %refs_0_.1), channel_id=1, source_target_pairs={{0,4},{1,5},{2,6},{3,7},{4,0},{5,1},{6,2},{7,3},{8,12},{9,13},{10,... | collective-permute-start | bytes 196616 | tf_op jit(solution)/shard_map/ppermute | solution.py:16
  5.8 6.3 %collective-permute-start = (bf16[128,256]{1,0:T(8,128)(2,1)}, bf16[128,256]{1,0:T(8,128)(2,1)S(1)}, u32[]{:S(2)}, u32[]{:S(2)}) collective-permute-start(bf16[128,256]{1,0:T(8,128)(2,1)} %refs_0_.1), channel_id=1, source_target_pairs={{0,2},{1,3},{2,0},{3,1},{4,6},{5,7},{6,4},{7,5},{8,10},{9,11},{10,... | collective-permute-start | bytes 196616 | tf_op jit(solution)/shard_map/ppermute | solution.py:16
  6.5 6.1 %collective-permute-start.4 = (bf16[128,256]{1,0:T(8,128)(2,1)}, bf16[128,256]{1,0:T(8,128)(2,1)S(1)}, u32[]{:S(2)}, u32[]{:S(2)}) collective-permute-start(bf16[128,256]{1,0:T(8,128)(2,1)} %refs_0_.1), channel_id=1, source_target_pairs={{0,1},{1,0},{2,3},{3,2},{4,5},{5,4},{6,7},{7,6},{8,9},{9,8},{10,11... | collective-permute-start | bytes 196616 | tf_op jit(solution)/shard_map/ppermute | solution.py:16
  15.2 6.8 %collective-permute-start.8 = (bf16[64,512]{1,0:T(8,128)(2,1)S(1)}, bf16[64,512]{1,0:T(8,128)(2,1)S(1)}, u32[]{:S(2)}, u32[]{:S(2)}) collective-permute-start(bf16[64,512]{1,0:T(8,128)(2,1)S(1)} %get-tuple-element.40), channel_id=1, source_target_pairs={{0,6},{1,7},{2,4},{3,5},{4,2},{5,3},{6,0},{7,1},{8,14},{9,15},{10,... | collective-permute-start | bytes 196616 | tf_op jit(solution)/shard_map/ppermute | solution.py:16
  17.8 6.7 %collective-permute-start.9 = (bf16[64,512]{1,0:T(8,128)(2,1)S(1)}, bf16[64,512]{1,0:T(8,128)(2,1)S(1)}, u32[]{:S(2)}, u32[]{:S(2)}) collective-permute-start(bf16[64,512]{1,0:T(8,128)(2,1)S(1)} %get-tuple-element.41), channel_id=1, source_target_pairs={{0,4},{1,5},{2,6},{3,7},{4,0},{5,1},{6,2},{7,3},{8,12},{9,13},{10,... | collective-permute-start | bytes 196616 | tf_op jit(solution)/shard_map/ppermute | solution.py:16
  17.9 6.6 %collective-permute-start.10 = (bf16[64,512]{1,0:T(8,128)(2,1)S(1)}, bf16[64,512]{1,0:T(8,128)(2,1)S(1)}, u32[]{:S(2)}, u32[]{:S(2)}) collective-permute-start(bf16[64,512]{1,0:T(8,128)(2,1)S(1)} %get-tuple-element.42), channel_id=1, source_target_pairs={{0,2},{1,3},{2,0},{3,1},{4,6},{5,7},{6,4},{7,5},{8,10},{9,11},{10,... | collective-permute-start | bytes 196616 | tf_op jit(solution)/shard_map/ppermute | solution.py:16
  20.7 14.4 %collective-permute-start.18 = (bf16[2,32,1536]{2,1,0:T(8,128)(2,1)S(1)}, bf16[2,32,1536]{2,1,0:T(8,128)(2,1)S(1)}, u32[]{:S(2)}, u32[]{:S(2)}) collective-permute-start(bf16[2,32,1536]{2,1,0:T(8,128)(2,1)S(1)} %get-tuple-element.45), channel_id=1, source_target_pairs={{0,2},{1,3},{2,0},{3,1},{4,6},{5,7},{6,4},{7,5},{8,10},{9,11},{10,... | collective-permute-start | bytes 589832 | tf_op jit(solution)/shard_map/ppermute | solution.py:16
  24.6 6.5 %collective-permute-start.13 = (bf16[64,512]{1,0:T(8,128)(2,1)S(1)}, bf16[64,512]{1,0:T(8,128)(2,1)S(1)}, u32[]{:S(2)}, u32[]{:S(2)}) collective-permute-start(bf16[64,512]{1,0:T(8,128)(2,1)S(1)} %get-tuple-element.43.refs_0_), channel_id=1, source_target_pairs={{0,6},{1,7},{2,4},{3,5},{4,2},{5,3},{6,0},{7,1},{8,14},{9,15},{10,... | collective-permute-start | bytes 196616 | tf_op jit(solution)/shard_map/ppermute | solution.py:16
  26.9 6.8 %collective-permute-start.12 = (bf16[64,512]{1,0:T(8,128)(2,1)S(1)}, bf16[64,512]{1,0:T(8,128)(2,1)S(1)}, u32[]{:S(2)}, u32[]{:S(2)}) collective-permute-start(bf16[64,512]{1,0:T(8,128)(2,1)S(1)} %get-tuple-element.43.refs_0_), channel_id=1, source_target_pairs={{0,4},{1,5},{2,6},{3,7},{4,0},{5,1},{6,2},{7,3},{8,12},{9,13},{10,... | collective-permute-start | bytes 196616 | tf_op jit(solution)/shard_map/ppermute | solution.py:16
  27.2 6.5 %collective-permute-start.11 = (bf16[64,512]{1,0:T(8,128)(2,1)S(1)}, bf16[64,512]{1,0:T(8,128)(2,1)S(1)}, u32[]{:S(2)}, u32[]{:S(2)}) collective-permute-start(bf16[64,512]{1,0:T(8,128)(2,1)S(1)} %get-tuple-element.43.refs_0_), channel_id=1, source_target_pairs={{0,2},{1,3},{2,0},{3,1},{4,6},{5,7},{6,4},{7,5},{8,10},{9,11},{10,... | collective-permute-start | bytes 196616 | tf_op jit(solution)/shard_map/ppermute | solution.py:16
  29.0 6.1 %collective-permute-start.14 = (bf16[64,512]{1,0:T(8,128)(2,1)S(1)}, bf16[64,512]{1,0:T(8,128)(2,1)S(1)}, u32[]{:S(2)}, u32[]{:S(2)}) collective-permute-start(bf16[64,512]{1,0:T(8,128)(2,1)S(1)} %get-tuple-element.43.refs_0_), channel_id=1, source_target_pairs={{0,1},{1,0},{2,3},{3,2},{4,5},{5,4},{6,7},{7,6},{8,9},{9,8},{10,11... | collective-permute-start | bytes 196616 | tf_op jit(solution)/shard_map/ppermute | solution.py:16
  31.1 4.1 %collective-permute-start.17 = (bf16[64,512]{1,0:T(8,128)(2,1)S(1)}, bf16[64,512]{1,0:T(8,128)(2,1)S(1)}, u32[]{:S(2)}, u32[]{:S(2)}) collective-permute-start(bf16[64,512]{1,0:T(8,128)(2,1)S(1)} %collective-permute-done.13.refs_3_), channel_id=1, source_target_pairs={{0,1},{1,0},{2,3},{3,2},{4,5},{5,4},{6,7},{7,6},{8,9},{9,8},{10,11... | collective-permute-start | bytes 196616 | tf_op jit(solution)/shard_map/ppermute | solution.py:16
  36.1 5.3 %collective-permute-start.19 = (bf16[448,128]{1,0:T(8,128)(2,1)S(1)}, bf16[448,128]{1,0:T(8,128)(2,1)S(1)}, u32[]{:S(2)}, u32[]{:S(2)}) collective-permute-start(bf16[448,128]{1,0:T(8,128)(2,1)S(1)} %get-tuple-element.52), channel_id=1, source_target_pairs={{0,8},{8,0},{16,24},{24,16},{1,9},{9,1},{17,25},{25,17},{2,10},{10... | collective-permute-start | bytes 344072 | tf_op jit(solution)/shard_map/ppermute | solution.py:16
  37.9 7.5 %collective-permute-start.20 = (bf16[448,128]{1,0:T(8,128)(2,1)S(1)}, bf16[448,128]{1,0:T(8,128)(2,1)S(1)}, u32[]{:S(2)}, u32[]{:S(2)}) collective-permute-start(bf16[448,128]{1,0:T(8,128)(2,1)S(1)} %get-tuple-element.53), channel_id=1, source_target_pairs={{0,16},{8,24},{16,0},{24,8},{1,17},{9,25},{17,1},{25,9},{2,18},{10... | collective-permute-start | bytes 344072 | tf_op jit(solution)/shard_map/ppermute | solution.py:16
  39.3 6.0 %collective-permute-start.21 = (bf16[448,128]{1,0:T(8,128)(2,1)S(1)}, bf16[448,128]{1,0:T(8,128)(2,1)S(1)}, u32[]{:S(2)}, u32[]{:S(2)}) collective-permute-start(bf16[448,128]{1,0:T(8,128)(2,1)S(1)} %get-tuple-element.54), channel_id=1, source_target_pairs={{0,24},{8,16},{16,8},{24,0},{1,25},{9,17},{17,9},{25,1},{2,26},{10... | collective-permute-start | bytes 344072 | tf_op jit(solution)/shard_map/ppermute | solution.py:16
  45.4 6.8 %collective-permute-start.22 = (bf16[256,128]{1,0:T(8,128)(2,1)S(1)}, bf16[256,128]{1,0:T(8,128)(2,1)S(1)}, u32[]{:S(2)}, u32[]{:S(2)}) collective-permute-start(bf16[256,128]{1,0:T(8,128)(2,1)S(1)} %get-tuple-element.62), channel_id=1, source_target_pairs={{0,6},{1,7},{2,4},{3,5},{4,2},{5,3},{6,0},{7,1},{8,14},{9,15},{10,... | collective-permute-start | bytes 196616 | tf_op jit(solution)/shard_map/ppermute | solution.py:16
  47.2 6.3 %collective-permute-start.23 = (bf16[256,128]{1,0:T(8,128)(2,1)S(1)}, bf16[256,128]{1,0:T(8,128)(2,1)S(1)}, u32[]{:S(2)}, u32[]{:S(2)}) collective-permute-start(bf16[256,128]{1,0:T(8,128)(2,1)S(1)} %get-tuple-element.63), channel_id=1, source_target_pairs={{0,4},{1,5},{2,6},{3,7},{4,0},{5,1},{6,2},{7,3},{8,12},{9,13},{10,... | collective-permute-start | bytes 196616 | tf_op jit(solution)/shard_map/ppermute | solution.py:16
  47.2 6.3 %collective-permute-start.24 = (bf16[256,128]{1,0:T(8,128)(2,1)S(1)}, bf16[256,128]{1,0:T(8,128)(2,1)S(1)}, u32[]{:S(2)}, u32[]{:S(2)}) collective-permute-start(bf16[256,128]{1,0:T(8,128)(2,1)S(1)} %get-tuple-element.64), channel_id=1, source_target_pairs={{0,2},{1,3},{2,0},{3,1},{4,6},{5,7},{6,4},{7,5},{8,10},{9,11},{10,... | collective-permute-start | bytes 196616 | tf_op jit(solution)/shard_map/ppermute | solution.py:16
  53.5 6.8 %collective-permute-start.27 = (bf16[448,128]{1,0:T(8,128)(2,1)S(1)}, bf16[448,128]{1,0:T(8,128)(2,1)S(1)}, u32[]{:S(2)}, u32[]{:S(2)}) collective-permute-start(bf16[448,128]{1,0:T(8,128)(2,1)S(1)} %shard_map.93.refs_0_), channel_id=1, source_target_pairs={{0,24},{8,16},{16,8},{24,0},{1,25},{9,17},{17,9},{25,1},{2,26},{10... | collective-permute-start | bytes 344072 | tf_op jit(solution)/shard_map/ppermute | solution.py:16
  55.1 5.7 %collective-permute-start.26 = (bf16[448,128]{1,0:T(8,128)(2,1)S(1)}, bf16[448,128]{1,0:T(8,128)(2,1)S(1)}, u32[]{:S(2)}, u32[]{:S(2)}) collective-permute-start(bf16[448,128]{1,0:T(8,128)(2,1)S(1)} %shard_map.93.refs_0_), channel_id=1, source_target_pairs={{0,16},{8,24},{16,0},{24,8},{1,17},{9,25},{17,1},{25,9},{2,18},{10... | collective-permute-start | bytes 344072 | tf_op jit(solution)/shard_map/ppermute | solution.py:16
  56.2 4.8 %collective-permute-start.25 = (bf16[448,128]{1,0:T(8,128)(2,1)S(1)}, bf16[448,128]{1,0:T(8,128)(2,1)S(1)}, u32[]{:S(2)}, u32[]{:S(2)}) collective-permute-start(bf16[448,128]{1,0:T(8,128)(2,1)S(1)} %shard_map.93.refs_0_), channel_id=1, source_target_pairs={{0,8},{8,0},{16,24},{24,16},{1,9},{9,1},{17,25},{25,17},{2,10},{10... | collective-permute-start | bytes 344072 | tf_op jit(solution)/shard_map/ppermute | solution.py:16
  57.1 5.3 %collective-permute-start.28 = (bf16[448,128]{1,0:T(8,128)(2,1)S(1)}, bf16[448,128]{1,0:T(8,128)(2,1)S(1)}, u32[]{:S(2)}, u32[]{:S(2)}) collective-permute-start(bf16[448,128]{1,0:T(8,128)(2,1)S(1)} %shard_map.93.refs_0_), channel_id=1, source_target_pairs={{0,1},{1,0},{2,3},{3,2},{4,5},{5,4},{6,7},{7,6},{8,9},{9,8},{10,11... | collective-permute-start | bytes 344072 | tf_op jit(solution)/shard_map/ppermute | solution.py:16
  (14 other events, 37.5 us)

commit v5 on v4

--- a/solution.py
+++ b/solution.py
@@ -123,21 +123,39 @@
                 copy(number, tiles, t, before, strip).wait()
 
 
-def forward(chips, dense, weights, *refs):
-    pieces = refs[: 2 * chips]
-    features, own, *sends, pre = refs[2 * chips:]
+def stack(pieces, out):
+    chip, _ = here()
+    size = pieces[0].shape[0]
+    for k, piece in enumerate(pieces):
+        out[pl.ds(pl.multiple_of((chip ^ k) * size, size), size), :] = piece[...]
+
+
+def columns_of(dense, parity):
+    half = dense.shape[2] // 2
+    return pl.ds(pl.multiple_of(parity * half, half), half)
+
+
+def forward_mine(dense, *refs):
+    *pieces, features, terms = refs
+    _, core = here()
+    stack(pieces, features)
+    terms[...] = jnp.dot(
+        dense[core, :, columns_of(dense, core)], features[...], preferred_element_type=F32
+    )
+
+
+def forward_theirs(chips, dense, weights, *refs):
+    pieces = refs[:chips]
+    before, features, own, *sends, pre = refs[chips:]
     chip, core = here()
     levels, _, hidden = weights.shape
-    tile = pieces[0].shape[0]
-    for k in range(chips):
-        for other in range(2):
-            row = ((core ^ other) * chips + (chip ^ k)) * tile
-            features[pl.ds(pl.multiple_of(row, tile), tile), :] = pieces[2 * k + other][...]
+    stack(pieces, features)
     rows = dense.shape[1] // levels
     total = jnp.zeros((rows, hidden), F32)
     for r in range(levels):
-        block = jnp.dot(
-            dense[core, r * rows:(r + 1) * rows, :], features[...], preferred_element_type=F32
+        at = pl.ds(r * rows, rows)
+        block = before[at, :] + jnp.dot(
+            dense[core, at, columns_of(dense, 1 - core)], features[...], preferred_element_type=F32
         )
         total = total + jnp.dot(block.astype(BF16), weights[r], preferred_element_type=F32)
     pre[...] = total.reshape(pre.shape)
@@ -146,22 +164,36 @@
         sends[k - 1][...] = pre[chip ^ k].astype(BF16)
 
 
-def turn(levels, dense, features, own, send, turned):
+def turn(levels, dense, mine, theirs, own, send, turned):
     chip, core = here()
     chips, part, _ = turned.shape
     half = chips * part
     rows = dense.shape[1] // levels
-    columns = features[:, pl.ds(pl.multiple_of(core * half, half), half)]
+    width = pl.ds(pl.multiple_of(core * half, half), half)
     for p in range(2):
         for r in range(levels):
-            block = jnp.dot(
-                dense[p, r * rows:(r + 1) * rows, :], columns, preferred_element_type=F32
-            )
-            at = (p * levels + r) * rows
+            at = p * levels * rows + r * rows
+            block = jnp.zeros((rows, half), F32)
+            for parity, features in ((core, mine), (1 - core, theirs)):
+                block = block + jnp.dot(
+                    dense[p, pl.ds(r * rows, rows), columns_of(dense, parity)],
+                    features[:, width],
+                    preferred_element_type=F32,
+                )
             turned[:, :, at:at + rows] = block.T.reshape(chips, part, rows)
     for k in range(0, chips, 2):
         own[k // 2] = turned[chip ^ k]
         send[k // 2] = turned[chip ^ (k + 1)].astype(BF16)
+
+
+def flip(dense, weights, flipped, weights_t):
+    _, core = here()
+    step = dense.shape[1] // weights.shape[0]
+    for r in range(weights.shape[0]):
+        weights_t[r] = weights[r].T
+        for p in range(2):
+            at = pl.ds(r * step, step)
+            flipped[p, :, at] = dense[p, at, columns_of(dense, core)].T
 
 
 def slopes_of(own, *refs):
@@ -178,39 +210,29 @@
     hidden[...] = (pre[...] / (1.0 + jnp.exp(-pre[...]))).astype(BF16)
 
 
-def item_terms(chips, other, dense, weights, pieces, slopes):
-    chip, core = here()
-    levels, width, _ = weights.shape
-    share = pieces[0].shape[0]
-    for k in range(chips):
-        slopes[pl.ds(pl.multiple_of((chip ^ k) * share, share), share), :] = pieces[k][...]
-    rows = chips * share
-    half = dense.shape[2] // 2
-    columns = pl.ds(pl.multiple_of(core * half, half), half)
-    total = jnp.zeros((half, width), F32)
-    for r in range(levels):
-        back = lax.dot_general(
-            slopes[...], weights[r], (((1,), (1,)), ((), ())), preferred_element_type=F32
+def item_terms(other, flipped, weights_t, pieces, slopes, back):
+    _, core = here()
+    stack(pieces, slopes)
+    rows = slopes.shape[0]
+    for r in range(weights_t.shape[0]):
+        back[r * rows:(r + 1) * rows, :] = jnp.dot(
+            slopes[...], weights_t[r], preferred_element_type=F32
         ).astype(BF16)
-        total = total + lax.dot_general(
-            dense[core ^ other, r * rows:(r + 1) * rows, columns], back,
-            (((0,), (0,)), ((), ())), preferred_element_type=F32,
-        )
-    return total
-
-
-def backward_mine(chips, dense, weights, *refs):
-    *pieces, out, slopes = refs
-    out[...] = item_terms(chips, 0, dense, weights, pieces, slopes).reshape(out.shape)
-
-
-def backward_theirs(chips, few, dense, weights, *refs):
+    return jnp.dot(flipped[core ^ other], back[...], preferred_element_type=F32)
+
+
+def backward_mine(flipped, weights_t, *refs):
+    *pieces, out, slopes, back = refs
+    out[...] = item_terms(0, flipped, weights_t, pieces, slopes, back).reshape(out.shape)
+
+
+def backward_theirs(chips, few, flipped, weights_t, *refs):
     mine, theirs = refs[:chips], refs[chips:2 * chips]
-    before, keep, got, *outs, their_slopes, items, turned, slopes, chunks = refs[2 * chips:]
+    before, keep, got, *outs, their_slopes, back, items, turned, slopes, chunks = refs[2 * chips:]
     chip, core = here()
     user = lax.axis_index("user")
-    levels = weights.shape[0]
-    terms = item_terms(chips, 1, dense, weights, theirs, their_slopes)
+    levels = weights_t.shape[0]
+    terms = item_terms(1, flipped, weights_t, theirs, their_slopes, back)
     items[...] = before[...] + terms.reshape(items.shape)
 
     share = mine[0].shape[0]
@@ -290,20 +312,26 @@
     fill(out, *blocks)
 
 
-def weight_out(chips, items, few, other, scale, *refs):
-    *pieces, out, wide, loose, item_rows, sems = refs
-    if other:
-        pieces = pieces[:-1]
-    else:
-        *pieces, item_grad = pieces
+def weight_out(chips, items, few, scale, counts, *refs):
+    users, places = counts
+    pieces = refs[:users + len(places)]
+    out, wide, loose, item_rows, sems = refs[-5:]
     chip, core = here()
     user = lax.axis_index("user")
-    levels, half, _ = wide.shape
-    users = len(pieces)
+    _, levels, half, hidden = wide.shape
     part = half // chips
     groups = part // few
     copies = []
-    if not other:
+
+    def send(source, target):
+        copies.append(pltpu.make_async_copy(source, target, sems.at[len(copies)]))
+        copies[-1].start()
+
+    def rows_of(piece, k, r):
+        at = items + (k * levels + r) * few
+        return piece[at:at + few].astype(F32) * scale
+
+    if users:
         item_few = item_rows.shape[0] // users
         for j in range(users):
             row = pl.multiple_of((user ^ j) * item_few, item_few)
@@ -311,27 +339,30 @@
                 item_rows[pl.ds(row, item_few), block * LANES:(block + 1) * LANES] = (
                     pieces[j][block * item_few:(block + 1) * item_few].astype(F32)
                 )
-        copies.append(pltpu.make_async_copy(item_rows, item_grad, sems.at[levels]))
-        copies[-1].start()
-    for r in range(levels):
-        for j in range(users):
-            for k in range(chips):
-                at = items + (k * levels + r) * few
-                block = pieces[j][at:at + few].astype(F32) * scale
-                if groups == 1:
-                    row = pl.multiple_of((chip ^ k) * part, part)
-                    column = pl.multiple_of((user ^ j) * LANES, LANES)
-                    wide[r, pl.ds(row, part), pl.ds(column, LANES)] = block
-                else:
-                    loose[chip ^ k, user ^ j] = block
-        if groups > 1:
-            for z in range(chips):
-                for u in range(users):
-                    row, column = z * part + (u % groups) * few, (u // groups) * LANES
-                    wide[r, row:row + few, column:column + LANES] = loose[z, u]
+        send(item_rows, refs[-6])
+    for other, js in ((0, range(users)), (1, places)):
         first = pl.multiple_of((core ^ other) * half, half)
-        copies.append(pltpu.make_async_copy(wide.at[r], out.at[r, pl.ds(first, half), :], sems.at[r]))
-        copies[-1].start()
+        base = users if other else 0
+        for r in range(levels):
+            for at, j in enumerate(js):
+                column = pl.multiple_of((user ^ j) // groups * LANES, LANES)
+                for k in range(chips):
+                    block = rows_of(pieces[base + at], k, r)
+                    if groups == 1:
+                        row = pl.multiple_of((chip ^ k) * part, part)
+                        wide[other, r, pl.ds(row, part), pl.ds(column, LANES)] = block
+                    else:
+                        loose[chip ^ k, user ^ j] = block
+                if groups == 1 and other:
+                    send(wide.at[other, r, :, pl.ds(column, LANES)],
+                         out.at[r, pl.ds(first, half), pl.ds(column, LANES)])
+            if groups > 1 and len(js):
+                for z in range(chips):
+                    for u in range(len(js)):
+                        row, column = z * part + (u % groups) * few, (u // groups) * LANES
+                        wide[other, r, row:row + few, column:column + LANES] = loose[z, u]
+            if len(js) and (groups > 1 or not other):
+                send(wide.at[other, r], out.at[r, pl.ds(first, half), :])
     for copy in copies:
         copy.wait()
 
@@ -368,16 +399,21 @@
         specs=[space(pltpu.HBM)] * 3 + [anywhere],
     )
     far, dense = together(far, dense)
-    feature_pieces = []
-    for piece in [item_features, *far]:
-        feature_pieces += [piece, swap(piece, "item", 1)]
-
+    mine = [item_features, *far]
+    theirs = [swap(piece, "item", 1) for piece in mine]
+    half_features = struct((items // 2, width), BF16)
+    my_features, aggregate = call(
+        forward_mine,
+        (half_features, struct((rows, width), F32)),
+        (dense, *mine),
+        0.7,
+    )
     piece = struct((share, hidden_width), BF16)
-    features, pre_own, *pre_sends = call(
-        functools.partial(forward, chips),
-        (struct((items, width), BF16), struct((share, hidden_width), F32)) + (piece,) * (chips - 1),
-        (dense, level_weights, *feature_pieces),
-        1.5,
+    their_features, pre_own, *pre_sends = call(
+        functools.partial(forward_theirs, chips),
+        (half_features, struct((share, hidden_width), F32)) + (piece,) * (chips - 1),
+        (dense, level_weights, *theirs, aggregate),
+        1,
         scratch=[pltpu.VMEM((chips, share, hidden_width), F32)],
     )
     pre_parts = swap_each(pre_sends, "item", 2)
@@ -387,16 +423,25 @@
     turned_own, turned_send = call(
         functools.partial(turn, levels),
         (struct((kept, part, 2 * rows), F32), struct((kept, part, 2 * rows), BF16)),
-        (dense, features),
+        (dense, my_features, their_features),
         3,
         scratch=[pltpu.VMEM((chips, part, 2 * rows), F32)],
     )
     turned_got = swap(turned_send, "item", 2)
 
+    flipped, weights_t = call(
+        flip,
+        (struct((2, items // 2, rows), BF16), struct((levels, hidden_width, width), BF16)),
+        (dense, level_weights),
+        1.5,
+    )
+    *pre_parts, flipped, weights_t = lax.optimization_barrier(
+        (*by_reach(pre_parts), flipped, weights_t)
+    )
     pre, slope = call(
         slopes_of,
         (struct((share, hidden_width), F32), piece),
-        (pre_own, *by_reach(pre_parts), cotangent),
+        (pre_own, *pre_parts, cotangent),
         0.1,
     )
     far = swap_each([slope] * (chips - 1), "item", 2)
@@ -406,11 +451,13 @@
     *theirs, turned_got = lax.optimization_barrier((*theirs, turned_got))
 
     item_part = call(
-        functools.partial(backward_mine, chips),
+        backward_mine,
         struct((chips, tile, width), F32),
-        (dense, level_weights, *mine),
+        (flipped, weights_t, *mine),
         1,
-        scratch=[pltpu.VMEM((chips * share, hidden_width), BF16)],
+        scratch=[
+            pltpu.VMEM((chips * share, hidden_width), BF16), pltpu.VMEM((rows, width), BF16)
+        ],
     )
 
     def padded(amount):
@@ -424,10 +471,11 @@
     own, *sends = call(
         functools.partial(backward_theirs, chips, few),
         (struct((amount, LANES), F32),) + (struct((amount, LANES), BF16),) * (user_size - 1),
-        (dense, level_weights, *mine, *theirs, item_part, turned_own, turned_got),
+        (flipped, weights_t, *mine, *theirs, item_part, turned_own, turned_got),
         1.3,
         scratch=[
             pltpu.VMEM((chips * share, hidden_width), BF16),
+            pltpu.VMEM((rows, width), BF16),
             pltpu.VMEM((chips, tile, width), F32),
             pltpu.VMEM((kept * levels * part, group_rows), BF16),
             pltpu.VMEM((group_rows, hidden_width), BF16),
@@ -455,30 +503,34 @@
     gathered = [gathered] + swap_each([gathered] * (user_size - 1), "user", 1)
     others = [swap(piece, "item", 1) for piece in gathered]
     weight_grad = struct((levels, width, hidden_width), F32)
+    late = list(range(user_size))
+    soon = [late.pop(0), late.pop()] if few == part else []
     scratch = [
-        pltpu.VMEM((levels, width // 2, hidden_width), F32),
+        pltpu.VMEM((2, levels, width // 2, hidden_width), F32),
         pltpu.VMEM((chips, user_size, few, LANES), F32),
         pltpu.VMEM((tile, width), F32),
-        pltpu.SemaphoreType.DMA((levels + 1,)),
+        pltpu.SemaphoreType.DMA((levels * (user_size + 1) + 1,)),
     ]
-    scale = (group_rows * user_size) ** -0.5
+    put = functools.partial(
+        weight_out, chips, blocks * item_few, few, (group_rows * user_size) ** -0.5
+    )
     item_grad, half_grad = call(
-        functools.partial(weight_out, chips, blocks * item_few, few, 0, scale),
+        functools.partial(put, (user_size, soon)),
         (struct((tile, width), F32), weight_grad),
-        gathered,
+        (*gathered, *[others[j] for j in soon]),
         0.9,
         scratch=scratch,
         out_specs=(anywhere, anywhere),
     )
     weight_grad = call(
-        functools.partial(weight_out, chips, blocks * item_few, few, 1, scale),
+        functools.partial(put, (0, late)),
         weight_grad,
-        (*others, half_grad),
+        (*[others[j] for j in late], half_grad),
         0.9,
         scratch=scratch,
-        specs=[vmem] * user_size + [anywhere],
+        specs=[vmem] * len(late) + [anywhere],
         out_specs=anywhere,
-        aliases={user_size: 0},
+        aliases={len(late): 0},
     )
     return hidden, item_grad, weight_grad
 

time: 63.5 us -> 63.7 us (level)
    pallas_call x11 -> x13, Pallas kernels: 9.04 us -> 9.28 us  [call(): pl.pallas_call(body, out_shape=outs, in_specs=specs or [vmem] * len(args)...]
  transfers between devices with their start and end apart: 32 -> 32, of which waited for: 15 -> 16; matrix products, arithmetic and copies ran while one was open for 0% -> 0% of each run, Pallas kernels for 9% -> 10%
where the time goes in v5:
time: 63.7 us
  starting transfers between devices  28.7 us (45%)
  waiting for transfers between devices  22.4 us (35%)
  Pallas kernels  9.28 us (15%)
  local copies, waits for them, and re-layouts  2.46 us (4%)
  between operations  0.83 us (1%)
    ppermute x32, starting transfers between devices, swap(): lax.ppermute(array, axis, [(i, i ^ step) for i in range(lax.axis_size(axi...  28.7 us
    ppermute x32, waiting for transfers between devices, swap(): lax.ppermute(array, axis, [(i, i ^ step) for i in range(lax.axis_size(axi...  22.4 us
    pallas_call x13, Pallas kernels, call(): pl.pallas_call(body, out_shape=outs, in_specs=specs or [vmem] * len(args)...  9.28 us
    unnamed x12, local copies, waits for them, and re-layouts  2.46 us
  transfers between devices with their start and end apart: 32, of which 16 were waited for; matrix products, arithmetic and copies ran while one was open for 0% of the time, Pallas kernels for 10%

profile of v5, /device:TPU:0, one launch (start us, length us, event | category | flops | bytes accessed | tf_op | source)
XLA Modules:
  0.0 63.7 jit_solution(16113237480393757995)
XLA Ops:
  1.2 4.7 %collective-permute-start.2 = (bf16[128,256]{1,0:T(8,128)(2,1)}, bf16[128,256]{1,0:T(8,128)(2,1)S(1)}, u32[]{:S(2)}, u32[]{:S(2)}) collective-permute-start(bf16[128,256]{1,0:T(8,128)(2,1)} %refs_0_.1), channel_id=1, source_target_pairs={{0,6},{1,7},{2,4},{3,5},{4,2},{5,3},{6,0},{7,1},{8,14},{9,15},{10,... | collective-permute-start | bytes 196616 | tf_op jit(solution)/shard_map/ppermute | solution.py:16
  6.5 1.1 %copy-done.3 = bf16[1,1,24,128,128]{4,3,2,1,0:T(8,128)(2,1)S(1)} copy-done((bf16[1,1,24,128,128]{4,3,2,1,0:T(8,128)(2,1)S(1)}, bf16[1,1,24,128,128]{4,3,2,1,0:T(8,128)(2,1)}, u32[]{:S(2)}) %copy-start.3) | copy-done | bytes 786456
  8.9 1.6 %shard_map.85.dense = bf16[2,768,1024]{2,1,0:T(8,128)(2,1)S(1)} custom-call(s32[1,96]{1,0:T(1,128)S(1)} %copy-done.4, s32[1,8]{1,0:T(1,128)S(1)} %copy-done.5, bf16[1,24,1,2,64,128]{5,4,3,2,1,0:T(8,128)(2,1)S(1)} %bitcast.2, bf16[1,24,1,2,64,128]{5,4,3,2,1,0:T(8,128)(2,1)S(1)} %collective-permute-done.3.theirs), custom_call_target="tpu_custom_call" | custom-call | flops 4000000000 | bytes 12000000 | tf_op jit(solution)/shard_map/pallas_call | solution.py:60
  10.6 1.5 %collective-permute-done.1.refs_2_ = bf16[128,256]{1,0:T(8,128)(2,1)S(1)} collective-permute-done((bf16[128,256]{1,0:T(8,128)(2,1)}, bf16[128,256]{1,0:T(8,128)(2,1)S(1)}, u32[]{:S(2)}, u32[]{:S(2)}) %collective-permute-start.1) | collective-permute-done | bytes 65568 | tf_op jit(solution)/shard_map/ppermute | solution.py:16
  14.8 3.6 %collective-permute-start.8 = (bf16[64,512]{1,0:T(8,128)(2,1)S(1)}, bf16[64,512]{1,0:T(8,128)(2,1)S(1)}, u32[]{:S(2)}, u32[]{:S(2)}) collective-permute-start(bf16[64,512]{1,0:T(8,128)(2,1)S(1)} %get-tuple-element.49), channel_id=1, source_target_pairs={{0,6},{1,7},{2,4},{3,5},{4,2},{5,3},{6,0},{7,1},{8,14},{9,15},{10,... | collective-permute-start | bytes 196616 | tf_op jit(solution)/shard_map/ppermute | solution.py:16
  20.4 1.2 %collective-permute-start.18 = (bf16[2,32,1536]{2,1,0:T(8,128)(2,1)S(1)}, bf16[2,32,1536]{2,1,0:T(8,128)(2,1)S(1)}, u32[]{:S(2)}, u32[]{:S(2)}) collective-permute-start(bf16[2,32,1536]{2,1,0:T(8,128)(2,1)S(1)} %get-tuple-element.63), channel_id=1, source_target_pairs={{0,2},{1,3},{2,0},{3,1},{4,6},{5,7},{6,4},{7,5},{8,10},{9,11},{10,... | collective-permute-start | bytes 589832 | tf_op jit(solution)/shard_map/ppermute | solution.py:16
  22.3 1.8 %collective-permute-done.9.refs_1_ = bf16[64,512]{1,0:T(8,128)(2,1)S(1)} collective-permute-done((bf16[64,512]{1,0:T(8,128)(2,1)S(1)}, bf16[64,512]{1,0:T(8,128)(2,1)S(1)}, u32[]{:S(2)}, u32[]{:S(2)}) %collective-permute-start.9) | collective-permute-done | bytes 65568 | tf_op jit(solution)/shard_map/ppermute | solution.py:16
  24.5 2.4 %collective-permute-start.13 = (bf16[64,512]{1,0:T(8,128)(2,1)S(1)}, bf16[64,512]{1,0:T(8,128)(2,1)S(1)}, u32[]{:S(2)}, u32[]{:S(2)}) collective-permute-start(bf16[64,512]{1,0:T(8,128)(2,1)S(1)} %get-tuple-element.60.refs_0_), channel_id=1, source_target_pairs={{0,6},{1,7},{2,4},{3,5},{4,2},{5,3},{6,0},{7,1},{8,14},{9,15},{10,... | collective-permute-start | bytes 196616 | tf_op jit(solution)/shard_map/ppermute | solution.py:16
  27.8 1.2 %collective-permute-start.11 = (bf16[64,512]{1,0:T(8,128)(2,1)S(1)}, bf16[64,512]{1,0:T(8,128)(2,1)S(1)}, u32[]{:S(2)}, u32[]{:S(2)}) collective-permute-start(bf16[64,512]{1,0:T(8,128)(2,1)S(1)} %get-tuple-element.60.refs_0_), channel_id=1, source_target_pairs={{0,2},{1,3},{2,0},{3,1},{4,6},{5,7},{6,4},{7,5},{8,10},{9,11},{10,... | collective-permute-start | bytes 196616 | tf_op jit(solution)/shard_map/ppermute | solution.py:16
  29.0 2.5 %collective-permute-done.13.refs_3_ = bf16[64,512]{1,0:T(8,128)(2,1)S(1)} collective-permute-done((bf16[64,512]{1,0:T(8,128)(2,1)S(1)}, bf16[64,512]{1,0:T(8,128)(2,1)S(1)}, u32[]{:S(2)}, u32[]{:S(2)}) %collective-permute-start.13) | collective-permute-done | bytes 65568 | tf_op jit(solution)/shard_map/ppermute | solution.py:16
  31.5 2.4 %collective-permute-done.12.refs_2_ = bf16[64,512]{1,0:T(8,128)(2,1)S(1)} collective-permute-done((bf16[64,512]{1,0:T(8,128)(2,1)S(1)}, bf16[64,512]{1,0:T(8,128)(2,1)S(1)}, u32[]{:S(2)}, u32[]{:S(2)}) %collective-permute-start.12) | collective-permute-done | bytes 65568 | tf_op jit(solution)/shard_map/ppermute | solution.py:16
  36.1 1.3 %collective-permute-start.19 = (bf16[448,128]{1,0:T(8,128)(2,1)S(1)}, bf16[448,128]{1,0:T(8,128)(2,1)S(1)}, u32[]{:S(2)}, u32[]{:S(2)}) collective-permute-start(bf16[448,128]{1,0:T(8,128)(2,1)S(1)} %get-tuple-element.70), channel_id=1, source_target_pairs={{0,8},{8,0},{16,24},{24,16},{1,9},{9,1},{17,25},{25,17},{2,10},{10... | collective-permute-start | bytes 344072 | tf_op jit(solution)/shard_map/ppermute | solution.py:16
  37.4 1.5 %collective-permute-start.20 = (bf16[448,128]{1,0:T(8,128)(2,1)S(1)}, bf16[448,128]{1,0:T(8,128)(2,1)S(1)}, u32[]{:S(2)}, u32[]{:S(2)}) collective-permute-start(bf16[448,128]{1,0:T(8,128)(2,1)S(1)} %get-tuple-element.71), channel_id=1, source_target_pairs={{0,16},{8,24},{16,0},{24,8},{1,17},{9,25},{17,1},{25,9},{2,18},{10... | collective-permute-start | bytes 344072 | tf_op jit(solution)/shard_map/ppermute | solution.py:16
  40.4 1.5 %collective-permute-done.19.refs_3_ = bf16[448,128]{1,0:T(8,128)(2,1)S(1)} collective-permute-done((bf16[448,128]{1,0:T(8,128)(2,1)S(1)}, bf16[448,128]{1,0:T(8,128)(2,1)S(1)}, u32[]{:S(2)}, u32[]{:S(2)}) %collective-permute-start.19) | collective-permute-done | bytes 114720 | tf_op jit(solution)/shard_map/ppermute | solution.py:16
  41.9 3.1 %collective-permute-done.20.refs_2_ = bf16[448,128]{1,0:T(8,128)(2,1)S(1)} collective-permute-done((bf16[448,128]{1,0:T(8,128)(2,1)S(1)}, bf16[448,128]{1,0:T(8,128)(2,1)S(1)}, u32[]{:S(2)}, u32[]{:S(2)}) %collective-permute-start.20) | collective-permute-done | bytes 114720 | tf_op jit(solution)/shard_map/ppermute | solution.py:16
  45.1 1.8 %collective-permute-start.22 = (bf16[256,128]{1,0:T(8,128)(2,1)S(1)}, bf16[256,128]{1,0:T(8,128)(2,1)S(1)}, u32[]{:S(2)}, u32[]{:S(2)}) collective-permute-start(bf16[256,128]{1,0:T(8,128)(2,1)S(1)} %get-tuple-element.80), channel_id=1, source_target_pairs={{0,6},{1,7},{2,4},{3,5},{4,2},{5,3},{6,0},{7,1},{8,14},{9,15},{10,... | collective-permute-start | bytes 196616 | tf_op jit(solution)/shard_map/ppermute | solution.py:16
  46.9 2.7 %collective-permute-start.24 = (bf16[256,128]{1,0:T(8,128)(2,1)S(1)}, bf16[256,128]{1,0:T(8,128)(2,1)S(1)}, u32[]{:S(2)}, u32[]{:S(2)}) collective-permute-start(bf16[256,128]{1,0:T(8,128)(2,1)S(1)} %get-tuple-element.82), channel_id=1, source_target_pairs={{0,2},{1,3},{2,0},{3,1},{4,6},{5,7},{6,4},{7,5},{8,10},{9,11},{10,... | collective-permute-start | bytes 196616 | tf_op jit(solution)/shard_map/ppermute | solution.py:16
  49.6 1.9 %collective-permute-done.22.refs_0_ = bf16[256,128]{1,0:T(8,128)(2,1)S(1)} collective-permute-done((bf16[256,128]{1,0:T(8,128)(2,1)S(1)}, bf16[256,128]{1,0:T(8,128)(2,1)S(1)}, u32[]{:S(2)}, u32[]{:S(2)}) %collective-permute-start.22) | collective-permute-done | bytes 65568 | tf_op jit(solution)/shard_map/ppermute | solution.py:16
  51.4 1.5 %collective-permute-done.23.refs_1_ = bf16[256,128]{1,0:T(8,128)(2,1)S(1)} collective-permute-done((bf16[256,128]{1,0:T(8,128)(2,1)S(1)}, bf16[256,128]{1,0:T(8,128)(2,1)S(1)}, u32[]{:S(2)}, u32[]{:S(2)}) %collective-permute-start.23) | collective-permute-done | bytes 65568 | tf_op jit(solution)/shard_map/ppermute | solution.py:16
  53.0 1.6 %collective-permute-start.27 = (bf16[448,128]{1,0:T(8,128)(2,1)S(1)}, bf16[448,128]{1,0:T(8,128)(2,1)S(1)}, u32[]{:S(2)}, u32[]{:S(2)}) collective-permute-start(bf16[448,128]{1,0:T(8,128)(2,1)S(1)} %shard_map.95.refs_0_), channel_id=1, source_target_pairs={{0,24},{8,16},{16,8},{24,0},{1,25},{9,17},{17,9},{25,1},{2,26},{10... | collective-permute-start | bytes 344072 | tf_op jit(solution)/shard_map/ppermute | solution.py:16
  54.6 1.5 %collective-permute-start.26 = (bf16[448,128]{1,0:T(8,128)(2,1)S(1)}, bf16[448,128]{1,0:T(8,128)(2,1)S(1)}, u32[]{:S(2)}, u32[]{:S(2)}) collective-permute-start(bf16[448,128]{1,0:T(8,128)(2,1)S(1)} %shard_map.95.refs_0_), channel_id=1, source_target_pairs={{0,16},{8,24},{16,0},{24,8},{1,17},{9,25},{17,1},{25,9},{2,18},{10... | collective-permute-start | bytes 344072 | tf_op jit(solution)/shard_map/ppermute | solution.py:16
  56.6 3.2 %collective-permute-done.27.refs_3_ = bf16[448,128]{1,0:T(8,128)(2,1)S(1)} collective-permute-done((bf16[448,128]{1,0:T(8,128)(2,1)S(1)}, bf16[448,128]{1,0:T(8,128)(2,1)S(1)}, u32[]{:S(2)}, u32[]{:S(2)}) %collective-permute-start.27) | collective-permute-done | bytes 114720 | tf_op jit(solution)/shard_map/ppermute | solution.py:16
  59.8 1.2 %collective-permute-done.26.refs_2_ = bf16[448,128]{1,0:T(8,128)(2,1)S(1)} collective-permute-done((bf16[448,128]{1,0:T(8,128)(2,1)S(1)}, bf16[448,128]{1,0:T(8,128)(2,1)S(1)}, u32[]{:S(2)}, u32[]{:S(2)}) %collective-permute-start.26) | collective-permute-done | bytes 114720 | tf_op jit(solution)/shard_map/ppermute | solution.py:16
  61.5 1.2 %shard_map.96 = (f32[128,256]{1,0:T(8,128)}, f32[3,256,512]{2,1,0:T(8,128)}) custom-call(bf16[448,128]{1,0:T(8,128)(2,1)S(1)} %shard_map.95.refs_0_, bf16[448,128]{1,0:T(8,128)(2,1)S(1)} %collective-permute-done.25.refs_1_, bf16[448,128]{1,0:T(8,128)(2,1)S(1)} %collective-permute-done.26.refs_2_, bf16[448,128]{1,0:T(8,128)(2,1)S(1)} %collective-permute-done.27.refs_3_, ...), custom_call_target="tpu_custom_call" | custom-call | flops 900000000 | bytes 2700000 | tf_op jit(solution)/shard_map/pallas_call | solution.py:60
  (65 shorter events, 14.7 us)
Async XLA Ops:
  0.6 5.9 %collective-permute-start.3 = (bf16[1,24,1,2,64,128]{5,4,3,2,1,0:T(8,128)(2,1)}, bf16[1,24,1,2,64,128]{5,4,3,2,1,0:T(8,128)(2,1)S(1)}, u32[]{:S(2)}, u32[]{:S(2)}) collective-permute-start(bf16[1,24,1,2,64,128]{5,4,3,2,1,0:T(8,128)(2,1)} %bitcast.1), channel_id=1, source_target_pairs={{0,1},{1,0},{2,3},{3,2},{4,5},{5,4},{6,7},{7,6},{8,9},{9,8},{10,11... | collective-permute-start | bytes 2359304 | tf_op jit(solution)/shard_map/ppermute | solution.py:16
  1.2 9.4 %collective-permute-start.2 = (bf16[128,256]{1,0:T(8,128)(2,1)}, bf16[128,256]{1,0:T(8,128)(2,1)S(1)}, u32[]{:S(2)}, u32[]{:S(2)}) collective-permute-start(bf16[128,256]{1,0:T(8,128)(2,1)} %refs_0_.1), channel_id=1, source_target_pairs={{0,6},{1,7},{2,4},{3,5},{4,2},{5,3},{6,0},{7,1},{8,14},{9,15},{10,... | collective-permute-start | bytes 196616 | tf_op jit(solution)/shard_map/ppermute | solution.py:16
  5.8 6.3 %collective-permute-start.1 = (bf16[128,256]{1,0:T(8,128)(2,1)}, bf16[128,256]{1,0:T(8,128)(2,1)S(1)}, u32[]{:S(2)}, u32[]{:S(2)}) collective-permute-start(bf16[128,256]{1,0:T(8,128)(2,1)} %refs_0_.1), channel_id=1, source_target_pairs={{0,4},{1,5},{2,6},{3,7},{4,0},{5,1},{6,2},{7,3},{8,12},{9,13},{10,... | collective-permute-start | bytes 196616 | tf_op jit(solution)/shard_map/ppermute | solution.py:16
  5.8 6.3 %collective-permute-start = (bf16[128,256]{1,0:T(8,128)(2,1)}, bf16[128,256]{1,0:T(8,128)(2,1)S(1)}, u32[]{:S(2)}, u32[]{:S(2)}) collective-permute-start(bf16[128,256]{1,0:T(8,128)(2,1)} %refs_0_.1), channel_id=1, source_target_pairs={{0,2},{1,3},{2,0},{3,1},{4,6},{5,7},{6,4},{7,5},{8,10},{9,11},{10,... | collective-permute-start | bytes 196616 | tf_op jit(solution)/shard_map/ppermute | solution.py:16
  6.5 6.5 %collective-permute-start.4 = (bf16[128,256]{1,0:T(8,128)(2,1)}, bf16[128,256]{1,0:T(8,128)(2,1)S(1)}, u32[]{:S(2)}, u32[]{:S(2)}) collective-permute-start(bf16[128,256]{1,0:T(8,128)(2,1)} %refs_0_.1), channel_id=1, source_target_pairs={{0,1},{1,0},{2,3},{3,2},{4,5},{5,4},{6,7},{7,6},{8,9},{9,8},{10,11... | collective-permute-start | bytes 196616 | tf_op jit(solution)/shard_map/ppermute | solution.py:16
  14.8 7.5 %collective-permute-start.8 = (bf16[64,512]{1,0:T(8,128)(2,1)S(1)}, bf16[64,512]{1,0:T(8,128)(2,1)S(1)}, u32[]{:S(2)}, u32[]{:S(2)}) collective-permute-start(bf16[64,512]{1,0:T(8,128)(2,1)S(1)} %get-tuple-element.49), channel_id=1, source_target_pairs={{0,6},{1,7},{2,4},{3,5},{4,2},{5,3},{6,0},{7,1},{8,14},{9,15},{10,... | collective-permute-start | bytes 196616 | tf_op jit(solution)/shard_map/ppermute | solution.py:16
  18.4 5.7 %collective-permute-start.9 = (bf16[64,512]{1,0:T(8,128)(2,1)S(1)}, bf16[64,512]{1,0:T(8,128)(2,1)S(1)}, u32[]{:S(2)}, u32[]{:S(2)}) collective-permute-start(bf16[64,512]{1,0:T(8,128)(2,1)S(1)} %get-tuple-element.50), channel_id=1, source_target_pairs={{0,4},{1,5},{2,6},{3,7},{4,0},{5,1},{6,2},{7,3},{8,12},{9,13},{10,... | collective-permute-start | bytes 196616 | tf_op jit(solution)/shard_map/ppermute | solution.py:16
  18.4 6.0 %collective-permute-start.10 = (bf16[64,512]{1,0:T(8,128)(2,1)S(1)}, bf16[64,512]{1,0:T(8,128)(2,1)S(1)}, u32[]{:S(2)}, u32[]{:S(2)}) collective-permute-start(bf16[64,512]{1,0:T(8,128)(2,1)S(1)} %get-tuple-element.51), channel_id=1, source_target_pairs={{0,2},{1,3},{2,0},{3,1},{4,6},{5,7},{6,4},{7,5},{8,10},{9,11},{10,... | collective-permute-start | bytes 196616 | tf_op jit(solution)/shard_map/ppermute | solution.py:16
  20.4 14.7 %collective-permute-start.18 = (bf16[2,32,1536]{2,1,0:T(8,128)(2,1)S(1)}, bf16[2,32,1536]{2,1,0:T(8,128)(2,1)S(1)}, u32[]{:S(2)}, u32[]{:S(2)}) collective-permute-start(bf16[2,32,1536]{2,1,0:T(8,128)(2,1)S(1)} %get-tuple-element.63), channel_id=1, source_target_pairs={{0,2},{1,3},{2,0},{3,1},{4,6},{5,7},{6,4},{7,5},{8,10},{9,11},{10,... | collective-permute-start | bytes 589832 | tf_op jit(solution)/shard_map/ppermute | solution.py:16
  24.5 6.9 %collective-permute-start.13 = (bf16[64,512]{1,0:T(8,128)(2,1)S(1)}, bf16[64,512]{1,0:T(8,128)(2,1)S(1)}, u32[]{:S(2)}, u32[]{:S(2)}) collective-permute-start(bf16[64,512]{1,0:T(8,128)(2,1)S(1)} %get-tuple-element.60.refs_0_), channel_id=1, source_target_pairs={{0,6},{1,7},{2,4},{3,5},{4,2},{5,3},{6,0},{7,1},{8,14},{9,15},{10,... | collective-permute-start | bytes 196616 | tf_op jit(solution)/shard_map/ppermute | solution.py:16
  26.9 6.9 %collective-permute-start.12 = (bf16[64,512]{1,0:T(8,128)(2,1)S(1)}, bf16[64,512]{1,0:T(8,128)(2,1)S(1)}, u32[]{:S(2)}, u32[]{:S(2)}) collective-permute-start(bf16[64,512]{1,0:T(8,128)(2,1)S(1)} %get-tuple-element.60.refs_0_), channel_id=1, source_target_pairs={{0,4},{1,5},{2,6},{3,7},{4,0},{5,1},{6,2},{7,3},{8,12},{9,13},{10,... | collective-permute-start | bytes 196616 | tf_op jit(solution)/shard_map/ppermute | solution.py:16
  27.8 6.1 %collective-permute-start.11 = (bf16[64,512]{1,0:T(8,128)(2,1)S(1)}, bf16[64,512]{1,0:T(8,128)(2,1)S(1)}, u32[]{:S(2)}, u32[]{:S(2)}) collective-permute-start(bf16[64,512]{1,0:T(8,128)(2,1)S(1)} %get-tuple-element.60.refs_0_), channel_id=1, source_target_pairs={{0,2},{1,3},{2,0},{3,1},{4,6},{5,7},{6,4},{7,5},{8,10},{9,11},{10,... | collective-permute-start | bytes 196616 | tf_op jit(solution)/shard_map/ppermute | solution.py:16
  29.0 6.1 %collective-permute-start.14 = (bf16[64,512]{1,0:T(8,128)(2,1)S(1)}, bf16[64,512]{1,0:T(8,128)(2,1)S(1)}, u32[]{:S(2)}, u32[]{:S(2)}) collective-permute-start(bf16[64,512]{1,0:T(8,128)(2,1)S(1)} %get-tuple-element.60.refs_0_), channel_id=1, source_target_pairs={{0,1},{1,0},{2,3},{3,2},{4,5},{5,4},{6,7},{7,6},{8,9},{9,8},{10,11... | collective-permute-start | bytes 196616 | tf_op jit(solution)/shard_map/ppermute | solution.py:16
  31.5 3.6 %collective-permute-start.17 = (bf16[64,512]{1,0:T(8,128)(2,1)S(1)}, bf16[64,512]{1,0:T(8,128)(2,1)S(1)}, u32[]{:S(2)}, u32[]{:S(2)}) collective-permute-start(bf16[64,512]{1,0:T(8,128)(2,1)S(1)} %collective-permute-done.13.refs_3_), channel_id=1, source_target_pairs={{0,1},{1,0},{2,3},{3,2},{4,5},{5,4},{6,7},{7,6},{8,9},{9,8},{10,11... | collective-permute-start | bytes 196616 | tf_op jit(solution)/shard_map/ppermute | solution.py:16
  36.1 5.7 %collective-permute-start.19 = (bf16[448,128]{1,0:T(8,128)(2,1)S(1)}, bf16[448,128]{1,0:T(8,128)(2,1)S(1)}, u32[]{:S(2)}, u32[]{:S(2)}) collective-permute-start(bf16[448,128]{1,0:T(8,128)(2,1)S(1)} %get-tuple-element.70), channel_id=1, source_target_pairs={{0,8},{8,0},{16,24},{24,16},{1,9},{9,1},{17,25},{25,17},{2,10},{10... | collective-permute-start | bytes 344072 | tf_op jit(solution)/shard_map/ppermute | solution.py:16
  37.4 7.6 %collective-permute-start.20 = (bf16[448,128]{1,0:T(8,128)(2,1)S(1)}, bf16[448,128]{1,0:T(8,128)(2,1)S(1)}, u32[]{:S(2)}, u32[]{:S(2)}) collective-permute-start(bf16[448,128]{1,0:T(8,128)(2,1)S(1)} %get-tuple-element.71), channel_id=1, source_target_pairs={{0,16},{8,24},{16,0},{24,8},{1,17},{9,25},{17,1},{25,9},{2,18},{10... | collective-permute-start | bytes 344072 | tf_op jit(solution)/shard_map/ppermute | solution.py:16
  39.0 6.0 %collective-permute-start.21 = (bf16[448,128]{1,0:T(8,128)(2,1)S(1)}, bf16[448,128]{1,0:T(8,128)(2,1)S(1)}, u32[]{:S(2)}, u32[]{:S(2)}) collective-permute-start(bf16[448,128]{1,0:T(8,128)(2,1)S(1)} %get-tuple-element.72), channel_id=1, source_target_pairs={{0,24},{8,16},{16,8},{24,0},{1,25},{9,17},{17,9},{25,1},{2,26},{10... | collective-permute-start | bytes 344072 | tf_op jit(solution)/shard_map/ppermute | solution.py:16
  45.1 6.3 %collective-permute-start.22 = (bf16[256,128]{1,0:T(8,128)(2,1)S(1)}, bf16[256,128]{1,0:T(8,128)(2,1)S(1)}, u32[]{:S(2)}, u32[]{:S(2)}) collective-permute-start(bf16[256,128]{1,0:T(8,128)(2,1)S(1)} %get-tuple-element.80), channel_id=1, source_target_pairs={{0,6},{1,7},{2,4},{3,5},{4,2},{5,3},{6,0},{7,1},{8,14},{9,15},{10,... | collective-permute-start | bytes 196616 | tf_op jit(solution)/shard_map/ppermute | solution.py:16
  46.9 6.1 %collective-permute-start.23 = (bf16[256,128]{1,0:T(8,128)(2,1)S(1)}, bf16[256,128]{1,0:T(8,128)(2,1)S(1)}, u32[]{:S(2)}, u32[]{:S(2)}) collective-permute-start(bf16[256,128]{1,0:T(8,128)(2,1)S(1)} %get-tuple-element.81), channel_id=1, source_target_pairs={{0,4},{1,5},{2,6},{3,7},{4,0},{5,1},{6,2},{7,3},{8,12},{9,13},{10,... | collective-permute-start | bytes 196616 | tf_op jit(solution)/shard_map/ppermute | solution.py:16
  46.9 6.1 %collective-permute-start.24 = (bf16[256,128]{1,0:T(8,128)(2,1)S(1)}, bf16[256,128]{1,0:T(8,128)(2,1)S(1)}, u32[]{:S(2)}, u32[]{:S(2)}) collective-permute-start(bf16[256,128]{1,0:T(8,128)(2,1)S(1)} %get-tuple-element.82), channel_id=1, source_target_pairs={{0,2},{1,3},{2,0},{3,1},{4,6},{5,7},{6,4},{7,5},{8,10},{9,11},{10,... | collective-permute-start | bytes 196616 | tf_op jit(solution)/shard_map/ppermute | solution.py:16
  53.0 6.8 %collective-permute-start.27 = (bf16[448,128]{1,0:T(8,128)(2,1)S(1)}, bf16[448,128]{1,0:T(8,128)(2,1)S(1)}, u32[]{:S(2)}, u32[]{:S(2)}) collective-permute-start(bf16[448,128]{1,0:T(8,128)(2,1)S(1)} %shard_map.95.refs_0_), channel_id=1, source_target_pairs={{0,24},{8,16},{16,8},{24,0},{1,25},{9,17},{17,9},{25,1},{2,26},{10... | collective-permute-start | bytes 344072 | tf_op jit(solution)/shard_map/ppermute | solution.py:16
  54.6 6.3 %collective-permute-start.26 = (bf16[448,128]{1,0:T(8,128)(2,1)S(1)}, bf16[448,128]{1,0:T(8,128)(2,1)S(1)}, u32[]{:S(2)}, u32[]{:S(2)}) collective-permute-start(bf16[448,128]{1,0:T(8,128)(2,1)S(1)} %shard_map.95.refs_0_), channel_id=1, source_target_pairs={{0,16},{8,24},{16,0},{24,8},{1,17},{9,25},{17,1},{25,9},{2,18},{10... | collective-permute-start | bytes 344072 | tf_op jit(solution)/shard_map/ppermute | solution.py:16
  56.1 5.2 %collective-permute-start.25 = (bf16[448,128]{1,0:T(8,128)(2,1)S(1)}, bf16[448,128]{1,0:T(8,128)(2,1)S(1)}, u32[]{:S(2)}, u32[]{:S(2)}) collective-permute-start(bf16[448,128]{1,0:T(8,128)(2,1)S(1)} %shard_map.95.refs_0_), channel_id=1, source_target_pairs={{0,8},{8,0},{16,24},{24,16},{1,9},{9,1},{17,25},{25,17},{2,10},{10... | collective-permute-start | bytes 344072 | tf_op jit(solution)/shard_map/ppermute | solution.py:16
  56.5 5.0 %collective-permute-start.28 = (bf16[448,128]{1,0:T(8,128)(2,1)S(1)}, bf16[448,128]{1,0:T(8,128)(2,1)S(1)}, u32[]{:S(2)}, u32[]{:S(2)}) collective-permute-start(bf16[448,128]{1,0:T(8,128)(2,1)S(1)} %shard_map.95.refs_0_), channel_id=1, source_target_pairs={{0,1},{1,0},{2,3},{3,2},{4,5},{5,4},{6,7},{7,6},{8,9},{9,8},{10,11... | collective-permute-start | bytes 344072 | tf_op jit(solution)/shard_map/ppermute | solution.py:16
  (14 other events, 33.4 us)

commit v6 on v5

--- a/solution.py
+++ b/solution.py
@@ -20,19 +20,17 @@
     return [swap(array, axis, (k + 1) * unit) for k, array in enumerate(arrays)]
 
 
+def reach(count):
+    return sorted(range(1, count + 1), key=lambda k: (-k.bit_length(), k))
+
+
 def by_reach(parts):
     return [parts[k - 1] for k in reach(len(parts))]
 
 
-def reach(count):
-    return sorted(range(1, count + 1), reverse=True)
-
-
 def together(parts, *others):
-    ks = reach(len(parts))[::-1]
-    out = lax.optimization_barrier((*[parts[k - 1] for k in ks], *others))
-    made = dict(zip(ks, out))
-    return [made[k] for k in sorted(made)], *out[len(ks):]
+    out = lax.optimization_barrier((*parts, *others))
+    return list(out[:len(parts)]), *out[len(parts):]
 
 
 def tree_sum(parts):
@@ -67,6 +65,10 @@
         cost_estimate=cost(time),
         input_output_aliases=aliases or {},
     )(*args)
+
+
+def hbm(array):
+    return pltpu.with_memory_space_constraint(array, pltpu.HBM)
 
 
 def here():
@@ -389,7 +391,7 @@
     dense = call(
         functools.partial(place_tiles, block_count),
         struct((2, rows, items), BF16),
-        (tile_order, tile_counts, tiles, other_tiles),
+        (hbm(tile_order), hbm(tile_counts), hbm(tiles), other_tiles),
         4,
         scratch=[
             pltpu.SMEM(tile_order.shape, jnp.int32),

time: 63.7 us -> 62.2 us (0.976)
  local copies, waits for them, and re-layouts: 2.46 us -> 0.02 us
  Pallas kernels: 9.28 us -> 10.3 us
  starting transfers between devices: 28.7 us -> 27.8 us
  waiting for transfers between devices: 22.4 us -> 23.1 us
    unnamed x12 -> x6, local copies, waits for them, and re-layouts: 2.46 us -> 0.02 us
    pallas_call x13, Pallas kernels: 9.28 us -> 10.3 us  [call(): pl.pallas_call(body, out_shape=outs, in_specs=specs or [vmem] * len(args)...]
    ppermute x32, starting transfers between devices: 28.7 us -> 27.8 us  [swap(): lax.ppermute(array, axis, [(i, i ^ step) for i in range(lax.axis_size(axi...]
    ppermute x32, waiting for transfers between devices: 22.4 us -> 23.1 us  [swap(): lax.ppermute(array, axis, [(i, i ^ step) for i in range(lax.axis_size(axi...]
  transfers between devices with their start and end apart: 32 -> 32, of which waited for: 16 -> 16; matrix products, arithmetic and copies ran while one was open for 0% -> 0% of each run, Pallas kernels for 10% -> 12%
where the time goes in v6:
time: 62.2 us; the launch traced here: 62 us
  starting transfers between devices  27.8 us (45%)
  waiting for transfers between devices  23.1 us (37%)
  Pallas kernels  10.3 us (17%)
  between operations  0.81 us (1%)
    ppermute x32, starting transfers between devices, swap(): lax.ppermute(array, axis, [(i, i ^ step) for i in range(lax.axis_size(axi...  27.8 us
    ppermute x32, waiting for transfers between devices, swap(): lax.ppermute(array, axis, [(i, i ^ step) for i in range(lax.axis_size(axi...  23.1 us
    pallas_call x13, Pallas kernels, call(): pl.pallas_call(body, out_shape=outs, in_specs=specs or [vmem] * len(args)...  10.3 us
  transfers between devices with their start and end apart: 32, of which 16 were waited for; matrix products, arithmetic and copies ran while one was open for 0% of the time, Pallas kernels for 12%

profile of v6, /device:TPU:0, one launch (start us, length us, event | category | flops | bytes accessed | tf_op | source)
XLA Modules:
  0.0 62.0 jit_solution(9720582946927427400)
XLA Ops:
  1.2 4.7 %collective-permute-start.2 = (bf16[128,256]{1,0:T(8,128)(2,1)}, bf16[128,256]{1,0:T(8,128)(2,1)S(1)}, u32[]{:S(2)}, u32[]{:S(2)}) collective-permute-start(bf16[128,256]{1,0:T(8,128)(2,1)} %refs_0_.1), channel_id=1, source_target_pairs={{0,6},{1,7},{2,4},{3,5},{4,2},{5,3},{6,0},{7,1},{8,14},{9,15},{10,... | collective-permute-start | bytes 196616 | tf_op jit(solution)/shard_map/ppermute | solution.py:16
  6.5 2.6 %shard_map.85.dense = bf16[2,768,1024]{2,1,0:T(8,128)(2,1)S(1)} custom-call(s32[1,96]{1,0:T(1,128)} %order.1, s32[1,8]{1,0:T(1,128)} %counts.1, bf16[1,24,1,2,64,128]{5,4,3,2,1,0:T(8,128)(2,1)} %bitcast.2, bf16[1,24,1,2,64,128]{5,4,3,2,1,0:T(8,128)(2,1)S(1)} %collective-permute-done.3.theirs), custom_call_target="tpu_custom_call" | custom-call | flops 4000000000 | bytes 12000000 | tf_op jit(solution)/shard_map/pallas_call | solution.py:58
  9.2 3.0 %collective-permute-done.1.refs_2_ = bf16[128,256]{1,0:T(8,128)(2,1)S(1)} collective-permute-done((bf16[128,256]{1,0:T(8,128)(2,1)}, bf16[128,256]{1,0:T(8,128)(2,1)S(1)}, u32[]{:S(2)}, u32[]{:S(2)}) %collective-permute-start.1) | collective-permute-done | bytes 65568 | tf_op jit(solution)/shard_map/ppermute | solution.py:16
  14.8 1.2 %collective-permute-start.8 = (bf16[64,512]{1,0:T(8,128)(2,1)S(1)}, bf16[64,512]{1,0:T(8,128)(2,1)S(1)}, u32[]{:S(2)}, u32[]{:S(2)}) collective-permute-start(bf16[64,512]{1,0:T(8,128)(2,1)S(1)} %get-tuple-element.49), channel_id=1, source_target_pairs={{0,4},{1,5},{2,6},{3,7},{4,0},{5,1},{6,2},{7,3},{8,12},{9,13},{10,... | collective-permute-start | bytes 196616 | tf_op jit(solution)/shard_map/ppermute | solution.py:16
  16.1 2.4 %collective-permute-start.9 = (bf16[64,512]{1,0:T(8,128)(2,1)S(1)}, bf16[64,512]{1,0:T(8,128)(2,1)S(1)}, u32[]{:S(2)}, u32[]{:S(2)}) collective-permute-start(bf16[64,512]{1,0:T(8,128)(2,1)S(1)} %get-tuple-element.50), channel_id=1, source_target_pairs={{0,6},{1,7},{2,4},{3,5},{4,2},{5,3},{6,0},{7,1},{8,14},{9,15},{10,... | collective-permute-start | bytes 196616 | tf_op jit(solution)/shard_map/ppermute | solution.py:16
  18.5 1.1 %shard_map.90 = (f32[2,32,1536]{2,1,0:T(8,128)S(1)}, bf16[2,32,1536]{2,1,0:T(8,128)(2,1)S(1)}) custom-call(bf16[2,768,1024]{2,1,0:T(8,128)(2,1)S(1)} %shard_map.85.dense, bf16[512,256]{1,0:T(8,128)(2,1)S(1)} %get-tuple-element.61.mine, bf16[512,256]{1,0:T(8,128)(2,1)S(1)} %get-tuple-element.62.theirs), custom_call_target="tpu_custom_call" | custom-call | flops 3000000000 | bytes 9000000 | tf_op jit(solution)/shard_map/pallas_call | solution.py:58
  19.6 2.1 %collective-permute-start.18 = (bf16[2,32,1536]{2,1,0:T(8,128)(2,1)S(1)}, bf16[2,32,1536]{2,1,0:T(8,128)(2,1)S(1)}, u32[]{:S(2)}, u32[]{:S(2)}) collective-permute-start(bf16[2,32,1536]{2,1,0:T(8,128)(2,1)S(1)} %get-tuple-element.63), channel_id=1, source_target_pairs={{0,2},{1,3},{2,0},{3,1},{4,6},{5,7},{6,4},{7,5},{8,10},{9,11},{10,... | collective-permute-start | bytes 589832 | tf_op jit(solution)/shard_map/ppermute | solution.py:16
  22.4 1.1 %collective-permute-done.8.refs_0_ = bf16[64,512]{1,0:T(8,128)(2,1)S(1)} collective-permute-done((bf16[64,512]{1,0:T(8,128)(2,1)S(1)}, bf16[64,512]{1,0:T(8,128)(2,1)S(1)}, u32[]{:S(2)}, u32[]{:S(2)}) %collective-permute-start.8) | collective-permute-done | bytes 65568 | tf_op jit(solution)/shard_map/ppermute | solution.py:16
  24.5 2.0 %collective-permute-start.13 = (bf16[64,512]{1,0:T(8,128)(2,1)S(1)}, bf16[64,512]{1,0:T(8,128)(2,1)S(1)}, u32[]{:S(2)}, u32[]{:S(2)}) collective-permute-start(bf16[64,512]{1,0:T(8,128)(2,1)S(1)} %get-tuple-element.60.refs_0_), channel_id=1, source_target_pairs={{0,6},{1,7},{2,4},{3,5},{4,2},{5,3},{6,0},{7,1},{8,14},{9,15},{10,... | collective-permute-start | bytes 196616 | tf_op jit(solution)/shard_map/ppermute | solution.py:16
  26.5 2.4 %collective-permute-start.11 = (bf16[64,512]{1,0:T(8,128)(2,1)S(1)}, bf16[64,512]{1,0:T(8,128)(2,1)S(1)}, u32[]{:S(2)}, u32[]{:S(2)}) collective-permute-start(bf16[64,512]{1,0:T(8,128)(2,1)S(1)} %get-tuple-element.60.refs_0_), channel_id=1, source_target_pairs={{0,2},{1,3},{2,0},{3,1},{4,6},{5,7},{6,4},{7,5},{8,10},{9,11},{10,... | collective-permute-start | bytes 196616 | tf_op jit(solution)/shard_map/ppermute | solution.py:16
  28.9 1.7 %collective-permute-done.13.refs_3_ = bf16[64,512]{1,0:T(8,128)(2,1)S(1)} collective-permute-done((bf16[64,512]{1,0:T(8,128)(2,1)S(1)}, bf16[64,512]{1,0:T(8,128)(2,1)S(1)}, u32[]{:S(2)}, u32[]{:S(2)}) %collective-permute-start.13) | collective-permute-done | bytes 65568 | tf_op jit(solution)/shard_map/ppermute | solution.py:16
  30.6 2.2 %collective-permute-done.12.refs_2_ = bf16[64,512]{1,0:T(8,128)(2,1)S(1)} collective-permute-done((bf16[64,512]{1,0:T(8,128)(2,1)S(1)}, bf16[64,512]{1,0:T(8,128)(2,1)S(1)}, u32[]{:S(2)}, u32[]{:S(2)}) %collective-permute-start.12) | collective-permute-done | bytes 65568 | tf_op jit(solution)/shard_map/ppermute | solution.py:16
  35.1 1.6 %collective-permute-start.19 = (bf16[448,128]{1,0:T(8,128)(2,1)S(1)}, bf16[448,128]{1,0:T(8,128)(2,1)S(1)}, u32[]{:S(2)}, u32[]{:S(2)}) collective-permute-start(bf16[448,128]{1,0:T(8,128)(2,1)S(1)} %get-tuple-element.70), channel_id=1, source_target_pairs={{0,8},{8,0},{16,24},{24,16},{1,9},{9,1},{17,25},{25,17},{2,10},{10... | collective-permute-start | bytes 344072 | tf_op jit(solution)/shard_map/ppermute | solution.py:16
  36.6 1.5 %collective-permute-start.20 = (bf16[448,128]{1,0:T(8,128)(2,1)S(1)}, bf16[448,128]{1,0:T(8,128)(2,1)S(1)}, u32[]{:S(2)}, u32[]{:S(2)}) collective-permute-start(bf16[448,128]{1,0:T(8,128)(2,1)S(1)} %get-tuple-element.71), channel_id=1, source_target_pairs={{0,16},{8,24},{16,0},{24,8},{1,17},{9,25},{17,1},{25,9},{2,18},{10... | collective-permute-start | bytes 344072 | tf_op jit(solution)/shard_map/ppermute | solution.py:16
  39.3 1.2 %collective-permute-done.19.refs_3_ = bf16[448,128]{1,0:T(8,128)(2,1)S(1)} collective-permute-done((bf16[448,128]{1,0:T(8,128)(2,1)S(1)}, bf16[448,128]{1,0:T(8,128)(2,1)S(1)}, u32[]{:S(2)}, u32[]{:S(2)}) %collective-permute-start.19) | collective-permute-done | bytes 114720 | tf_op jit(solution)/shard_map/ppermute | solution.py:16
  40.6 3.7 %collective-permute-done.20.refs_2_ = bf16[448,128]{1,0:T(8,128)(2,1)S(1)} collective-permute-done((bf16[448,128]{1,0:T(8,128)(2,1)S(1)}, bf16[448,128]{1,0:T(8,128)(2,1)S(1)}, u32[]{:S(2)}, u32[]{:S(2)}) %collective-permute-start.20) | collective-permute-done | bytes 114720 | tf_op jit(solution)/shard_map/ppermute | solution.py:16
  44.9 1.9 %collective-permute-start.23 = (bf16[256,128]{1,0:T(8,128)(2,1)S(1)}, bf16[256,128]{1,0:T(8,128)(2,1)S(1)}, u32[]{:S(2)}, u32[]{:S(2)}) collective-permute-start(bf16[256,128]{1,0:T(8,128)(2,1)S(1)} %get-tuple-element.81), channel_id=1, source_target_pairs={{0,6},{1,7},{2,4},{3,5},{4,2},{5,3},{6,0},{7,1},{8,14},{9,15},{10,... | collective-permute-start | bytes 196616 | tf_op jit(solution)/shard_map/ppermute | solution.py:16
  46.8 1.1 %collective-permute-start.24 = (bf16[256,128]{1,0:T(8,128)(2,1)S(1)}, bf16[256,128]{1,0:T(8,128)(2,1)S(1)}, u32[]{:S(2)}, u32[]{:S(2)}) collective-permute-start(bf16[256,128]{1,0:T(8,128)(2,1)S(1)} %get-tuple-element.82), channel_id=1, source_target_pairs={{0,2},{1,3},{2,0},{3,1},{4,6},{5,7},{6,4},{7,5},{8,10},{9,11},{10,... | collective-permute-start | bytes 196616 | tf_op jit(solution)/shard_map/ppermute | solution.py:16
  47.9 3.3 %collective-permute-done.22.refs_0_ = bf16[256,128]{1,0:T(8,128)(2,1)S(1)} collective-permute-done((bf16[256,128]{1,0:T(8,128)(2,1)S(1)}, bf16[256,128]{1,0:T(8,128)(2,1)S(1)}, u32[]{:S(2)}, u32[]{:S(2)}) %collective-permute-start.22) | collective-permute-done | bytes 65568 | tf_op jit(solution)/shard_map/ppermute | solution.py:16
  51.9 1.8 %collective-permute-start.27 = (bf16[448,128]{1,0:T(8,128)(2,1)S(1)}, bf16[448,128]{1,0:T(8,128)(2,1)S(1)}, u32[]{:S(2)}, u32[]{:S(2)}) collective-permute-start(bf16[448,128]{1,0:T(8,128)(2,1)S(1)} %shard_map.95.refs_0_), channel_id=1, source_target_pairs={{0,24},{8,16},{16,8},{24,0},{1,25},{9,17},{17,9},{25,1},{2,26},{10... | collective-permute-start | bytes 344072 | tf_op jit(solution)/shard_map/ppermute | solution.py:16
  53.7 1.3 %collective-permute-start.26 = (bf16[448,128]{1,0:T(8,128)(2,1)S(1)}, bf16[448,128]{1,0:T(8,128)(2,1)S(1)}, u32[]{:S(2)}, u32[]{:S(2)}) collective-permute-start(bf16[448,128]{1,0:T(8,128)(2,1)S(1)} %shard_map.95.refs_0_), channel_id=1, source_target_pairs={{0,16},{8,24},{16,0},{24,8},{1,17},{9,25},{17,1},{25,9},{2,18},{10... | collective-permute-start | bytes 344072 | tf_op jit(solution)/shard_map/ppermute | solution.py:16
  55.4 2.2 %collective-permute-done.27.refs_3_ = bf16[448,128]{1,0:T(8,128)(2,1)S(1)} collective-permute-done((bf16[448,128]{1,0:T(8,128)(2,1)S(1)}, bf16[448,128]{1,0:T(8,128)(2,1)S(1)}, u32[]{:S(2)}, u32[]{:S(2)}) %collective-permute-start.27) | collective-permute-done | bytes 114720 | tf_op jit(solution)/shard_map/ppermute | solution.py:16
  57.7 1.2 %collective-permute-done.26.refs_2_ = bf16[448,128]{1,0:T(8,128)(2,1)S(1)} collective-permute-done((bf16[448,128]{1,0:T(8,128)(2,1)S(1)}, bf16[448,128]{1,0:T(8,128)(2,1)S(1)}, u32[]{:S(2)}, u32[]{:S(2)}) %collective-permute-start.26) | collective-permute-done | bytes 114720 | tf_op jit(solution)/shard_map/ppermute | solution.py:16
  59.8 1.2 %shard_map.96 = (f32[128,256]{1,0:T(8,128)}, f32[3,256,512]{2,1,0:T(8,128)}) custom-call(bf16[448,128]{1,0:T(8,128)(2,1)S(1)} %shard_map.95.refs_0_, bf16[448,128]{1,0:T(8,128)(2,1)S(1)} %collective-permute-done.25.refs_1_, bf16[448,128]{1,0:T(8,128)(2,1)S(1)} %collective-permute-done.26.refs_2_, bf16[448,128]{1,0:T(8,128)(2,1)S(1)} %collective-permute-done.27.refs_3_, ...), custom_call_target="tpu_custom_call" | custom-call | flops 900000000 | bytes 2700000 | tf_op jit(solution)/shard_map/pallas_call | solution.py:58
  (59 shorter events, 12.6 us)
Async XLA Ops:
  0.6 5.9 %collective-permute-start.3 = (bf16[1,24,1,2,64,128]{5,4,3,2,1,0:T(8,128)(2,1)}, bf16[1,24,1,2,64,128]{5,4,3,2,1,0:T(8,128)(2,1)S(1)}, u32[]{:S(2)}, u32[]{:S(2)}) collective-permute-start(bf16[1,24,1,2,64,128]{5,4,3,2,1,0:T(8,128)(2,1)} %bitcast.1), channel_id=1, source_target_pairs={{0,1},{1,0},{2,3},{3,2},{4,5},{5,4},{6,7},{7,6},{8,9},{9,8},{10,11... | collective-permute-start | bytes 2359304 | tf_op jit(solution)/shard_map/ppermute | solution.py:16
  1.2 8.0 %collective-permute-start.2 = (bf16[128,256]{1,0:T(8,128)(2,1)}, bf16[128,256]{1,0:T(8,128)(2,1)S(1)}, u32[]{:S(2)}, u32[]{:S(2)}) collective-permute-start(bf16[128,256]{1,0:T(8,128)(2,1)} %refs_0_.1), channel_id=1, source_target_pairs={{0,6},{1,7},{2,4},{3,5},{4,2},{5,3},{6,0},{7,1},{8,14},{9,15},{10,... | collective-permute-start | bytes 196616 | tf_op jit(solution)/shard_map/ppermute | solution.py:16
  5.8 6.3 %collective-permute-start.1 = (bf16[128,256]{1,0:T(8,128)(2,1)}, bf16[128,256]{1,0:T(8,128)(2,1)S(1)}, u32[]{:S(2)}, u32[]{:S(2)}) collective-permute-start(bf16[128,256]{1,0:T(8,128)(2,1)} %refs_0_.1), channel_id=1, source_target_pairs={{0,4},{1,5},{2,6},{3,7},{4,0},{5,1},{6,2},{7,3},{8,12},{9,13},{10,... | collective-permute-start | bytes 196616 | tf_op jit(solution)/shard_map/ppermute | solution.py:16
  5.8 6.3 %collective-permute-start = (bf16[128,256]{1,0:T(8,128)(2,1)}, bf16[128,256]{1,0:T(8,128)(2,1)S(1)}, u32[]{:S(2)}, u32[]{:S(2)}) collective-permute-start(bf16[128,256]{1,0:T(8,128)(2,1)} %refs_0_.1), channel_id=1, source_target_pairs={{0,2},{1,3},{2,0},{3,1},{4,6},{5,7},{6,4},{7,5},{8,10},{9,11},{10,... | collective-permute-start | bytes 196616 | tf_op jit(solution)/shard_map/ppermute | solution.py:16
  6.5 6.5 %collective-permute-start.4 = (bf16[128,256]{1,0:T(8,128)(2,1)}, bf16[128,256]{1,0:T(8,128)(2,1)S(1)}, u32[]{:S(2)}, u32[]{:S(2)}) collective-permute-start(bf16[128,256]{1,0:T(8,128)(2,1)} %refs_0_.1), channel_id=1, source_target_pairs={{0,1},{1,0},{2,3},{3,2},{4,5},{5,4},{6,7},{7,6},{8,9},{9,8},{10,11... | collective-permute-start | bytes 196616 | tf_op jit(solution)/shard_map/ppermute | solution.py:16
  14.8 8.6 %collective-permute-start.8 = (bf16[64,512]{1,0:T(8,128)(2,1)S(1)}, bf16[64,512]{1,0:T(8,128)(2,1)S(1)}, u32[]{:S(2)}, u32[]{:S(2)}) collective-permute-start(bf16[64,512]{1,0:T(8,128)(2,1)S(1)} %get-tuple-element.49), channel_id=1, source_target_pairs={{0,4},{1,5},{2,6},{3,7},{4,0},{5,1},{6,2},{7,3},{8,12},{9,13},{10,... | collective-permute-start | bytes 196616 | tf_op jit(solution)/shard_map/ppermute | solution.py:16
  16.1 7.3 %collective-permute-start.9 = (bf16[64,512]{1,0:T(8,128)(2,1)S(1)}, bf16[64,512]{1,0:T(8,128)(2,1)S(1)}, u32[]{:S(2)}, u32[]{:S(2)}) collective-permute-start(bf16[64,512]{1,0:T(8,128)(2,1)S(1)} %get-tuple-element.50), channel_id=1, source_target_pairs={{0,6},{1,7},{2,4},{3,5},{4,2},{5,3},{6,0},{7,1},{8,14},{9,15},{10,... | collective-permute-start | bytes 196616 | tf_op jit(solution)/shard_map/ppermute | solution.py:16
  18.5 5.9 %collective-permute-start.10 = (bf16[64,512]{1,0:T(8,128)(2,1)S(1)}, bf16[64,512]{1,0:T(8,128)(2,1)S(1)}, u32[]{:S(2)}, u32[]{:S(2)}) collective-permute-start(bf16[64,512]{1,0:T(8,128)(2,1)S(1)} %get-tuple-element.51), channel_id=1, source_target_pairs={{0,2},{1,3},{2,0},{3,1},{4,6},{5,7},{6,4},{7,5},{8,10},{9,11},{10,... | collective-permute-start | bytes 196616 | tf_op jit(solution)/shard_map/ppermute | solution.py:16
  19.6 14.4 %collective-permute-start.18 = (bf16[2,32,1536]{2,1,0:T(8,128)(2,1)S(1)}, bf16[2,32,1536]{2,1,0:T(8,128)(2,1)S(1)}, u32[]{:S(2)}, u32[]{:S(2)}) collective-permute-start(bf16[2,32,1536]{2,1,0:T(8,128)(2,1)S(1)} %get-tuple-element.63), channel_id=1, source_target_pairs={{0,2},{1,3},{2,0},{3,1},{4,6},{5,7},{6,4},{7,5},{8,10},{9,11},{10,... | collective-permute-start | bytes 589832 | tf_op jit(solution)/shard_map/ppermute | solution.py:16
  24.5 6.1 %collective-permute-start.13 = (bf16[64,512]{1,0:T(8,128)(2,1)S(1)}, bf16[64,512]{1,0:T(8,128)(2,1)S(1)}, u32[]{:S(2)}, u32[]{:S(2)}) collective-permute-start(bf16[64,512]{1,0:T(8,128)(2,1)S(1)} %get-tuple-element.60.refs_0_), channel_id=1, source_target_pairs={{0,6},{1,7},{2,4},{3,5},{4,2},{5,3},{6,0},{7,1},{8,14},{9,15},{10,... | collective-permute-start | bytes 196616 | tf_op jit(solution)/shard_map/ppermute | solution.py:16
  26.5 6.3 %collective-permute-start.12 = (bf16[64,512]{1,0:T(8,128)(2,1)S(1)}, bf16[64,512]{1,0:T(8,128)(2,1)S(1)}, u32[]{:S(2)}, u32[]{:S(2)}) collective-permute-start(bf16[64,512]{1,0:T(8,128)(2,1)S(1)} %get-tuple-element.60.refs_0_), channel_id=1, source_target_pairs={{0,4},{1,5},{2,6},{3,7},{4,0},{5,1},{6,2},{7,3},{8,12},{9,13},{10,... | collective-permute-start | bytes 196616 | tf_op jit(solution)/shard_map/ppermute | solution.py:16
  26.5 6.3 %collective-permute-start.11 = (bf16[64,512]{1,0:T(8,128)(2,1)S(1)}, bf16[64,512]{1,0:T(8,128)(2,1)S(1)}, u32[]{:S(2)}, u32[]{:S(2)}) collective-permute-start(bf16[64,512]{1,0:T(8,128)(2,1)S(1)} %get-tuple-element.60.refs_0_), channel_id=1, source_target_pairs={{0,2},{1,3},{2,0},{3,1},{4,6},{5,7},{6,4},{7,5},{8,10},{9,11},{10,... | collective-permute-start | bytes 196616 | tf_op jit(solution)/shard_map/ppermute | solution.py:16
  28.9 5.1 %collective-permute-start.14 = (bf16[64,512]{1,0:T(8,128)(2,1)S(1)}, bf16[64,512]{1,0:T(8,128)(2,1)S(1)}, u32[]{:S(2)}, u32[]{:S(2)}) collective-permute-start(bf16[64,512]{1,0:T(8,128)(2,1)S(1)} %get-tuple-element.60.refs_0_), channel_id=1, source_target_pairs={{0,1},{1,0},{2,3},{3,2},{4,5},{5,4},{6,7},{7,6},{8,9},{9,8},{10,11... | collective-permute-start | bytes 196616 | tf_op jit(solution)/shard_map/ppermute | solution.py:16
  30.6 3.4 %collective-permute-start.17 = (bf16[64,512]{1,0:T(8,128)(2,1)S(1)}, bf16[64,512]{1,0:T(8,128)(2,1)S(1)}, u32[]{:S(2)}, u32[]{:S(2)}) collective-permute-start(bf16[64,512]{1,0:T(8,128)(2,1)S(1)} %collective-permute-done.13.refs_3_), channel_id=1, source_target_pairs={{0,1},{1,0},{2,3},{3,2},{4,5},{5,4},{6,7},{7,6},{8,9},{9,8},{10,11... | collective-permute-start | bytes 196616 | tf_op jit(solution)/shard_map/ppermute | solution.py:16
  35.1 5.5 %collective-permute-start.19 = (bf16[448,128]{1,0:T(8,128)(2,1)S(1)}, bf16[448,128]{1,0:T(8,128)(2,1)S(1)}, u32[]{:S(2)}, u32[]{:S(2)}) collective-permute-start(bf16[448,128]{1,0:T(8,128)(2,1)S(1)} %get-tuple-element.70), channel_id=1, source_target_pairs={{0,8},{8,0},{16,24},{24,16},{1,9},{9,1},{17,25},{25,17},{2,10},{10... | collective-permute-start | bytes 344072 | tf_op jit(solution)/shard_map/ppermute | solution.py:16
  36.6 7.6 %collective-permute-start.20 = (bf16[448,128]{1,0:T(8,128)(2,1)S(1)}, bf16[448,128]{1,0:T(8,128)(2,1)S(1)}, u32[]{:S(2)}, u32[]{:S(2)}) collective-permute-start(bf16[448,128]{1,0:T(8,128)(2,1)S(1)} %get-tuple-element.71), channel_id=1, source_target_pairs={{0,16},{8,24},{16,0},{24,8},{1,17},{9,25},{17,1},{25,9},{2,18},{10... | collective-permute-start | bytes 344072 | tf_op jit(solution)/shard_map/ppermute | solution.py:16
  38.2 6.0 %collective-permute-start.21 = (bf16[448,128]{1,0:T(8,128)(2,1)S(1)}, bf16[448,128]{1,0:T(8,128)(2,1)S(1)}, u32[]{:S(2)}, u32[]{:S(2)}) collective-permute-start(bf16[448,128]{1,0:T(8,128)(2,1)S(1)} %get-tuple-element.72), channel_id=1, source_target_pairs={{0,24},{8,16},{16,8},{24,0},{1,25},{9,17},{17,9},{25,1},{2,26},{10... | collective-permute-start | bytes 344072 | tf_op jit(solution)/shard_map/ppermute | solution.py:16
  44.3 6.9 %collective-permute-start.22 = (bf16[256,128]{1,0:T(8,128)(2,1)S(1)}, bf16[256,128]{1,0:T(8,128)(2,1)S(1)}, u32[]{:S(2)}, u32[]{:S(2)}) collective-permute-start(bf16[256,128]{1,0:T(8,128)(2,1)S(1)} %get-tuple-element.80), channel_id=1, source_target_pairs={{0,4},{1,5},{2,6},{3,7},{4,0},{5,1},{6,2},{7,3},{8,12},{9,13},{10,... | collective-permute-start | bytes 196616 | tf_op jit(solution)/shard_map/ppermute | solution.py:16
  44.9 6.3 %collective-permute-start.23 = (bf16[256,128]{1,0:T(8,128)(2,1)S(1)}, bf16[256,128]{1,0:T(8,128)(2,1)S(1)}, u32[]{:S(2)}, u32[]{:S(2)}) collective-permute-start(bf16[256,128]{1,0:T(8,128)(2,1)S(1)} %get-tuple-element.81), channel_id=1, source_target_pairs={{0,6},{1,7},{2,4},{3,5},{4,2},{5,3},{6,0},{7,1},{8,14},{9,15},{10,... | collective-permute-start | bytes 196616 | tf_op jit(solution)/shard_map/ppermute | solution.py:16
  46.8 5.1 %collective-permute-start.24 = (bf16[256,128]{1,0:T(8,128)(2,1)S(1)}, bf16[256,128]{1,0:T(8,128)(2,1)S(1)}, u32[]{:S(2)}, u32[]{:S(2)}) collective-permute-start(bf16[256,128]{1,0:T(8,128)(2,1)S(1)} %get-tuple-element.82), channel_id=1, source_target_pairs={{0,2},{1,3},{2,0},{3,1},{4,6},{5,7},{6,4},{7,5},{8,10},{9,11},{10,... | collective-permute-start | bytes 196616 | tf_op jit(solution)/shard_map/ppermute | solution.py:16
  51.9 5.8 %collective-permute-start.27 = (bf16[448,128]{1,0:T(8,128)(2,1)S(1)}, bf16[448,128]{1,0:T(8,128)(2,1)S(1)}, u32[]{:S(2)}, u32[]{:S(2)}) collective-permute-start(bf16[448,128]{1,0:T(8,128)(2,1)S(1)} %shard_map.95.refs_0_), channel_id=1, source_target_pairs={{0,24},{8,16},{16,8},{24,0},{1,25},{9,17},{17,9},{25,1},{2,26},{10... | collective-permute-start | bytes 344072 | tf_op jit(solution)/shard_map/ppermute | solution.py:16
  53.7 5.2 %collective-permute-start.26 = (bf16[448,128]{1,0:T(8,128)(2,1)S(1)}, bf16[448,128]{1,0:T(8,128)(2,1)S(1)}, u32[]{:S(2)}, u32[]{:S(2)}) collective-permute-start(bf16[448,128]{1,0:T(8,128)(2,1)S(1)} %shard_map.95.refs_0_), channel_id=1, source_target_pairs={{0,16},{8,24},{16,0},{24,8},{1,17},{9,25},{17,1},{25,9},{2,18},{10... | collective-permute-start | bytes 344072 | tf_op jit(solution)/shard_map/ppermute | solution.py:16
  55.0 4.8 %collective-permute-start.25 = (bf16[448,128]{1,0:T(8,128)(2,1)S(1)}, bf16[448,128]{1,0:T(8,128)(2,1)S(1)}, u32[]{:S(2)}, u32[]{:S(2)}) collective-permute-start(bf16[448,128]{1,0:T(8,128)(2,1)S(1)} %shard_map.95.refs_0_), channel_id=1, source_target_pairs={{0,8},{8,0},{16,24},{24,16},{1,9},{9,1},{17,25},{25,17},{2,10},{10... | collective-permute-start | bytes 344072 | tf_op jit(solution)/shard_map/ppermute | solution.py:16
  55.4 4.3 %collective-permute-start.28 = (bf16[448,128]{1,0:T(8,128)(2,1)S(1)}, bf16[448,128]{1,0:T(8,128)(2,1)S(1)}, u32[]{:S(2)}, u32[]{:S(2)}) collective-permute-start(bf16[448,128]{1,0:T(8,128)(2,1)S(1)} %shard_map.95.refs_0_), channel_id=1, source_target_pairs={{0,1},{1,0},{2,3},{3,2},{4,5},{5,4},{6,7},{7,6},{8,9},{9,8},{10,11... | collective-permute-start | bytes 344072 | tf_op jit(solution)/shard_map/ppermute | solution.py:16
  (11 other events, 33.7 us)

commit v7 on v6

--- a/solution.py
+++ b/solution.py
@@ -485,7 +485,7 @@
         ],
     )
     parts = swap_each(sends, "user", 1)
-    parts, hidden = together(parts, hidden)
+    parts, = together(parts)
     amount = padded(blocks * item_few + count)
     own, *sends = call(
         functools.partial(user_sum, chips, item_few, blocks, count),
@@ -495,18 +495,19 @@
         scratch=[pltpu.VMEM((chips, blocks * item_few, LANES), F32)],
     )
     parts = swap_each(sends, "item", 2)
+    *parts, hidden = lax.optimization_barrier((*by_reach(parts), hidden))
     amount = padded(blocks * item_few + chips * levels * few)
     gathered = call(
         functools.partial(line_sum, blocks * item_few, levels * few, chips // kept),
         struct((amount, LANES), BF16),
-        (own, *by_reach(parts)),
+        (own, *parts),
         0.1,
     )
     gathered = [gathered] + swap_each([gathered] * (user_size - 1), "user", 1)
     others = [swap(piece, "item", 1) for piece in gathered]
     weight_grad = struct((levels, width, hidden_width), F32)
     late = list(range(user_size))
-    soon = [late.pop(0), late.pop()] if few == part else []
+    soon = [late.pop(0)] if few == part else []
     scratch = [
         pltpu.VMEM((2, levels, width // 2, hidden_width), F32),
         pltpu.VMEM((chips, user_size, few, LANES), F32),

time: 62.2 us -> 62.3 us (level)
  transfers between devices with their start and end apart: 32 -> 32, of which waited for: 16 -> 17; matrix products, arithmetic and copies ran while one was open for 0% -> 0% of each run, Pallas kernels for 12% -> 12%
where the time goes in v7:
time: 62.3 us; the launch traced here: 62.1 us
  starting transfers between devices  27.8 us (45%)
  waiting for transfers between devices  23.2 us (37%)
  Pallas kernels  10.3 us (17%)
  between operations  0.82 us (1%)
    ppermute x32, starting transfers between devices, swap(): lax.ppermute(array, axis, [(i, i ^ step) for i in range(lax.axis_size(axi...  27.8 us
    ppermute x32, waiting for transfers between devices, swap(): lax.ppermute(array, axis, [(i, i ^ step) for i in range(lax.axis_size(axi...  23.2 us
    pallas_call x13, Pallas kernels, call(): pl.pallas_call(body, out_shape=outs, in_specs=specs or [vmem] * len(args)...  10.3 us
  transfers between devices with their start and end apart: 32, of which 17 were waited for; matrix products, arithmetic and copies ran while one was open for 0% of the time, Pallas kernels for 12%

profile of v7, /device:TPU:0, one launch (start us, length us, event | category | flops | bytes accessed | tf_op | source)
XLA Modules:
  0.0 62.1 jit_solution(9703755219327305943)
XLA Ops:
  1.2 4.7 %collective-permute-start.2 = (bf16[128,256]{1,0:T(8,128)(2,1)}, bf16[128,256]{1,0:T(8,128)(2,1)S(1)}, u32[]{:S(2)}, u32[]{:S(2)}) collective-permute-start(bf16[128,256]{1,0:T(8,128)(2,1)} %refs_0_.1), channel_id=1, source_target_pairs={{0,6},{1,7},{2,4},{3,5},{4,2},{5,3},{6,0},{7,1},{8,14},{9,15},{10,... | collective-permute-start | bytes 196616 | tf_op jit(solution)/shard_map/ppermute | solution.py:16
  6.5 2.6 %shard_map.85.dense = bf16[2,768,1024]{2,1,0:T(8,128)(2,1)S(1)} custom-call(s32[1,96]{1,0:T(1,128)} %order.1, s32[1,8]{1,0:T(1,128)} %counts.1, bf16[1,24,1,2,64,128]{5,4,3,2,1,0:T(8,128)(2,1)} %bitcast.2, bf16[1,24,1,2,64,128]{5,4,3,2,1,0:T(8,128)(2,1)S(1)} %collective-permute-done.3.theirs), custom_call_target="tpu_custom_call" | custom-call | flops 4000000000 | bytes 12000000 | tf_op jit(solution)/shard_map/pallas_call | solution.py:58
  9.2 2.9 %collective-permute-done.1.refs_2_ = bf16[128,256]{1,0:T(8,128)(2,1)S(1)} collective-permute-done((bf16[128,256]{1,0:T(8,128)(2,1)}, bf16[128,256]{1,0:T(8,128)(2,1)S(1)}, u32[]{:S(2)}, u32[]{:S(2)}) %collective-permute-start.1) | collective-permute-done | bytes 65568 | tf_op jit(solution)/shard_map/ppermute | solution.py:16
  14.8 1.2 %collective-permute-start.8 = (bf16[64,512]{1,0:T(8,128)(2,1)S(1)}, bf16[64,512]{1,0:T(8,128)(2,1)S(1)}, u32[]{:S(2)}, u32[]{:S(2)}) collective-permute-start(bf16[64,512]{1,0:T(8,128)(2,1)S(1)} %get-tuple-element.52), channel_id=1, source_target_pairs={{0,4},{1,5},{2,6},{3,7},{4,0},{5,1},{6,2},{7,3},{8,12},{9,13},{10,... | collective-permute-start | bytes 196616 | tf_op jit(solution)/shard_map/ppermute | solution.py:16
  16.1 2.4 %collective-permute-start.9 = (bf16[64,512]{1,0:T(8,128)(2,1)S(1)}, bf16[64,512]{1,0:T(8,128)(2,1)S(1)}, u32[]{:S(2)}, u32[]{:S(2)}) collective-permute-start(bf16[64,512]{1,0:T(8,128)(2,1)S(1)} %get-tuple-element.53), channel_id=1, source_target_pairs={{0,6},{1,7},{2,4},{3,5},{4,2},{5,3},{6,0},{7,1},{8,14},{9,15},{10,... | collective-permute-start | bytes 196616 | tf_op jit(solution)/shard_map/ppermute | solution.py:16
  18.5 1.1 %shard_map.90 = (f32[2,32,1536]{2,1,0:T(8,128)S(1)}, bf16[2,32,1536]{2,1,0:T(8,128)(2,1)S(1)}) custom-call(bf16[2,768,1024]{2,1,0:T(8,128)(2,1)S(1)} %shard_map.85.dense, bf16[512,256]{1,0:T(8,128)(2,1)S(1)} %get-tuple-element.64.mine, bf16[512,256]{1,0:T(8,128)(2,1)S(1)} %get-tuple-element.65.theirs), custom_call_target="tpu_custom_call" | custom-call | flops 3000000000 | bytes 9000000 | tf_op jit(solution)/shard_map/pallas_call | solution.py:58
  19.6 2.1 %collective-permute-start.18 = (bf16[2,32,1536]{2,1,0:T(8,128)(2,1)S(1)}, bf16[2,32,1536]{2,1,0:T(8,128)(2,1)S(1)}, u32[]{:S(2)}, u32[]{:S(2)}) collective-permute-start(bf16[2,32,1536]{2,1,0:T(8,128)(2,1)S(1)} %get-tuple-element.66), channel_id=1, source_target_pairs={{0,2},{1,3},{2,0},{3,1},{4,6},{5,7},{6,4},{7,5},{8,10},{9,11},{10,... | collective-permute-start | bytes 589832 | tf_op jit(solution)/shard_map/ppermute | solution.py:16
  22.4 1.1 %collective-permute-done.8.refs_0_ = bf16[64,512]{1,0:T(8,128)(2,1)S(1)} collective-permute-done((bf16[64,512]{1,0:T(8,128)(2,1)S(1)}, bf16[64,512]{1,0:T(8,128)(2,1)S(1)}, u32[]{:S(2)}, u32[]{:S(2)}) %collective-permute-start.8) | collective-permute-done | bytes 65568 | tf_op jit(solution)/shard_map/ppermute | solution.py:16
  24.5 2.0 %collective-permute-start.13 = (bf16[64,512]{1,0:T(8,128)(2,1)S(1)}, bf16[64,512]{1,0:T(8,128)(2,1)S(1)}, u32[]{:S(2)}, u32[]{:S(2)}) collective-permute-start(bf16[64,512]{1,0:T(8,128)(2,1)S(1)} %get-tuple-element.63.refs_0_), channel_id=1, source_target_pairs={{0,6},{1,7},{2,4},{3,5},{4,2},{5,3},{6,0},{7,1},{8,14},{9,15},{10,... | collective-permute-start | bytes 196616 | tf_op jit(solution)/shard_map/ppermute | solution.py:16
  26.5 2.4 %collective-permute-start.11 = (bf16[64,512]{1,0:T(8,128)(2,1)S(1)}, bf16[64,512]{1,0:T(8,128)(2,1)S(1)}, u32[]{:S(2)}, u32[]{:S(2)}) collective-permute-start(bf16[64,512]{1,0:T(8,128)(2,1)S(1)} %get-tuple-element.63.refs_0_), channel_id=1, source_target_pairs={{0,2},{1,3},{2,0},{3,1},{4,6},{5,7},{6,4},{7,5},{8,10},{9,11},{10,... | collective-permute-start | bytes 196616 | tf_op jit(solution)/shard_map/ppermute | solution.py:16
  28.9 1.7 %collective-permute-done.13.refs_3_ = bf16[64,512]{1,0:T(8,128)(2,1)S(1)} collective-permute-done((bf16[64,512]{1,0:T(8,128)(2,1)S(1)}, bf16[64,512]{1,0:T(8,128)(2,1)S(1)}, u32[]{:S(2)}, u32[]{:S(2)}) %collective-permute-start.13) | collective-permute-done | bytes 65568 | tf_op jit(solution)/shard_map/ppermute | solution.py:16
  30.6 2.2 %collective-permute-done.12.refs_2_ = bf16[64,512]{1,0:T(8,128)(2,1)S(1)} collective-permute-done((bf16[64,512]{1,0:T(8,128)(2,1)S(1)}, bf16[64,512]{1,0:T(8,128)(2,1)S(1)}, u32[]{:S(2)}, u32[]{:S(2)}) %collective-permute-start.12) | collective-permute-done | bytes 65568 | tf_op jit(solution)/shard_map/ppermute | solution.py:16
  35.1 1.6 %collective-permute-start.19 = (bf16[448,128]{1,0:T(8,128)(2,1)S(1)}, bf16[448,128]{1,0:T(8,128)(2,1)S(1)}, u32[]{:S(2)}, u32[]{:S(2)}) collective-permute-start(bf16[448,128]{1,0:T(8,128)(2,1)S(1)} %get-tuple-element.74), channel_id=1, source_target_pairs={{0,8},{8,0},{16,24},{24,16},{1,9},{9,1},{17,25},{25,17},{2,10},{10... | collective-permute-start | bytes 344072 | tf_op jit(solution)/shard_map/ppermute | solution.py:16
  36.6 1.5 %collective-permute-start.20 = (bf16[448,128]{1,0:T(8,128)(2,1)S(1)}, bf16[448,128]{1,0:T(8,128)(2,1)S(1)}, u32[]{:S(2)}, u32[]{:S(2)}) collective-permute-start(bf16[448,128]{1,0:T(8,128)(2,1)S(1)} %get-tuple-element.75), channel_id=1, source_target_pairs={{0,16},{8,24},{16,0},{24,8},{1,17},{9,25},{17,1},{25,9},{2,18},{10... | collective-permute-start | bytes 344072 | tf_op jit(solution)/shard_map/ppermute | solution.py:16
  38.6 1.9 %collective-permute-done.19.refs_3_ = bf16[448,128]{1,0:T(8,128)(2,1)S(1)} collective-permute-done((bf16[448,128]{1,0:T(8,128)(2,1)S(1)}, bf16[448,128]{1,0:T(8,128)(2,1)S(1)}, u32[]{:S(2)}, u32[]{:S(2)}) %collective-permute-start.19) | collective-permute-done | bytes 114720 | tf_op jit(solution)/shard_map/ppermute | solution.py:16
  40.6 3.7 %collective-permute-done.20.refs_2_ = bf16[448,128]{1,0:T(8,128)(2,1)S(1)} collective-permute-done((bf16[448,128]{1,0:T(8,128)(2,1)S(1)}, bf16[448,128]{1,0:T(8,128)(2,1)S(1)}, u32[]{:S(2)}, u32[]{:S(2)}) %collective-permute-start.20) | collective-permute-done | bytes 114720 | tf_op jit(solution)/shard_map/ppermute | solution.py:16
  44.9 1.9 %collective-permute-start.23 = (bf16[256,128]{1,0:T(8,128)(2,1)S(1)}, bf16[256,128]{1,0:T(8,128)(2,1)S(1)}, u32[]{:S(2)}, u32[]{:S(2)}) collective-permute-start(bf16[256,128]{1,0:T(8,128)(2,1)S(1)} %get-tuple-element.81), channel_id=1, source_target_pairs={{0,6},{1,7},{2,4},{3,5},{4,2},{5,3},{6,0},{7,1},{8,14},{9,15},{10,... | collective-permute-start | bytes 196616 | tf_op jit(solution)/shard_map/ppermute | solution.py:16
  46.8 1.1 %collective-permute-start.24 = (bf16[256,128]{1,0:T(8,128)(2,1)S(1)}, bf16[256,128]{1,0:T(8,128)(2,1)S(1)}, u32[]{:S(2)}, u32[]{:S(2)}) collective-permute-start(bf16[256,128]{1,0:T(8,128)(2,1)S(1)} %get-tuple-element.82), channel_id=1, source_target_pairs={{0,2},{1,3},{2,0},{3,1},{4,6},{5,7},{6,4},{7,5},{8,10},{9,11},{10,... | collective-permute-start | bytes 196616 | tf_op jit(solution)/shard_map/ppermute | solution.py:16
  48.5 2.7 %collective-permute-done.22.refs_0_ = bf16[256,128]{1,0:T(8,128)(2,1)S(1)} collective-permute-done((bf16[256,128]{1,0:T(8,128)(2,1)S(1)}, bf16[256,128]{1,0:T(8,128)(2,1)S(1)}, u32[]{:S(2)}, u32[]{:S(2)}) %collective-permute-start.22) | collective-permute-done | bytes 65568 | tf_op jit(solution)/shard_map/ppermute | solution.py:16
  51.9 1.8 %collective-permute-start.27 = (bf16[448,128]{1,0:T(8,128)(2,1)S(1)}, bf16[448,128]{1,0:T(8,128)(2,1)S(1)}, u32[]{:S(2)}, u32[]{:S(2)}) collective-permute-start(bf16[448,128]{1,0:T(8,128)(2,1)S(1)} %shard_map.95.refs_0_), channel_id=1, source_target_pairs={{0,24},{8,16},{16,8},{24,0},{1,25},{9,17},{17,9},{25,1},{2,26},{10... | collective-permute-start | bytes 344072 | tf_op jit(solution)/shard_map/ppermute | solution.py:16
  53.7 1.3 %collective-permute-start.26 = (bf16[448,128]{1,0:T(8,128)(2,1)S(1)}, bf16[448,128]{1,0:T(8,128)(2,1)S(1)}, u32[]{:S(2)}, u32[]{:S(2)}) collective-permute-start(bf16[448,128]{1,0:T(8,128)(2,1)S(1)} %shard_map.95.refs_0_), channel_id=1, source_target_pairs={{0,16},{8,24},{16,0},{24,8},{1,17},{9,25},{17,1},{25,9},{2,18},{10... | collective-permute-start | bytes 344072 | tf_op jit(solution)/shard_map/ppermute | solution.py:16
  55.4 2.2 %collective-permute-done.27.refs_3_ = bf16[448,128]{1,0:T(8,128)(2,1)S(1)} collective-permute-done((bf16[448,128]{1,0:T(8,128)(2,1)S(1)}, bf16[448,128]{1,0:T(8,128)(2,1)S(1)}, u32[]{:S(2)}, u32[]{:S(2)}) %collective-permute-start.27) | collective-permute-done | bytes 114720 | tf_op jit(solution)/shard_map/ppermute | solution.py:16
  57.7 1.2 %collective-permute-done.26.refs_2_ = bf16[448,128]{1,0:T(8,128)(2,1)S(1)} collective-permute-done((bf16[448,128]{1,0:T(8,128)(2,1)S(1)}, bf16[448,128]{1,0:T(8,128)(2,1)S(1)}, u32[]{:S(2)}, u32[]{:S(2)}) %collective-permute-start.26) | collective-permute-done | bytes 114720 | tf_op jit(solution)/shard_map/ppermute | solution.py:16
  59.8 1.2 %shard_map.96 = (f32[128,256]{1,0:T(8,128)}, f32[3,256,512]{2,1,0:T(8,128)}) custom-call(bf16[448,128]{1,0:T(8,128)(2,1)S(1)} %shard_map.95.refs_0_, bf16[448,128]{1,0:T(8,128)(2,1)S(1)} %collective-permute-done.25.refs_1_, bf16[448,128]{1,0:T(8,128)(2,1)S(1)} %collective-permute-done.26.refs_2_, bf16[448,128]{1,0:T(8,128)(2,1)S(1)} %collective-permute-done.27.refs_3_, ...), custom_call_target="tpu_custom_call" | custom-call | flops 900000000 | bytes 2700000 | tf_op jit(solution)/shard_map/pallas_call | solution.py:58
  (59 shorter events, 12.8 us)
Async XLA Ops:
  0.6 5.9 %collective-permute-start.3 = (bf16[1,24,1,2,64,128]{5,4,3,2,1,0:T(8,128)(2,1)}, bf16[1,24,1,2,64,128]{5,4,3,2,1,0:T(8,128)(2,1)S(1)}, u32[]{:S(2)}, u32[]{:S(2)}) collective-permute-start(bf16[1,24,1,2,64,128]{5,4,3,2,1,0:T(8,128)(2,1)} %bitcast.1), channel_id=1, source_target_pairs={{0,1},{1,0},{2,3},{3,2},{4,5},{5,4},{6,7},{7,6},{8,9},{9,8},{10,11... | collective-permute-start | bytes 2359304 | tf_op jit(solution)/shard_map/ppermute | solution.py:16
  1.2 8.0 %collective-permute-start.2 = (bf16[128,256]{1,0:T(8,128)(2,1)}, bf16[128,256]{1,0:T(8,128)(2,1)S(1)}, u32[]{:S(2)}, u32[]{:S(2)}) collective-permute-start(bf16[128,256]{1,0:T(8,128)(2,1)} %refs_0_.1), channel_id=1, source_target_pairs={{0,6},{1,7},{2,4},{3,5},{4,2},{5,3},{6,0},{7,1},{8,14},{9,15},{10,... | collective-permute-start | bytes 196616 | tf_op jit(solution)/shard_map/ppermute | solution.py:16
  5.8 6.3 %collective-permute-start.1 = (bf16[128,256]{1,0:T(8,128)(2,1)}, bf16[128,256]{1,0:T(8,128)(2,1)S(1)}, u32[]{:S(2)}, u32[]{:S(2)}) collective-permute-start(bf16[128,256]{1,0:T(8,128)(2,1)} %refs_0_.1), channel_id=1, source_target_pairs={{0,4},{1,5},{2,6},{3,7},{4,0},{5,1},{6,2},{7,3},{8,12},{9,13},{10,... | collective-permute-start | bytes 196616 | tf_op jit(solution)/shard_map/ppermute | solution.py:16
  5.8 6.3 %collective-permute-start = (bf16[128,256]{1,0:T(8,128)(2,1)}, bf16[128,256]{1,0:T(8,128)(2,1)S(1)}, u32[]{:S(2)}, u32[]{:S(2)}) collective-permute-start(bf16[128,256]{1,0:T(8,128)(2,1)} %refs_0_.1), channel_id=1, source_target_pairs={{0,2},{1,3},{2,0},{3,1},{4,6},{5,7},{6,4},{7,5},{8,10},{9,11},{10,... | collective-permute-start | bytes 196616 | tf_op jit(solution)/shard_map/ppermute | solution.py:16
  6.5 6.5 %collective-permute-start.4 = (bf16[128,256]{1,0:T(8,128)(2,1)}, bf16[128,256]{1,0:T(8,128)(2,1)S(1)}, u32[]{:S(2)}, u32[]{:S(2)}) collective-permute-start(bf16[128,256]{1,0:T(8,128)(2,1)} %refs_0_.1), channel_id=1, source_target_pairs={{0,1},{1,0},{2,3},{3,2},{4,5},{5,4},{6,7},{7,6},{8,9},{9,8},{10,11... | collective-permute-start | bytes 196616 | tf_op jit(solution)/shard_map/ppermute | solution.py:16
  14.8 8.6 %collective-permute-start.8 = (bf16[64,512]{1,0:T(8,128)(2,1)S(1)}, bf16[64,512]{1,0:T(8,128)(2,1)S(1)}, u32[]{:S(2)}, u32[]{:S(2)}) collective-permute-start(bf16[64,512]{1,0:T(8,128)(2,1)S(1)} %get-tuple-element.52), channel_id=1, source_target_pairs={{0,4},{1,5},{2,6},{3,7},{4,0},{5,1},{6,2},{7,3},{8,12},{9,13},{10,... | collective-permute-start | bytes 196616 | tf_op jit(solution)/shard_map/ppermute | solution.py:16
  16.1 7.3 %collective-permute-start.9 = (bf16[64,512]{1,0:T(8,128)(2,1)S(1)}, bf16[64,512]{1,0:T(8,128)(2,1)S(1)}, u32[]{:S(2)}, u32[]{:S(2)}) collective-permute-start(bf16[64,512]{1,0:T(8,128)(2,1)S(1)} %get-tuple-element.53), channel_id=1, source_target_pairs={{0,6},{1,7},{2,4},{3,5},{4,2},{5,3},{6,0},{7,1},{8,14},{9,15},{10,... | collective-permute-start | bytes 196616 | tf_op jit(solution)/shard_map/ppermute | solution.py:16
  18.5 5.9 %collective-permute-start.10 = (bf16[64,512]{1,0:T(8,128)(2,1)S(1)}, bf16[64,512]{1,0:T(8,128)(2,1)S(1)}, u32[]{:S(2)}, u32[]{:S(2)}) collective-permute-start(bf16[64,512]{1,0:T(8,128)(2,1)S(1)} %get-tuple-element.54), channel_id=1, source_target_pairs={{0,2},{1,3},{2,0},{3,1},{4,6},{5,7},{6,4},{7,5},{8,10},{9,11},{10,... | collective-permute-start | bytes 196616 | tf_op jit(solution)/shard_map/ppermute | solution.py:16
  19.6 14.4 %collective-permute-start.18 = (bf16[2,32,1536]{2,1,0:T(8,128)(2,1)S(1)}, bf16[2,32,1536]{2,1,0:T(8,128)(2,1)S(1)}, u32[]{:S(2)}, u32[]{:S(2)}) collective-permute-start(bf16[2,32,1536]{2,1,0:T(8,128)(2,1)S(1)} %get-tuple-element.66), channel_id=1, source_target_pairs={{0,2},{1,3},{2,0},{3,1},{4,6},{5,7},{6,4},{7,5},{8,10},{9,11},{10,... | collective-permute-start | bytes 589832 | tf_op jit(solution)/shard_map/ppermute | solution.py:16
  24.5 6.1 %collective-permute-start.13 = (bf16[64,512]{1,0:T(8,128)(2,1)S(1)}, bf16[64,512]{1,0:T(8,128)(2,1)S(1)}, u32[]{:S(2)}, u32[]{:S(2)}) collective-permute-start(bf16[64,512]{1,0:T(8,128)(2,1)S(1)} %get-tuple-element.63.refs_0_), channel_id=1, source_target_pairs={{0,6},{1,7},{2,4},{3,5},{4,2},{5,3},{6,0},{7,1},{8,14},{9,15},{10,... | collective-permute-start | bytes 196616 | tf_op jit(solution)/shard_map/ppermute | solution.py:16
  26.5 6.3 %collective-permute-start.12 = (bf16[64,512]{1,0:T(8,128)(2,1)S(1)}, bf16[64,512]{1,0:T(8,128)(2,1)S(1)}, u32[]{:S(2)}, u32[]{:S(2)}) collective-permute-start(bf16[64,512]{1,0:T(8,128)(2,1)S(1)} %get-tuple-element.63.refs_0_), channel_id=1, source_target_pairs={{0,4},{1,5},{2,6},{3,7},{4,0},{5,1},{6,2},{7,3},{8,12},{9,13},{10,... | collective-permute-start | bytes 196616 | tf_op jit(solution)/shard_map/ppermute | solution.py:16
  26.5 6.3 %collective-permute-start.11 = (bf16[64,512]{1,0:T(8,128)(2,1)S(1)}, bf16[64,512]{1,0:T(8,128)(2,1)S(1)}, u32[]{:S(2)}, u32[]{:S(2)}) collective-permute-start(bf16[64,512]{1,0:T(8,128)(2,1)S(1)} %get-tuple-element.63.refs_0_), channel_id=1, source_target_pairs={{0,2},{1,3},{2,0},{3,1},{4,6},{5,7},{6,4},{7,5},{8,10},{9,11},{10,... | collective-permute-start | bytes 196616 | tf_op jit(solution)/shard_map/ppermute | solution.py:16
  28.9 5.1 %collective-permute-start.14 = (bf16[64,512]{1,0:T(8,128)(2,1)S(1)}, bf16[64,512]{1,0:T(8,128)(2,1)S(1)}, u32[]{:S(2)}, u32[]{:S(2)}) collective-permute-start(bf16[64,512]{1,0:T(8,128)(2,1)S(1)} %get-tuple-element.63.refs_0_), channel_id=1, source_target_pairs={{0,1},{1,0},{2,3},{3,2},{4,5},{5,4},{6,7},{7,6},{8,9},{9,8},{10,11... | collective-permute-start | bytes 196616 | tf_op jit(solution)/shard_map/ppermute | solution.py:16
  30.6 3.4 %collective-permute-start.17 = (bf16[64,512]{1,0:T(8,128)(2,1)S(1)}, bf16[64,512]{1,0:T(8,128)(2,1)S(1)}, u32[]{:S(2)}, u32[]{:S(2)}) collective-permute-start(bf16[64,512]{1,0:T(8,128)(2,1)S(1)} %collective-permute-done.13.refs_3_), channel_id=1, source_target_pairs={{0,1},{1,0},{2,3},{3,2},{4,5},{5,4},{6,7},{7,6},{8,9},{9,8},{10,11... | collective-permute-start | bytes 196616 | tf_op jit(solution)/shard_map/ppermute | solution.py:16
  35.1 5.5 %collective-permute-start.19 = (bf16[448,128]{1,0:T(8,128)(2,1)S(1)}, bf16[448,128]{1,0:T(8,128)(2,1)S(1)}, u32[]{:S(2)}, u32[]{:S(2)}) collective-permute-start(bf16[448,128]{1,0:T(8,128)(2,1)S(1)} %get-tuple-element.74), channel_id=1, source_target_pairs={{0,8},{8,0},{16,24},{24,16},{1,9},{9,1},{17,25},{25,17},{2,10},{10... | collective-permute-start | bytes 344072 | tf_op jit(solution)/shard_map/ppermute | solution.py:16
  36.6 7.6 %collective-permute-start.20 = (bf16[448,128]{1,0:T(8,128)(2,1)S(1)}, bf16[448,128]{1,0:T(8,128)(2,1)S(1)}, u32[]{:S(2)}, u32[]{:S(2)}) collective-permute-start(bf16[448,128]{1,0:T(8,128)(2,1)S(1)} %get-tuple-element.75), channel_id=1, source_target_pairs={{0,16},{8,24},{16,0},{24,8},{1,17},{9,25},{17,1},{25,9},{2,18},{10... | collective-permute-start | bytes 344072 | tf_op jit(solution)/shard_map/ppermute | solution.py:16
  38.2 6.0 %collective-permute-start.21 = (bf16[448,128]{1,0:T(8,128)(2,1)S(1)}, bf16[448,128]{1,0:T(8,128)(2,1)S(1)}, u32[]{:S(2)}, u32[]{:S(2)}) collective-permute-start(bf16[448,128]{1,0:T(8,128)(2,1)S(1)} %get-tuple-element.76), channel_id=1, source_target_pairs={{0,24},{8,16},{16,8},{24,0},{1,25},{9,17},{17,9},{25,1},{2,26},{10... | collective-permute-start | bytes 344072 | tf_op jit(solution)/shard_map/ppermute | solution.py:16
  44.3 6.9 %collective-permute-start.22 = (bf16[256,128]{1,0:T(8,128)(2,1)S(1)}, bf16[256,128]{1,0:T(8,128)(2,1)S(1)}, u32[]{:S(2)}, u32[]{:S(2)}) collective-permute-start(bf16[256,128]{1,0:T(8,128)(2,1)S(1)} %get-tuple-element.80), channel_id=1, source_target_pairs={{0,4},{1,5},{2,6},{3,7},{4,0},{5,1},{6,2},{7,3},{8,12},{9,13},{10,... | collective-permute-start | bytes 196616 | tf_op jit(solution)/shard_map/ppermute | solution.py:16
  44.9 6.3 %collective-permute-start.23 = (bf16[256,128]{1,0:T(8,128)(2,1)S(1)}, bf16[256,128]{1,0:T(8,128)(2,1)S(1)}, u32[]{:S(2)}, u32[]{:S(2)}) collective-permute-start(bf16[256,128]{1,0:T(8,128)(2,1)S(1)} %get-tuple-element.81), channel_id=1, source_target_pairs={{0,6},{1,7},{2,4},{3,5},{4,2},{5,3},{6,0},{7,1},{8,14},{9,15},{10,... | collective-permute-start | bytes 196616 | tf_op jit(solution)/shard_map/ppermute | solution.py:16
  46.8 5.1 %collective-permute-start.24 = (bf16[256,128]{1,0:T(8,128)(2,1)S(1)}, bf16[256,128]{1,0:T(8,128)(2,1)S(1)}, u32[]{:S(2)}, u32[]{:S(2)}) collective-permute-start(bf16[256,128]{1,0:T(8,128)(2,1)S(1)} %get-tuple-element.82), channel_id=1, source_target_pairs={{0,2},{1,3},{2,0},{3,1},{4,6},{5,7},{6,4},{7,5},{8,10},{9,11},{10,... | collective-permute-start | bytes 196616 | tf_op jit(solution)/shard_map/ppermute | solution.py:16
  51.9 5.8 %collective-permute-start.27 = (bf16[448,128]{1,0:T(8,128)(2,1)S(1)}, bf16[448,128]{1,0:T(8,128)(2,1)S(1)}, u32[]{:S(2)}, u32[]{:S(2)}) collective-permute-start(bf16[448,128]{1,0:T(8,128)(2,1)S(1)} %shard_map.95.refs_0_), channel_id=1, source_target_pairs={{0,24},{8,16},{16,8},{24,0},{1,25},{9,17},{17,9},{25,1},{2,26},{10... | collective-permute-start | bytes 344072 | tf_op jit(solution)/shard_map/ppermute | solution.py:16
  53.7 5.2 %collective-permute-start.26 = (bf16[448,128]{1,0:T(8,128)(2,1)S(1)}, bf16[448,128]{1,0:T(8,128)(2,1)S(1)}, u32[]{:S(2)}, u32[]{:S(2)}) collective-permute-start(bf16[448,128]{1,0:T(8,128)(2,1)S(1)} %shard_map.95.refs_0_), channel_id=1, source_target_pairs={{0,16},{8,24},{16,0},{24,8},{1,17},{9,25},{17,1},{25,9},{2,18},{10... | collective-permute-start | bytes 344072 | tf_op jit(solution)/shard_map/ppermute | solution.py:16
  55.0 4.8 %collective-permute-start.25 = (bf16[448,128]{1,0:T(8,128)(2,1)S(1)}, bf16[448,128]{1,0:T(8,128)(2,1)S(1)}, u32[]{:S(2)}, u32[]{:S(2)}) collective-permute-start(bf16[448,128]{1,0:T(8,128)(2,1)S(1)} %shard_map.95.refs_0_), channel_id=1, source_target_pairs={{0,8},{8,0},{16,24},{24,16},{1,9},{9,1},{17,25},{25,17},{2,10},{10... | collective-permute-start | bytes 344072 | tf_op jit(solution)/shard_map/ppermute | solution.py:16
  55.4 4.3 %collective-permute-start.28 = (bf16[448,128]{1,0:T(8,128)(2,1)S(1)}, bf16[448,128]{1,0:T(8,128)(2,1)S(1)}, u32[]{:S(2)}, u32[]{:S(2)}) collective-permute-start(bf16[448,128]{1,0:T(8,128)(2,1)S(1)} %shard_map.95.refs_0_), channel_id=1, source_target_pairs={{0,1},{1,0},{2,3},{3,2},{4,5},{5,4},{6,7},{7,6},{8,9},{9,8},{10,11... | collective-permute-start | bytes 344072 | tf_op jit(solution)/shard_map/ppermute | solution.py:16
  (11 other events, 34.8 us)
